TPU v7x, 256 devices: a whole 4x4x8 slice. The times are simulated.
256 devices in a mesh: story: 32 (over x, z_lo, core), plan: 8 (over z_hi, y).
Axes of the slice: x: 4, y: 4, z: 8 (z_hi: 2, z_lo: 4; z = z_hi * 4 + z_lo), core: 2. Of those that a mesh axis runs over, the one named last changes fastest.
Arguments:
- u_now: float32 [3, 512, 128, 256], P(None, 'story', 'plan'), may hold values from -6 to 6
- u_prev: float32 [3, 512, 128, 256], P(None, 'story', 'plan'), may hold values from -6 to 6
- occupancy: int32 [32, 8, 16], P('story', 'plan'), may hold values 0 or 1
- materials: int32 [32, 8, 16], P('story', 'plan'), may hold values from 0 to 7
- shear_table: float32 [8], replicated, may hold values from 0.5 to 1.5
- lame_table: float32 [8], replicated, may hold values from 0.3 to 1.5
- density_table: float32 [8], replicated, may hold values from 0.8 to 1.2
Outputs:
- u_final: float32 [3, 512, 128, 256], P(None, 'story', 'plan')
All inputs are finite; a program needn't handle non-finite values. No bound on the sum of `occupancy` on one device may be relied on, other than what follows from the above.
Results may differ from a plain program's by a relative error of at most 0.0003.
Values sent between devices are 32-bit elements; how exact they have to be, the bound alone decides.
No kernel may reach another device: no remote copies, remote signals or barrier semaphores. Data moves between devices by JAX's collectives and lax.ppermute only.
A program may use at most 128 MiB of HBM per device.

v0:
```python
import jax
import jax.numpy as jnp
from jax import lax
from jax.sharding import PartitionSpec as P

BLOCK = 16
STEPS = 2


def prefix(part, axis, combine, identity):
    count = lax.axis_size(axis)
    place = lax.axis_index(axis)
    ahead = count - 1 - place
    gathered = lax.all_gather(part, axis)
    state = jnp.zeros_like(part) + jnp.asarray(identity, part.dtype)

    def one(step, state):
        source = count - 1 - step
        return combine(state, lax.dynamic_index_in_dim(gathered, source, 0, False))

    return lax.fori_loop(0, ahead, one, state)


def padded_2(cells, sides, width):
    for axis, dim in sides:
        count = lax.axis_size(axis)
        ends = count - 1
        head = lax.slice_in_dim(cells, 0, width, axis=dim)
        tail = lax.slice_in_dim(cells, cells.shape[dim] - width, cells.shape[dim], axis=dim)
        cells = jnp.concatenate(
            [
                lax.ppermute(tail, axis, [(i, (i + 1) % count) for i in range(ends)]),
                cells,
                lax.ppermute(head, axis, [((i + 1) % count, i) for i in range(ends)]),
            ],
            axis=dim,
        )
    return cells


def filter_axis(values, axis, kind):
    count = values.shape[axis] - 2
    lower = lax.slice_in_dim(values, 0, count, axis=axis)
    middle = lax.slice_in_dim(values, 1, count + 1, axis=axis)
    upper = lax.slice_in_dim(values, 2, count + 2, axis=axis)
    if kind == "second":
        return lower - 2.0 * middle + upper
    if kind == "first":
        return (upper - lower) * 0.5
    return (lower + 4.0 * middle + upper) / 6.0


def derivatives(field):
    z_smooth = filter_axis(field, 0, "smooth")
    z_second = filter_axis(field, 0, "second")
    z_first = filter_axis(field, 0, "first")
    zs_xs = filter_axis(z_smooth, 1, "smooth")
    zs_xsecond = filter_axis(z_smooth, 1, "second")
    zs_xfirst = filter_axis(z_smooth, 1, "first")
    zsecond_xs = filter_axis(z_second, 1, "smooth")
    zfirst_xs = filter_axis(z_first, 1, "smooth")
    zfirst_xfirst = filter_axis(z_first, 1, "first")
    d_zz = filter_axis(zsecond_xs, 2, "smooth")
    d_xx = filter_axis(zs_xsecond, 2, "smooth")
    d_yy = filter_axis(zs_xs, 2, "second")
    d_zx = filter_axis(zfirst_xfirst, 2, "smooth")
    d_zy = filter_axis(zfirst_xs, 2, "first")
    d_xy = filter_axis(zs_xfirst, 2, "first")
    return ((d_zz, d_zx, d_zy), (d_zx, d_xx, d_xy), (d_zy, d_xy, d_yy))


def stiffness(padded, shear, lame, faces_load):
    tables = [derivatives(padded[index]) for index in range(3)]
    forces = []
    for comp_i in range(3):
        own = tables[comp_i]
        laplace = own[0][0] + own[1][1] + own[2][2]
        coupled = tables[0][comp_i][0] + tables[1][comp_i][1] + tables[2][comp_i][2]
        centre = padded[comp_i][:, 1:-1, 1:-1]
        upper_diff = centre[2:] - centre[1:-1]
        lower_diff = centre[1:-1] - centre[:-2]
        geometric = faces_load[1:] * upper_diff - faces_load[:-1] * lower_diff
        forces.append(shear * laplace + (lame + shear) * coupled - geometric)
    return jnp.stack(forces)


def expand(values, width):
    zcount, xcount, ycount = values.shape
    spread = jnp.broadcast_to(
        values[:, None, :, None, :, None], (zcount, width, xcount, width, ycount, width)
    )
    return spread.reshape(zcount * width, xcount * width, ycount * width)


def lookup(materials, table):
    onehot = (materials[..., None] == jnp.arange(table.shape[0], dtype=jnp.int32)).astype(
        jnp.float32
    )
    return jnp.sum(onehot * table, -1)


def add_arrays(first_term, second_term):
    return first_term + second_term


def carried_mass(totals):
    return prefix(totals, "story", add_arrays, jnp.zeros_like(totals))


def local(u_now, u_prev, occupancy, materials, shear_table, lame_table, density_table):
    height = u_now.shape[1] * lax.axis_size("story")
    factor = 0.8 / height
    occupied = expand(occupancy.astype(jnp.float32), BLOCK)
    shear = expand(lookup(materials, shear_table), BLOCK)
    lame = expand(lookup(materials, lame_table), BLOCK)
    density = expand(lookup(materials, density_table), BLOCK)
    mass = density * occupied
    local_above = jnp.cumsum(mass[::-1], axis=0)[::-1]
    carried = carried_mass(jnp.sum(mass, 0))
    faces_load = factor * jnp.concatenate([local_above + carried[None], carried[None]], 0)
    earlier = occupied * u_prev
    current = occupied * u_now
    for section in range(STEPS):
        extended = padded_2(current, (("story", 1), ("plan", 2)), 1)
        padded = jnp.pad(extended, ((0, 0), (0, 0), (0, 0), (1, 1)))
        forces = stiffness(padded, shear, lame, faces_load)
        following = occupied * (2.0 * current - earlier + 0.1 * forces / density)
        earlier = current
        current = following
    return current


def solution(mesh):
    in_specs = (
        P(None, "story", "plan", None),
        P(None, "story", "plan", None),
        P("story", "plan", None),
        P("story", "plan", None),
        P(),
        P(),
        P(),
    )
    out_specs = P(None, "story", "plan", None)
    return jax.shard_map(local, mesh=mesh, in_specs=in_specs, out_specs=out_specs, check_vma=False)
```

profile of v0, /device:TPU:25, one launch (start us, length us, event | category | flops | bytes accessed | tf_op | source)
XLA Modules:
  0.0 107.2 jit_solution(15143102684160313562)
XLA Ops:
  0.0 0.7 convert_bitcast_fusion
  0.7 0.1 broadcast_in_dim.57
  0.7 0.1 broadcast_in_dim.58
  0.8 1.2 %broadcast_multiply_fusion = f32[3,16,16,256]{3,2,1,0:T(8,128)S(1)} fusion(f32[3,16,16,256]{3,2,1,0:T(8,128)} %param.9, f32[256]{0:T(256)S(1)} %broadcast_in_dim.58), kind=kLoop, calls=%fused_computation.136 | loop fusion | flops 196608 | bytes 1573888 | tf_op jit(solution)/shard_map/mul | solution.py:122
  2.0 4.1 %collective-permute-start = (f32[3,1,16,256]{3,2,1,0:T(8,128)S(1)}, f32[3,1,16,256]{3,2,1,0:T(8,128)S(1)}, u32[]{:S(2)}, u32[]{:S(2)}) collective-permute-start(f32[3,1,16,256]{3,2,1,0:T(8,128)S(1)} %get-tuple-element.103), channel_id=1, source_target_pairs={{0,8},{8,16},{16,24},{24,32},{32,40},{40,48},{48,56},{56,64},{64,7... | collective-permute-start | bytes 147464 | tf_op jit(solution)/shard_map/ppermute | solution.py:32
  6.2 1.9 %collective-permute-start.1 = (f32[3,1,16,256]{3,2,1,0:T(8,128)S(1)}, f32[3,1,16,256]{3,2,1,0:T(8,128)S(1)}, u32[]{:S(2)}, u32[]{:S(2)}) collective-permute-start(f32[3,1,16,256]{3,2,1,0:T(8,128)S(1)} %get-tuple-element.104), channel_id=1, source_target_pairs={{8,0},{16,8},{24,16},{32,24},{40,32},{48,40},{56,48},{64,56},{72,6... | collective-permute-start | bytes 147464 | tf_op jit(solution)/shard_map/ppermute | solution.py:34
  8.1 0.8 select_reduce_fusion.2
  8.9 0.7 multiply_multiply_fusion
  9.5 0.1 broadcast_in_dim.65
  9.6 0.1 broadcast_in_dim.66
  9.8 1.4 %fusion.165 = f32[16,16,256]{2,1,0:T(8,128)S(1)} fusion(f32[16,16,256]{2,1,0:T(8,128)S(1)} %rev.6), kind=kOutput, calls=%fused_computation.332 | output fusion | flops 983040 | bytes 524288 | tf_op jit(solution)/shard_map/jit(cumsum)/reduce_window_sum | solution.py:118
  11.1 0.1 reduce_sum.40
  11.2 0.1 reshape.256
  11.3 44.4 %all-gather.1 = f32[32,1,256]{2,1,0:T(1,128)S(1)} all-gather(f32[1,1,256]{2,1,0:T(1,128)S(1)} %reshape.256), channel_id=3, replica_groups=mesh['story'=32,'plan'=8] {'story'}, dimensions={0}, use_global_device_ids=true | all-gather | bytes 33792 | tf_op jit(solution)/shard_map/all_gather | solution.py:14
  55.8 1.3 %while.12 = (s32[]{:T(128)}, f32[16,256]{1,0:T(8,128)S(1)}, s32[]{:T(128)}, f32[32,16,256]{2,1,0:T(8,128)S(1)}, s32[]{:T(128)}, /*index=5*/s32[]{:T(128)}, s32[]{:T(128)}, s32[]{:T(128)}) while((s32[]{:T(128)}, f32[16,256]{1,0:T(8,128)S(1)}, s32[]{:T(128)}, f32[32,16,256]{2,1,0:T(8,128)S(1)}, s32[]{:T(128)}, /*index=5*/s32[]{:T(128)}, ...), condition=%wide.region_5.6_spmd, body=%wide.region_4.5_spmd.sunk | while | flops 4102 | bytes 49287 | solution.py:21
  57.1 0.1 pad_maximum_fusion.5
  57.2 5.8 %collective-permute-start.2 = (f32[3,18,1,256]{3,2,1,0:T(1,128)S(1)}, f32[3,18,1,256]{3,2,1,0:T(1,128)S(1)}, u32[]{:S(2)}, u32[]{:S(2)}) collective-permute-start(f32[3,18,1,256]{3,2,1,0:T(1,128)S(1)} %get-tuple-element.99), channel_id=1, source_target_pairs={{0,1},{1,2},{2,3},{3,4},{4,5},{5,6},{6,7},{8,9},{9,10},{10,11},{11... | collective-permute-start | bytes 165896 | tf_op jit(solution)/shard_map/ppermute | solution.py:32
  63.0 1.9 %collective-permute-start.3 = (f32[3,18,1,256]{3,2,1,0:T(1,128)S(1)}, f32[3,18,1,256]{3,2,1,0:T(1,128)S(1)}, u32[]{:S(2)}, u32[]{:S(2)}) collective-permute-start(f32[3,18,1,256]{3,2,1,0:T(1,128)S(1)} %get-tuple-element.100), channel_id=1, source_target_pairs={{1,0},{2,1},{3,2},{4,3},{5,4},{6,5},{7,6},{9,8},{10,9},{11,10},{12... | collective-permute-start | bytes 165896 | tf_op jit(solution)/shard_map/ppermute | solution.py:34
  64.9 0.1 broadcast_in_dim.59
  65.0 0.1 broadcast_in_dim.60
  65.1 0.1 broadcast_in_dim.62
  65.2 0.1 broadcast_in_dim.63
  65.3 8.6 %collective-permute-done.3 = f32[3,18,1,256]{3,2,1,0:T(1,128)S(1)} collective-permute-done((f32[3,18,1,256]{3,2,1,0:T(1,128)S(1)}, f32[3,18,1,256]{3,2,1,0:T(1,128)S(1)}, u32[]{:S(2)}, u32[]{:S(2)}) %collective-permute-start.3) | collective-permute-done | bytes 55328 | tf_op jit(solution)/shard_map/ppermute | solution.py:34
  73.9 1.0 select_maximum_fusion.4
  74.9 0.4 fusion.24
  75.3 0.1 fusion.23
  75.5 0.1 slice_bitcast_fusion.5
  75.6 0.2 subtract_add_fusion.4
  75.8 0.3 subtract_multiply_fusion.10
  76.1 0.2 fusion.44
  76.2 0.3 subtract_multiply_fusion.11
  76.5 0.2 fusion.40
  76.7 0.9 fusion.146
  77.6 0.9 fusion.126
  78.6 0.0 copy-start
  78.6 0.0 copy-start.1
  78.6 0.8 fusion.109
  79.4 0.3 copy-done
  79.7 0.2 copy-done.1
  79.9 0.3 fusion.3
  80.2 1.9 %collective-permute-start.4 = (f32[3,1,16,256]{3,2,1,0:T(8,128)S(1)}, f32[3,1,16,256]{3,2,1,0:T(8,128)S(1)}, u32[]{:S(2)}, u32[]{:S(2)}) collective-permute-start(f32[3,1,16,256]{3,2,1,0:T(8,128)S(1)} %get-tuple-element.101), channel_id=1, source_target_pairs={{0,8},{8,16},{16,24},{24,32},{32,40},{40,48},{48,56},{56,64},{64,7... | collective-permute-start | bytes 147464 | tf_op jit(solution)/shard_map/ppermute | solution.py:32
  82.2 2.9 %collective-permute-start.5 = (f32[3,1,16,256]{3,2,1,0:T(8,128)S(1)}, f32[3,1,16,256]{3,2,1,0:T(8,128)S(1)}, u32[]{:S(2)}, u32[]{:S(2)}) collective-permute-start(f32[3,1,16,256]{3,2,1,0:T(8,128)S(1)} %get-tuple-element.102), channel_id=1, source_target_pairs={{8,0},{16,8},{24,16},{32,24},{40,32},{48,40},{56,48},{64,56},{72,6... | collective-permute-start | bytes 147464 | tf_op jit(solution)/shard_map/ppermute | solution.py:34
  85.1 2.4 %collective-permute-done.5 = f32[3,1,16,256]{3,2,1,0:T(8,128)S(1)} collective-permute-done((f32[3,1,16,256]{3,2,1,0:T(8,128)S(1)}, f32[3,1,16,256]{3,2,1,0:T(8,128)S(1)}, u32[]{:S(2)}, u32[]{:S(2)}) %collective-permute-start.5) | collective-permute-done | bytes 49184 | tf_op jit(solution)/shard_map/ppermute | solution.py:34
  87.6 0.1 pad_maximum_fusion.2
  87.7 1.9 %collective-permute-start.6 = (f32[3,18,1,256]{3,2,1,0:T(1,128)S(1)}, f32[3,18,1,256]{3,2,1,0:T(1,128)S(1)}, u32[]{:S(2)}, u32[]{:S(2)}) collective-permute-start(f32[3,18,1,256]{3,2,1,0:T(1,128)S(1)} %get-tuple-element.97), channel_id=1, source_target_pairs={{0,1},{1,2},{2,3},{3,4},{4,5},{5,6},{6,7},{8,9},{9,10},{10,11},{11... | collective-permute-start | bytes 165896 | tf_op jit(solution)/shard_map/ppermute | solution.py:32
  89.6 3.5 %collective-permute-start.7 = (f32[3,18,1,256]{3,2,1,0:T(1,128)S(1)}, f32[3,18,1,256]{3,2,1,0:T(1,128)S(1)}, u32[]{:S(2)}, u32[]{:S(2)}) collective-permute-start(f32[3,18,1,256]{3,2,1,0:T(1,128)S(1)} %get-tuple-element.98), channel_id=1, source_target_pairs={{1,0},{2,1},{3,2},{4,3},{5,4},{6,5},{7,6},{9,8},{10,9},{11,10},{12... | collective-permute-start | bytes 165896 | tf_op jit(solution)/shard_map/ppermute | solution.py:34
  93.1 7.4 %collective-permute-done.7 = f32[3,18,1,256]{3,2,1,0:T(1,128)S(1)} collective-permute-done((f32[3,18,1,256]{3,2,1,0:T(1,128)S(1)}, f32[3,18,1,256]{3,2,1,0:T(1,128)S(1)}, u32[]{:S(2)}, u32[]{:S(2)}) %collective-permute-start.7) | collective-permute-done | bytes 55328 | tf_op jit(solution)/shard_map/ppermute | solution.py:34
  100.5 1.0 select_maximum_fusion
  101.5 0.4 fusion.15
  102.0 0.1 slice_bitcast_fusion.2
  102.1 0.1 fusion.14
  102.2 0.1 fusion.32
  102.3 0.1 fusion.34
  102.4 0.1 fusion.35
  102.5 0.1 subtract_add_fusion.2
  102.7 0.2 subtract_add_fusion.1
  102.8 0.2 subtract_multiply_fusion.7
  103.0 0.1 fusion.30
  103.1 0.1 subtract_multiply_fusion.8
  103.3 0.1 fusion.28
  103.4 0.9 fusion.89
  104.3 0.9 fusion.69
  105.2 0.8 fusion.52
  106.1 1.2 %fusion.6 = f32[3,16,16,256]{3,2,1,0:T(8,128)} fusion(f32[1,16,16,256]{3,2,1,0:T(8,128)S(1)} %fusion.52, f32[1,16,16,256]{3,2,1,0:T(8,128)S(1)} %fusion.69, f32[1,16,16,256]{3,2,1,0:T(8,128)S(1)} %fusion.89, f32[3,16,16,256]{3,2,1,0:T(8,128)S(1)} %fusion.3, f32[256]{0:T(256)S(1)} %broadcast_in_dim.66, f32[256]{0:T(256)S(1)} %broadcast_in_dim.58, ...), kind=kLoop, calls=%fused_computation.19 | loop fusion | flops 1769472 | bytes 3147776 | tf_op jit(solution)/shard_map/mul | solution.py:127
  (46 shorter events, 0.5 us)
Async XLA Ops:
  2.0 55.0 %collective-permute-start = (f32[3,1,16,256]{3,2,1,0:T(8,128)S(1)}, f32[3,1,16,256]{3,2,1,0:T(8,128)S(1)}, u32[]{:S(2)}, u32[]{:S(2)}) collective-permute-start(f32[3,1,16,256]{3,2,1,0:T(8,128)S(1)} %get-tuple-element.103), channel_id=1, source_target_pairs={{0,8},{8,16},{16,24},{24,32},{32,40},{40,48},{48,56},{56,64},{64,7... | collective-permute-start | bytes 147464 | tf_op jit(solution)/shard_map/ppermute | solution.py:32
  6.2 50.9 %collective-permute-start.1 = (f32[3,1,16,256]{3,2,1,0:T(8,128)S(1)}, f32[3,1,16,256]{3,2,1,0:T(8,128)S(1)}, u32[]{:S(2)}, u32[]{:S(2)}) collective-permute-start(f32[3,1,16,256]{3,2,1,0:T(8,128)S(1)} %get-tuple-element.104), channel_id=1, source_target_pairs={{8,0},{16,8},{24,16},{32,24},{40,32},{48,40},{56,48},{64,56},{72,6... | collective-permute-start | bytes 147464 | tf_op jit(solution)/shard_map/ppermute | solution.py:34
  57.2 8.1 %collective-permute-start.2 = (f32[3,18,1,256]{3,2,1,0:T(1,128)S(1)}, f32[3,18,1,256]{3,2,1,0:T(1,128)S(1)}, u32[]{:S(2)}, u32[]{:S(2)}) collective-permute-start(f32[3,18,1,256]{3,2,1,0:T(1,128)S(1)} %get-tuple-element.99), channel_id=1, source_target_pairs={{0,1},{1,2},{2,3},{3,4},{4,5},{5,6},{6,7},{8,9},{9,10},{10,11},{11... | collective-permute-start | bytes 165896 | tf_op jit(solution)/shard_map/ppermute | solution.py:32
  63.0 10.9 %collective-permute-start.3 = (f32[3,18,1,256]{3,2,1,0:T(1,128)S(1)}, f32[3,18,1,256]{3,2,1,0:T(1,128)S(1)}, u32[]{:S(2)}, u32[]{:S(2)}) collective-permute-start(f32[3,18,1,256]{3,2,1,0:T(1,128)S(1)} %get-tuple-element.100), channel_id=1, source_target_pairs={{1,0},{2,1},{3,2},{4,3},{5,4},{6,5},{7,6},{9,8},{10,9},{11,10},{12... | collective-permute-start | bytes 165896 | tf_op jit(solution)/shard_map/ppermute | solution.py:34
  78.6 1.1 %copy-start = (f32[3,16,16,256]{3,2,1,0:T(8,128)S(1)}, f32[3,16,16,256]{3,2,1,0:T(8,128)}, u32[]{:S(2)}) copy-start(f32[3,16,16,256]{3,2,1,0:T(8,128)} %param.9) | copy-start | bytes 2359300
  78.6 1.4 %copy-start.1 = (f32[3,16,16,256]{3,2,1,0:T(8,128)S(1)}, f32[3,16,16,256]{3,2,1,0:T(8,128)}, u32[]{:S(2)}) copy-start(f32[3,16,16,256]{3,2,1,0:T(8,128)} %param.10) | copy-start | bytes 2359300
  80.2 4.9 %collective-permute-start.4 = (f32[3,1,16,256]{3,2,1,0:T(8,128)S(1)}, f32[3,1,16,256]{3,2,1,0:T(8,128)S(1)}, u32[]{:S(2)}, u32[]{:S(2)}) collective-permute-start(f32[3,1,16,256]{3,2,1,0:T(8,128)S(1)} %get-tuple-element.101), channel_id=1, source_target_pairs={{0,8},{8,16},{16,24},{24,32},{32,40},{40,48},{48,56},{56,64},{64,7... | collective-permute-start | bytes 147464 | tf_op jit(solution)/shard_map/ppermute | solution.py:32
  82.2 5.4 %collective-permute-start.5 = (f32[3,1,16,256]{3,2,1,0:T(8,128)S(1)}, f32[3,1,16,256]{3,2,1,0:T(8,128)S(1)}, u32[]{:S(2)}, u32[]{:S(2)}) collective-permute-start(f32[3,1,16,256]{3,2,1,0:T(8,128)S(1)} %get-tuple-element.102), channel_id=1, source_target_pairs={{8,0},{16,8},{24,16},{32,24},{40,32},{48,40},{56,48},{64,56},{72,6... | collective-permute-start | bytes 147464 | tf_op jit(solution)/shard_map/ppermute | solution.py:34
  87.7 5.5 %collective-permute-start.6 = (f32[3,18,1,256]{3,2,1,0:T(1,128)S(1)}, f32[3,18,1,256]{3,2,1,0:T(1,128)S(1)}, u32[]{:S(2)}, u32[]{:S(2)}) collective-permute-start(f32[3,18,1,256]{3,2,1,0:T(1,128)S(1)} %get-tuple-element.97), channel_id=1, source_target_pairs={{0,1},{1,2},{2,3},{3,4},{4,5},{5,6},{6,7},{8,9},{9,10},{10,11},{11... | collective-permute-start | bytes 165896 | tf_op jit(solution)/shard_map/ppermute | solution.py:32
  89.6 10.9 %collective-permute-start.7 = (f32[3,18,1,256]{3,2,1,0:T(1,128)S(1)}, f32[3,18,1,256]{3,2,1,0:T(1,128)S(1)}, u32[]{:S(2)}, u32[]{:S(2)}) collective-permute-start(f32[3,18,1,256]{3,2,1,0:T(1,128)S(1)} %get-tuple-element.98), channel_id=1, source_target_pairs={{1,0},{2,1},{3,2},{4,3},{5,4},{6,5},{7,6},{9,8},{10,9},{11,10},{12... | collective-permute-start | bytes 165896 | tf_op jit(solution)/shard_map/ppermute | solution.py:34
where the time goes:
time: 108 us; the launch traced here: 107 us
  blocking collectives  44.4 us (41%)
  starting transfers between devices  24.1 us (22%)
  waiting for transfers between devices  18.4 us (17%)
  other arithmetic  17.3 us (16%)
  local copies, waits for them, and re-layouts  1.64 us (2%)
    all_gather x1, blocking collectives, prefix(): gathered = lax.all_gather(part, axis)  44.4 us
    ppermute x4, waiting for transfers between devices, padded_2(): lax.ppermute(head, axis, [((i + 1) % count, i) for i in range(ends)])  18.4 us
    ppermute x4, starting transfers between devices, padded_2(): lax.ppermute(tail, axis, [(i, (i + 1) % count) for i in range(ends)])  13.7 us
    ppermute x4, starting transfers between devices, padded_2(): lax.ppermute(head, axis, [((i + 1) % count, i) for i in range(ends)])  10.3 us
    another operation x6, other arithmetic, stiffness(): return jnp.stack(forces)  5.33 us
  transfers between devices with their start and end apart: 8, of which 3 were waited for; matrix products, arithmetic and copies ran while one was open for 4% of the time, Pallas kernels for 0%

commit v1 on v0

v1 whole, which is shorter than its diff:
```python
import functools

import jax
import jax.numpy as jnp
from jax import lax
from jax.experimental import pallas as pl
from jax.experimental.pallas import tpu as pltpu
from jax.sharding import PartitionSpec as P

BLOCK = 16
WIDE = 256
PAD = 24
F32 = jnp.float32


def swap(values, axis, first):
    pairs = []
    for low in range(first, lax.axis_size(axis) - 1, 2):
        pairs += [(low, low + 1), (low + 1, low)]
    return lax.ppermute(values, axis, pairs)


def row_shift(v):
    rows = v.shape[0]
    return pltpu.roll(v, 1, 0), pltpu.roll(v, rows - 1, 0)


def lane_shift(v):
    lane = lax.broadcasted_iota(jnp.int32, v.shape, 1)
    lower = jnp.where(lane == 0, 0.0, pltpu.roll(v, 1, 1))
    upper = jnp.where(lane == WIDE - 1, 0.0, pltpu.roll(v, WIDE - 1, 1))
    return lower, upper


def lane_smooth(v):
    lower, upper = lane_shift(v)
    return lower + upper + 4.0 * v


def lane_first(v):
    lower, upper = lane_shift(v)
    return upper - lower


def stencil(below, here, above, sign=None):
    zs = [lo + up + 4.0 * mid for lo, mid, up in zip(below, here, above)]
    zf = [up - lo for lo, up in zip(below, above)]
    if sign is not None:
        zf = [sign * v for v in zf]
    zs_sh = [row_shift(v) for v in zs]
    zf_sh = [row_shift(v) for v in zf]
    mid_sh = [row_shift(v) for v in here]
    s_zs = [lo + up + 4.0 * v for (lo, up), v in zip(zs_sh, zs)]
    s_mid = [lo + up + 4.0 * v for (lo, up), v in zip(mid_sh, here)]
    lap = []
    for j in range(3):
        inner = s_zs[j] - 2.0 * (s_mid[j] + zs[j])
        lap.append(lane_smooth(inner) - 2.0 * s_zs[j])
    f_zf0 = zf_sh[0][1] - zf_sh[0][0]
    f_zf1 = zf_sh[1][1] - zf_sh[1][0]
    s_zf0 = zf_sh[0][0] + zf_sh[0][1] + 4.0 * zf[0]
    s_zf2 = zf_sh[2][0] + zf_sh[2][1] + 4.0 * zf[2]
    f_zs1 = zs_sh[1][1] - zs_sh[1][0]
    f_zs2 = zs_sh[2][1] - zs_sh[2][0]
    c0 = lane_smooth(2.0 * s_zs[0] - 12.0 * s_mid[0] + 3.0 * f_zf1) + lane_first(3.0 * s_zf2)
    c1 = lane_smooth(2.0 * s_zs[1] - 12.0 * zs[1] + 3.0 * f_zf0) + lane_first(3.0 * f_zs2)
    c2 = lane_first(3.0 * (s_zf0 + f_zs1)) + 2.0 * lane_smooth(s_zs[2]) - 12.0 * s_zs[2]
    return lap, [c0, c1, c2]


def coefficients(own, over, under, carried):
    z = lax.broadcasted_iota(jnp.int32, (PAD, WIDE), 0) - 4
    zf = z.astype(F32)

    def pick(k):
        return jnp.where(z < 0, under[k], jnp.where(z > 15, over[k], own[k]))

    a, b, g = pick(0), pick(1), pick(2)
    mass, mass_over, mass_under = own[3], over[3], under[3]
    upper = jnp.where(z > 15, carried - mass_over, carried + mass * (15.0 - zf))
    lower = jnp.where(z < 0, carried + 16.0 * mass + mass_under, carried + mass * (16.0 - zf))
    return a, b, g * upper, g * lower


def prep_kernel(place, occ, mat, shear_t, lame_t, dens_t, now, prev, se, so, masses, consts, held_now, held_prev, sems, *, factor):
    top_first = place[0] % 2 == 0
    copies = []
    for k in range(2):
        top = jnp.logical_xor(top_first, k == 1)
        copies.append(pltpu.make_async_copy(now.at[:, pl.ds(jnp.where(top, 14, 0), 2)], held_now.at[k], sems.at[2 * k]))
        copies.append(pltpu.make_async_copy(prev.at[:, pl.ds(jnp.where(top, 15, 0), 1)], held_prev.at[k], sems.at[2 * k + 1]))
    for copy in copies:
        copy.start()
    block = lax.broadcasted_iota(jnp.int32, (1, WIDE), 1) // BLOCK
    zero = jnp.zeros((1, WIDE), F32)
    occupied, shear, lame, dens = zero, zero, zero, zero
    for j in range(BLOCK):
        at = block == j
        which = mat[j]
        occupied = jnp.where(at, occ[j].astype(F32), occupied)
        shear = jnp.where(at, shear_t[which], shear)
        lame = jnp.where(at, lame_t[which], lame)
        dens = jnp.where(at, dens_t[which], dens)
    scale = occupied * (0.1 / dens)
    own = [scale * shear * (1.0 / 12.0), scale * (lame + shear) * (1.0 / 72.0), scale * factor, dens * occupied, occupied]
    for k, row in enumerate(own):
        consts[k : k + 1, :] = row
    consts[5:8, :] = jnp.zeros((3, WIDE), F32)
    masses[...] = jnp.broadcast_to(own[3], masses.shape)
    for copy in copies:
        copy.wait()
    for k, out in enumerate((se, so)):
        top = jnp.logical_xor(top_first, k == 1)
        for c in range(3):
            first, second = held_now[k, c, 0] * occupied, held_now[k, c, 1] * occupied
            out[c] = jnp.where(top, second, first)
            out[3 + c] = jnp.where(top, first, second)
            out[6 + c] = held_prev[k, c, 0] * occupied
        out[9, 0:8] = consts[...]


def pack_kernel(place, consts, se, so, masses, now, prev, pe, po, carried_out):
    even_story = place[0] % 2 == 0
    step = lax.broadcasted_iota(jnp.int32, masses.shape, 0)
    carried = 16.0 * jnp.sum(jnp.where(step > place[0], masses[...], 0.0), 0, keepdims=True)
    carried_out[...] = jnp.broadcast_to(carried, carried_out.shape)
    occupied = consts[4:5, :]

    def ghost(plane, x, over):
        take = even_story if over else jnp.logical_not(even_story)
        return jnp.where(take, se[plane, x : x + 1, :], so[plane, x : x + 1, :])

    def fill(out, near, far):
        for c in range(3):
            for kind, source, x in ((0, now, near), (3, now, far), (6, prev, near)):
                plane = kind + c
                base = plane * PAD
                out[base + 4 : base + 20, :] = source[c, :, x, :] * occupied
                if kind < 6:
                    out[base + 3 : base + 4, :] = ghost(c, x, False)
                    out[base + 2 : base + 3, :] = ghost(3 + c, x, False)
                    out[base + 20 : base + 21, :] = ghost(c, x, True)
                    out[base + 21 : base + 22, :] = ghost(3 + c, x, True)
                else:
                    out[base + 3 : base + 4, :] = ghost(6 + c, x, False)
                    out[base + 20 : base + 21, :] = ghost(6 + c, x, True)
        rows = (0, 1, 22, 23)
        for k, r in enumerate(rows):
            out[r : r + 1, :] = consts[k : k + 1, :]
            out[PAD + r : PAD + r + 1, :] = ghost(9, k, True)
            out[2 * PAD + r : 2 * PAD + r + 1, :] = ghost(9, k, False)
        out[3 * PAD : 3 * PAD + 1, :] = carried

    even_plan = place[1] % 2 == 0
    pe[...] = jnp.zeros(pe.shape, F32)
    po[...] = jnp.zeros(po.shape, F32)

    @pl.when(even_plan)
    def _():
        fill(pe, 15, 14)
        fill(po, 0, 1)

    @pl.when(jnp.logical_not(even_plan))
    def _():
        fill(pe, 0, 1)
        fill(po, 15, 14)


def pack_coefficients(pack):
    rows = (0, 1, 22, 23)
    sets = [[pack[k * PAD + r : k * PAD + r + 1, :] for r in rows] for k in range(3)]
    return coefficients(sets[0], sets[1], sets[2], pack[3 * PAD : 3 * PAD + 1, :])


def update(here, before, lap, coup, a, b, gu, gd, below, above):
    geometric = gu * (above - here) - gd * (here - below)
    return 2.0 * here - before + a * lap + b * coup - geometric


def main_kernel(place, consts, carried, se, so, now, prev, out, edge, u0, u1, before, coef):
    even_story = place[0] % 2 == 0

    def ghost(plane, over):
        take = even_story if over else jnp.logical_not(even_story)
        return jnp.where(take, se[plane], so[plane])

    own = [consts[k : k + 1, :] for k in range(4)]
    over_plane, under_plane = ghost(9, True), ghost(9, False)
    over = [over_plane[k : k + 1, :] for k in range(4)]
    under = [under_plane[k : k + 1, :] for k in range(4)]
    for k, rows in enumerate(coefficients(own, over, under, carried[0:1, :])):
        coef[k] = rows
    occupied = jnp.broadcast_to(consts[4:5, :], (16, WIDE))
    for c in range(3):
        u0[c, 0] = ghost(3 + c, False)
        u0[c, 1] = ghost(c, False)
        u0[c, 18] = ghost(c, True)
        u0[c, 19] = ghost(3 + c, True)
        before[c, 0] = ghost(6 + c, False)
        before[c, 17] = ghost(6 + c, True)

    @pl.loop(0, 16)
    def _(z):
        for c in range(3):
            u0[c, z + 2] = now[c, z] * occupied
            before[c, z + 1] = prev[c, z] * occupied

    @pl.loop(0, 18)
    def _(i):
        below = [u0[c, i] for c in range(3)]
        here = [u0[c, i + 1] for c in range(3)]
        above = [u0[c, i + 2] for c in range(3)]
        lap, coup = stencil(below, here, above)
        a, b, gu, gd = (coef[k, pl.ds(i + 3, 1), :] for k in range(4))
        for c in range(3):
            u1[c, i] = update(here[c], before[c, i], lap[c], coup[c], a, b, gu, gd, below[c], above[c])

    def level(c, i):
        return u1[c, i]

    @pl.loop(0, 16)
    def _(z):
        below = [level(c, z) for c in range(3)]
        here = [level(c, z + 1) for c in range(3)]
        above = [level(c, z + 2) for c in range(3)]
        lap, coup = stencil(below, here, above)
        a, b, gu, gd = (coef[k, pl.ds(z + 4, 1), :] for k in range(4))
        for c in range(3):
            out[c, z] = update(here[c], u0[c, z + 2], lap[c], coup[c], a, b, gu, gd, below[c], above[c])

    for k, x in enumerate((1, 2, 14, 13)):
        for c in range(3):
            base = (k * 3 + c) * PAD
            edge[base : base + 3, :] = jnp.zeros((3, WIDE), F32)
            edge[base + 3 : base + 21, :] = u1[c, :, x, :]
            edge[base + 21 : base + PAD, :] = jnp.zeros((3, WIDE), F32)


def tail_kernel(place, pe_sent, po_sent, pe_got, po_got, edge, inner, out):
    even_plan = place[1] % 2 == 0
    out[...] = inner[...]
    order = (1, 0, 2)

    def planes(ref, kind):
        return [ref[(kind + c) * PAD : (kind + c + 1) * PAD, :] for c in order]

    def advance(below, here, above, before, coefs, sign):
        a, b, gu, gd = coefs
        lap, coup = stencil(below, here, above, sign)
        news = []
        for c in range(3):
            lower, upper = row_shift(here[c])
            news.append(update(here[c], before[c], lap[c], coup[c], a, b, gu, gd, lower, upper))
        return news

    def one_side(sent, got, right, near, far):
        sign = 1.0 if right else -1.0
        base = 6 * PAD if right else 0

        def inner_plane(k):
            return [edge[base + (k * 3 + c) * PAD : base + (k * 3 + c + 1) * PAD, :] for c in order]

        own_coefs, got_coefs = pack_coefficients(sent), pack_coefficients(got)
        own_near, own_far = planes(sent, 0), planes(sent, 3)
        got_near, got_far = planes(got, 0), planes(got, 3)
        ghost_1 = advance(own_near, got_near, got_far, planes(got, 6), got_coefs, sign)
        near_1 = advance(own_far, own_near, got_near, planes(sent, 6), own_coefs, sign)
        near_2 = advance(inner_plane(0), near_1, ghost_1, own_near, own_coefs, sign)
        far_2 = advance(inner_plane(1), inner_plane(0), near_1, own_far, own_coefs, sign)
        for k, c in enumerate(order):
            out[c, :, near, :] = near_2[k][4:20]
            out[c, :, far, :] = far_2[k][4:20]

    @pl.when(even_plan)
    def _():
        one_side(pe_sent, pe_got, True, 15, 14)
        one_side(po_sent, po_got, False, 0, 1)

    @pl.when(jnp.logical_not(even_plan))
    def _():
        one_side(pe_sent, pe_got, False, 0, 1)
        one_side(po_sent, po_got, True, 15, 14)


VM = pl.BlockSpec(memory_space=pltpu.VMEM)
SM = pl.BlockSpec(memory_space=pltpu.SMEM)
HB = pl.BlockSpec(memory_space=pl.ANY)


def shape(*dims):
    return jax.ShapeDtypeStruct(dims, F32)


def call(kernel, outs, ins, scratch=(), flops=0, moved=0):
    return pl.pallas_call(
        kernel,
        out_shape=outs,
        in_specs=ins,
        out_specs=[VM] * len(outs),
        scratch_shapes=list(scratch),
        compiler_params=pltpu.CompilerParams(vmem_limit_bytes=24 * 2**20),
        cost_estimate=pl.CostEstimate(flops=flops, bytes_accessed=moved, transcendentals=0),
    )


def local(u_now, u_prev, occupancy, materials, shear_table, lame_table, density_table):
    height = u_now.shape[1] * lax.axis_size("story")
    stories = lax.axis_size("story")
    place = jnp.stack([lax.axis_index("story"), lax.axis_index("plan")]).astype(jnp.int32)
    face, slab = shape(10, 16, WIDE), shape(9 * PAD, WIDE)
    se, so, masses, consts = call(
        functools.partial(prep_kernel, factor=0.8 / height),
        [face, face, shape(stories, WIDE), shape(8, WIDE)],
        [SM] * 6 + [HB] * 2,
        [pltpu.VMEM((2, 3, 2, 16, WIDE), F32), pltpu.VMEM((2, 3, 1, 16, WIDE), F32), pltpu.SemaphoreType.DMA((4,))],
        moved=1 << 20,
    )(place, occupancy.reshape(-1), materials.reshape(-1), shear_table, lame_table, density_table, u_now, u_prev)
    so_got = swap(so, "story", 1)
    se_got = swap(se, "story", 0)
    masses = lax.all_to_all(masses, "story", 0, 0, tiled=True)
    cells = u_now.shape
    pe, po, carried = call(pack_kernel, [slab, slab, shape(8, WIDE)], [SM] + [VM] * 6, moved=2 << 20)(
        place, consts, se_got, so_got, masses, u_now, u_prev
    )
    po_got = swap(po, "plan", 1)
    pe_got = swap(pe, "plan", 0)
    inner, edge = call(
        main_kernel,
        [shape(*cells), shape(12 * PAD, WIDE)],
        [SM] + [VM] * 6,
        [
            pltpu.VMEM((3, 20, 16, WIDE), F32),
            pltpu.VMEM((3, 18, 16, WIDE), F32),
            pltpu.VMEM((3, 18, 16, WIDE), F32),
            pltpu.VMEM((4, PAD, WIDE), F32),
        ],
        flops=60_000_000,
        moved=4 << 20,
    )(place, consts, carried, se_got, so_got, u_now, u_prev)
    (out,) = call(tail_kernel, [shape(*cells)], [SM] + [VM] * 6, flops=10_000_000, moved=3 << 20)(
        place, pe, po, pe_got, po_got, edge, inner
    )
    return out


def solution(mesh):
    in_specs = (
        P(None, "story", "plan", None),
        P(None, "story", "plan", None),
        P("story", "plan", None),
        P("story", "plan", None),
        P(),
        P(),
        P(),
    )
    out_specs = P(None, "story", "plan", None)
    return jax.shard_map(local, mesh=mesh, in_specs=in_specs, out_specs=out_specs, check_vma=False)
```

time: 108 us -> 47 us (0.44)
  the two profiles are of different devices: /device:TPU:25 before, /device:TPU:57 now
where the time goes in v1:
time: 47 us; the launch traced here: 46.1 us
  blocking collectives  13.7 us (29%)
  starting transfers between devices  13 us (28%)
  Pallas kernels  11.2 us (24%)
  waiting for transfers between devices  5.1 us (11%)
  local copies, waits for them, and re-layouts  3.02 us (6%)
    all_to_all x1, blocking collectives, local(): masses = lax.all_to_all(masses, 'story', 0, 0, tiled=True)  13.7 us
    ppermute x4, starting transfers between devices, swap(): return lax.ppermute(values, axis, pairs)  13 us
    pallas_call x1, Pallas kernels, local(): call(main_kernel, [shape(*cells), shape(12 * PAD, WIDE)], [SM] + [VM] * 6...  6.55 us
    ppermute x4, waiting for transfers between devices, swap(): return lax.ppermute(values, axis, pairs)  5.1 us
    pallas_call x1, Pallas kernels, local(): call(tail_kernel, [shape(*cells)], [SM] + [VM] * 6, flops=10000000, moved...  3.07 us
    unnamed x19, local copies, waits for them, and re-layouts  2.98 us
  transfers between devices with their start and end apart: 4, of which 1 were waited for; matrix products, arithmetic and copies ran while one was open for 0% of the time, Pallas kernels for 14%

profile of v1, /device:TPU:57, one launch (start us, length us, event | category | flops | bytes accessed | tf_op | source)
XLA Modules:
  0.0 46.1 jit_solution(1902452096371125604)
XLA Ops:
  0.0 0.1 pad_add_fusion.place
  0.1 0.0 copy-start.7
  0.1 0.0 copy-start.8
  0.1 0.0 copy-start.4
  0.1 0.0 copy-start.5
  0.1 0.0 copy-start.6
  0.1 0.6 %copy-done.7 = f32[8]{0:T(128)S(1)} copy-done((f32[8]{0:T(128)S(1)}, f32[8]{0:T(128)}, u32[]{:S(2)}) %copy-start.7) | copy-done | bytes 56
  0.7 0.0 copy-done.8
  0.7 0.0 copy-done.4
  0.8 0.0 copy-done.5
  0.8 0.0 copy-done.6
  0.8 0.0 copy-start
  0.8 1.1 %copy-done = f32[3,16,16,256]{3,2,1,0:T(8,128)S(1)} copy-done((f32[3,16,16,256]{3,2,1,0:T(8,128)S(1)}, f32[3,16,16,256]{3,2,1,0:T(8,128)}, u32[]{:S(2)}) %copy-start) | copy-done | bytes 786456
  1.9 0.0 copy-start.2
  1.9 1.1 %copy-done.2 = f32[3,16,16,256]{3,2,1,0:T(8,128)S(1)} copy-done((f32[3,16,16,256]{3,2,1,0:T(8,128)S(1)}, f32[3,16,16,256]{3,2,1,0:T(8,128)}, u32[]{:S(2)}) %copy-start.2) | copy-done | bytes 786456
  3.1 0.0 copy-start.1
  3.1 0.0 copy-start.3
  3.1 0.8 %shard_map.73 = (f32[10,16,256]{2,1,0:T(8,128)S(1)}, f32[10,16,256]{2,1,0:T(8,128)S(1)}, f32[32,256]{1,0:T(8,128)S(1)}, f32[8,256]{1,0:T(8,128)S(1)}) custom-call(s32[2]{0:T(128)S(1)} %pad_add_fusion.place, s32[16]{0:T(128)S(1)} %bitcast.10, s32[16]{0:T(128)S(1)} %bitcast.11, f32[8]{0:T(128)S(1)} %copy-done.6, f32[8]{0:T(128)S(1)} %copy-done.7, ...), custom_call_target="tpu_custom_call" | custom-call | bytes 1048576 | tf_op jit(solution)/shard_map/pallas_call | solution.py:311
  3.9 0.8 %collective-permute-start = (f32[10,16,256]{2,1,0:T(8,128)S(1)}, f32[10,16,256]{2,1,0:T(8,128)S(1)}, u32[]{:S(2)}, u32[]{:S(2)}) collective-permute-start(f32[10,16,256]{2,1,0:T(8,128)S(1)} %get-tuple-element.15), channel_id=1, source_target_pairs={{0,8},{8,0},{16,24},{24,16},{32,40},{40,32},{48,56},{56,48},{64,72... | collective-permute-start | bytes 491528 | tf_op jit(solution)/shard_map/ppermute | solution.py:20
  4.7 3.4 %collective-permute-start.1 = (f32[10,16,256]{2,1,0:T(8,128)S(1)}, f32[10,16,256]{2,1,0:T(8,128)S(1)}, u32[]{:S(2)}, u32[]{:S(2)}) collective-permute-start(f32[10,16,256]{2,1,0:T(8,128)S(1)} %get-tuple-element.16), channel_id=1, source_target_pairs={{8,16},{16,8},{24,32},{32,24},{40,48},{48,40},{56,64},{64,56},{72,... | collective-permute-start | bytes 491528 | tf_op jit(solution)/shard_map/ppermute | solution.py:20
  8.2 13.7 %all_to_all.11 = f32[32,1,256]{2,1,0:T(1,128)S(1)} all-to-all(f32[32,1,256]{2,1,0:T(1,128)S(1)} %copy.8), channel_id=1, replica_groups=mesh['story'=32,'plan'=8] {'story'}, dimensions={0} | all-to-all | bytes 65536 | tf_op jit(solution)/shard_map/all_to_all | solution.py:320
  21.9 0.0 collective-permute-done.se
  21.9 0.0 collective-permute-done.1.so
  21.9 0.0 copy-done.1
  21.9 0.0 copy-done.3
  21.9 0.7 %shard_map.74 = (f32[216,256]{1,0:T(8,128)S(1)}, f32[216,256]{1,0:T(8,128)S(1)}, f32[8,256]{1,0:T(8,128)S(1)}) custom-call(s32[2]{0:T(128)S(1)} %pad_add_fusion.place, f32[8,256]{1,0:T(8,128)S(1)} %get-tuple-element.14.consts, f32[10,16,256]{2,1,0:T(8,128)S(1)} %collective-permute-done.se, f32[10,16,256]{2,1,0:T(8,128)S(1)} %collective-permute-done.1.so, ...), custom_call_target="tpu_custom_call" | custom-call | bytes 2097152 | tf_op jit(solution)/shard_map/pallas_call | solution.py:322
  22.6 0.5 %collective-permute-start.2 = (f32[216,256]{1,0:T(8,128)S(1)}, f32[216,256]{1,0:T(8,128)S(1)}, u32[]{:S(2)}, u32[]{:S(2)}) collective-permute-start(f32[216,256]{1,0:T(8,128)S(1)} %get-tuple-element.18.pe_sent), channel_id=1, source_target_pairs={{0,1},{1,0},{2,3},{3,2},{4,5},{5,4},{6,7},{7,6},{8,9},{9,8},{10,11... | collective-permute-start | bytes 663560 | tf_op jit(solution)/shard_map/ppermute | solution.py:20
  23.2 8.2 %collective-permute-start.3 = (f32[216,256]{1,0:T(8,128)S(1)}, f32[216,256]{1,0:T(8,128)S(1)}, u32[]{:S(2)}, u32[]{:S(2)}) collective-permute-start(f32[216,256]{1,0:T(8,128)S(1)} %get-tuple-element.19.po_sent), channel_id=1, source_target_pairs={{1,2},{2,1},{3,4},{4,3},{5,6},{6,5},{9,10},{10,9},{11,12},{12,11},... | collective-permute-start | bytes 663560 | tf_op jit(solution)/shard_map/ppermute | solution.py:20
  31.4 6.6 %shard_map.75 = (f32[3,16,16,256]{3,2,1,0:T(8,128)S(1)}, f32[288,256]{1,0:T(8,128)S(1)}) custom-call(s32[2]{0:T(128)S(1)} %pad_add_fusion.place, f32[8,256]{1,0:T(8,128)S(1)} %get-tuple-element.14.consts, f32[8,256]{1,0:T(8,128)S(1)} %get-tuple-element.20.carried, f32[10,16,256]{2,1,0:T(8,128)S(1)} %collective-permute-done.se, ...), custom_call_target="tpu_custom_call" | custom-call | flops 60000000 | bytes 4194304 | tf_op jit(solution)/shard_map/pallas_call | solution.py:327
  37.9 0.0 collective-permute-done.2.pe_got
  38.0 5.1 %collective-permute-done.3.po_got = f32[216,256]{1,0:T(8,128)S(1)} collective-permute-done((f32[216,256]{1,0:T(8,128)S(1)}, f32[216,256]{1,0:T(8,128)S(1)}, u32[]{:S(2)}, u32[]{:S(2)}) %collective-permute-start.3) | collective-permute-done | bytes 221216 | tf_op jit(solution)/shard_map/ppermute | solution.py:20
  43.0 3.1 %shard_map.76 = f32[3,16,16,256]{3,2,1,0:T(8,128)} custom-call(s32[2]{0:T(128)S(1)} %pad_add_fusion.place, f32[216,256]{1,0:T(8,128)S(1)} %get-tuple-element.18.pe_sent, f32[216,256]{1,0:T(8,128)S(1)} %get-tuple-element.19.po_sent, f32[216,256]{1,0:T(8,128)S(1)} %collective-permute-done.2.pe_got, f32[216,256]{1,0:T(8,128)S(1)} %collective-permute-done.3.po_got, ...), custom_call_target="tpu_custom_call" | custom-call | flops 10000000 | bytes 3145728 | tf_op jit(solution)/shard_map/pallas_call | solution.py:340
  (2 shorter events, 0.0 us)
Async XLA Ops:
  0.1 0.7 %copy-start.7 = (f32[8]{0:T(128)S(1)}, f32[8]{0:T(128)}, u32[]{:S(2)}) copy-start(f32[8]{0:T(128)} %lame_t.1) | copy-start | bytes 100
  0.1 0.7 %copy-start.8 = (f32[8]{0:T(128)S(1)}, f32[8]{0:T(128)}, u32[]{:S(2)}) copy-start(f32[8]{0:T(128)} %dens_t.1) | copy-start | bytes 100
  0.1 0.7 %copy-start.4 = (s32[1,1,16]{2,1,0:T(1,128)S(1)}, s32[1,1,16]{2,1,0:T(1,128)}, u32[]{:S(2)}) copy-start(s32[1,1,16]{2,1,0:T(1,128)} %param.9) | copy-start | bytes 196
  0.1 0.7 %copy-start.5 = (s32[1,1,16]{2,1,0:T(1,128)S(1)}, s32[1,1,16]{2,1,0:T(1,128)}, u32[]{:S(2)}) copy-start(s32[1,1,16]{2,1,0:T(1,128)} %param.10) | copy-start | bytes 196
  0.1 0.7 %copy-start.6 = (f32[8]{0:T(128)S(1)}, f32[8]{0:T(128)}, u32[]{:S(2)}) copy-start(f32[8]{0:T(128)} %shear_t.1) | copy-start | bytes 100
  0.8 1.1 %copy-start = (f32[3,16,16,256]{3,2,1,0:T(8,128)S(1)}, f32[3,16,16,256]{3,2,1,0:T(8,128)}, u32[]{:S(2)}) copy-start(f32[3,16,16,256]{3,2,1,0:T(8,128)} %now.5) | copy-start | bytes 2359300
  1.9 1.1 %copy-start.2 = (f32[3,16,16,256]{3,2,1,0:T(8,128)S(1)}, f32[3,16,16,256]{3,2,1,0:T(8,128)}, u32[]{:S(2)}) copy-start(f32[3,16,16,256]{3,2,1,0:T(8,128)} %prev.5) | copy-start | bytes 2359300
  3.1 18.8 %copy-start.1 = (f32[3,16,16,256]{3,2,1,0:T(8,128)S(1)}, f32[3,16,16,256]{3,2,1,0:T(8,128)}, u32[]{:S(2)}) copy-start(f32[3,16,16,256]{3,2,1,0:T(8,128)} %now.5) | copy-start | bytes 2359300
  3.1 18.8 %copy-start.3 = (f32[3,16,16,256]{3,2,1,0:T(8,128)S(1)}, f32[3,16,16,256]{3,2,1,0:T(8,128)}, u32[]{:S(2)}) copy-start(f32[3,16,16,256]{3,2,1,0:T(8,128)} %prev.5) | copy-start | bytes 2359300
  3.9 18.0 %collective-permute-start = (f32[10,16,256]{2,1,0:T(8,128)S(1)}, f32[10,16,256]{2,1,0:T(8,128)S(1)}, u32[]{:S(2)}, u32[]{:S(2)}) collective-permute-start(f32[10,16,256]{2,1,0:T(8,128)S(1)} %get-tuple-element.15), channel_id=1, source_target_pairs={{0,8},{8,0},{16,24},{24,16},{32,40},{40,32},{48,56},{56,48},{64,72... | collective-permute-start | bytes 491528 | tf_op jit(solution)/shard_map/ppermute | solution.py:20
  4.7 17.2 %collective-permute-start.1 = (f32[10,16,256]{2,1,0:T(8,128)S(1)}, f32[10,16,256]{2,1,0:T(8,128)S(1)}, u32[]{:S(2)}, u32[]{:S(2)}) collective-permute-start(f32[10,16,256]{2,1,0:T(8,128)S(1)} %get-tuple-element.16), channel_id=1, source_target_pairs={{8,16},{16,8},{24,32},{32,24},{40,48},{48,40},{56,64},{64,56},{72,... | collective-permute-start | bytes 491528 | tf_op jit(solution)/shard_map/ppermute | solution.py:20
  22.6 15.3 %collective-permute-start.2 = (f32[216,256]{1,0:T(8,128)S(1)}, f32[216,256]{1,0:T(8,128)S(1)}, u32[]{:S(2)}, u32[]{:S(2)}) collective-permute-start(f32[216,256]{1,0:T(8,128)S(1)} %get-tuple-element.18.pe_sent), channel_id=1, source_target_pairs={{0,1},{1,0},{2,3},{3,2},{4,5},{5,4},{6,7},{7,6},{8,9},{9,8},{10,11... | collective-permute-start | bytes 663560 | tf_op jit(solution)/shard_map/ppermute | solution.py:20
  23.2 19.9 %collective-permute-start.3 = (f32[216,256]{1,0:T(8,128)S(1)}, f32[216,256]{1,0:T(8,128)S(1)}, u32[]{:S(2)}, u32[]{:S(2)}) collective-permute-start(f32[216,256]{1,0:T(8,128)S(1)} %get-tuple-element.19.po_sent), channel_id=1, source_target_pairs={{1,2},{2,1},{3,4},{4,3},{5,6},{6,5},{9,10},{10,9},{11,12},{12,11},... | collective-permute-start | bytes 663560 | tf_op jit(solution)/shard_map/ppermute | solution.py:20

commit v2 on v1

v2 whole, which is shorter than its diff:
```python
import functools

import jax
import jax.numpy as jnp
from jax import lax
from jax.experimental import pallas as pl
from jax.experimental.pallas import tpu as pltpu
from jax.sharding import PartitionSpec as P

BLOCK = 16
WIDE = 256
PAD = 24
F32 = jnp.float32


def swap(values, axis, first):
    pairs = []
    for low in range(first, lax.axis_size(axis) - 1, 2):
        pairs += [(low, low + 1), (low + 1, low)]
    return lax.ppermute(values, axis, pairs)


def row_shift(v):
    count = v.shape[0] // 8
    row = lax.broadcasted_iota(jnp.int32, (8, v.shape[1]), 0)
    tiles = [v[8 * k : 8 * k + 8] for k in range(count)]
    down = [jnp.zeros_like(tiles[0])] + [pltpu.roll(t, 1, 0) for t in tiles]
    up = [pltpu.roll(t, 7, 0) for t in tiles] + [jnp.zeros_like(tiles[0])]
    lower = [jnp.where(row == 0, down[k], down[k + 1]) for k in range(count)]
    upper = [jnp.where(row == 7, up[k + 1], up[k]) for k in range(count)]
    return jnp.concatenate(lower, 0), jnp.concatenate(upper, 0)


def lane_shift(v):
    half = WIDE // 2
    lane = lax.broadcasted_iota(jnp.int32, (v.shape[0], half), 1)
    first, second = v[:, :half], v[:, half:]
    first_down, second_down = pltpu.roll(first, 1, 1), pltpu.roll(second, 1, 1)
    first_up, second_up = pltpu.roll(first, half - 1, 1), pltpu.roll(second, half - 1, 1)
    lower = [jnp.where(lane == 0, 0.0, first_down), jnp.where(lane == 0, first_down, second_down)]
    upper = [jnp.where(lane == half - 1, second_up, first_up), jnp.where(lane == half - 1, 0.0, second_up)]
    return jnp.concatenate(lower, 1), jnp.concatenate(upper, 1)


def lane_smooth(v):
    lower, upper = lane_shift(v)
    return lower + upper + 4.0 * v


def lane_first(v):
    lower, upper = lane_shift(v)
    return upper - lower


def total(terms):
    terms = [t for t in terms if t is not None]
    return functools.reduce(lambda p, q: p + q, terms)


def stencil(below, here, above, sign=None):
    zs, zf = [], []
    for j in range(3):
        zs.append(total([below and below[j], above and above[j], here and 4.0 * here[j]]))
        if below and above:
            zf.append(above[j] - below[j])
        else:
            zf.append(above[j] if above else -below[j])
    if sign is not None:
        zf = [sign * v for v in zf]
    zs_sh = [row_shift(v) for v in zs]
    zf_sh = [row_shift(v) for v in zf]
    s_zs = [lo + up + 4.0 * v for (lo, up), v in zip(zs_sh, zs)]
    lap = []
    if here:
        s_mid = [lo + up + 4.0 * v for (lo, up), v in zip([row_shift(v) for v in here], here)]
        inner = [s_zs[j] - 2.0 * (s_mid[j] + zs[j]) for j in range(3)]
        curl = 2.0 * s_zs[0] - 12.0 * s_mid[0]
    else:
        inner = [s_zs[j] - 2.0 * zs[j] for j in range(3)]
        curl = 2.0 * s_zs[0]
    for j in range(3):
        lap.append(lane_smooth(inner[j]) - 2.0 * s_zs[j])
    f_zf0 = zf_sh[0][1] - zf_sh[0][0]
    f_zf1 = zf_sh[1][1] - zf_sh[1][0]
    s_zf0 = zf_sh[0][0] + zf_sh[0][1] + 4.0 * zf[0]
    s_zf2 = zf_sh[2][0] + zf_sh[2][1] + 4.0 * zf[2]
    f_zs1 = zs_sh[1][1] - zs_sh[1][0]
    f_zs2 = zs_sh[2][1] - zs_sh[2][0]
    c0 = lane_smooth(curl + 3.0 * f_zf1) + lane_first(3.0 * s_zf2)
    c1 = lane_smooth(2.0 * s_zs[1] - 12.0 * zs[1] + 3.0 * f_zf0) + lane_first(3.0 * f_zs2)
    c2 = lane_first(3.0 * (s_zf0 + f_zs1)) + 2.0 * lane_smooth(s_zs[2]) - 12.0 * s_zs[2]
    return lap, [c0, c1, c2]


def coefficients(own, over, under, carried):
    z = lax.broadcasted_iota(jnp.int32, (PAD, WIDE), 0) - 4
    zf = z.astype(F32)

    def pick(k):
        return jnp.where(z < 0, under[k], jnp.where(z > 15, over[k], own[k]))

    a, b, g = pick(0), pick(1), pick(2)
    mass, mass_over, mass_under = own[3], over[3], under[3]
    upper = jnp.where(z > 15, carried - mass_over, carried + mass * (15.0 - zf))
    lower = jnp.where(z < 0, carried + 16.0 * mass + mass_under, carried + mass * (16.0 - zf))
    return a, b, g * upper, g * lower


def prep_kernel(place, occ_h, mat_h, shear_h, lame_h, dens_h, now, prev, se, so, masses, consts, occ, mat, shear_t, lame_t, dens_t, held_now, held_prev, sems, *, factor):
    top_first = place[0] % 2 == 0
    smalls = []
    for k, (source, target) in enumerate(((occ_h, occ), (mat_h, mat), (shear_h, shear_t), (lame_h, lame_t), (dens_h, dens_t))):
        smalls.append(pltpu.make_async_copy(source, target, sems.at[4 + k]))
    copies = []
    for k in range(2):
        top = jnp.logical_xor(top_first, k == 1)
        copies.append(pltpu.make_async_copy(now.at[:, pl.ds(jnp.where(top, 14, 0), 2)], held_now.at[k], sems.at[2 * k]))
        copies.append(pltpu.make_async_copy(prev.at[:, pl.ds(jnp.where(top, 15, 0), 1)], held_prev.at[k], sems.at[2 * k + 1]))
    for copy in smalls + copies:
        copy.start()
    for copy in smalls:
        copy.wait()
    block = lax.broadcasted_iota(jnp.int32, (1, WIDE), 1) // BLOCK
    zero = jnp.zeros((1, WIDE), F32)
    occupied, shear, lame, dens = zero, zero, zero, zero
    for j in range(BLOCK):
        at = block == j
        which = mat[j]
        occupied = jnp.where(at, occ[j].astype(F32), occupied)
        shear = jnp.where(at, shear_t[which], shear)
        lame = jnp.where(at, lame_t[which], lame)
        dens = jnp.where(at, dens_t[which], dens)
    scale = occupied * (0.1 / dens)
    own = [scale * shear * (1.0 / 12.0), scale * (lame + shear) * (1.0 / 72.0), scale * factor, dens * occupied, occupied]
    for k, row in enumerate(own):
        consts[k : k + 1, :] = row
    consts[5:8, :] = jnp.zeros((3, WIDE), F32)
    masses[...] = jnp.broadcast_to(own[3], masses.shape)
    for copy in copies:
        copy.wait()
    for k, out in enumerate((se, so)):
        top = jnp.logical_xor(top_first, k == 1)
        for c in range(3):
            first, second = held_now[k, c, 0] * occupied, held_now[k, c, 1] * occupied
            out[c] = jnp.where(top, second, first)
            out[3 + c] = jnp.where(top, first, second)
            out[6 + c] = held_prev[k, c, 0] * occupied
        out[9, 0:8] = consts[...]


def ghost_of(place, se, so):
    even_story = place[0] % 2 == 0

    def ghost(over, *where):
        take = even_story if over else jnp.logical_not(even_story)
        return jnp.where(take, se[where], so[where])

    return ghost


def fill(ghost, consts, coef, now, prev, out, far_rows, prev_rows, near, far, sign):
    occupied = consts[4:5, :]
    for c in range(3):
        for target, base, source, x in ((out, c * PAD, now, near), (far_rows, c * PAD, now, far), (prev_rows, c * PAD, prev, near)):
            target[base + 4 : base + 20, :] = source[c, :, x, :] * occupied
            kinds = (6,) if source is prev else (0, 3)
            for k, kind in enumerate(kinds):
                target[base + 3 - k : base + 4 - k, :] = ghost(False, kind + c, pl.ds(x, 1), slice(None))
                target[base + 20 + k : base + 21 + k, :] = ghost(True, kind + c, pl.ds(x, 1), slice(None))
    order = (1, 0, 2)

    def planes(ref):
        return [ref[c * PAD : (c + 1) * PAD, :] for c in order]

    here = planes(out)
    first = advance(planes(far_rows), here, None, planes(prev_rows), [coef[k] for k in range(4)], sign)
    for k, c in enumerate(order):
        out[3 * PAD + 16 * c : 3 * PAD + 16 * c + 16, :] = first[k][4:20]
        out[c * PAD : c * PAD + 1, :] = first[k][3:4]
        out[c * PAD + 23 : c * PAD + 24, :] = first[k][20:21]
    for k in range(2):
        row = 1 if k == 0 else 22
        out[row : row + 1, :] = consts[k : k + 1, :]
        out[PAD + row : PAD + row + 1, :] = ghost(True, 9, pl.ds(k, 1), slice(None))
        out[2 * PAD + row : 2 * PAD + row + 1, :] = ghost(False, 9, pl.ds(k, 1), slice(None))


def pack_po_kernel(place, consts, se, so, masses, now, prev, po, coef, far_rows, prev_rows):
    ghost = ghost_of(place, se, so)
    step = lax.broadcasted_iota(jnp.int32, masses.shape, 0)
    carried = 16.0 * jnp.sum(jnp.where(step > place[0], masses[...], 0.0), 0, keepdims=True)
    own = [consts[k : k + 1, :] for k in range(4)]
    over = [ghost(True, 9, pl.ds(k, 1), slice(None)) for k in range(4)]
    under = [ghost(False, 9, pl.ds(k, 1), slice(None)) for k in range(4)]
    for k, rows in enumerate(coefficients(own, over, under, carried)):
        coef[k] = rows
    even_plan = place[1] % 2 == 0

    @pl.when(even_plan)
    def _():
        fill(ghost, consts, coef, now, prev, po, far_rows, prev_rows, 0, 1, -1.0)

    @pl.when(jnp.logical_not(even_plan))
    def _():
        fill(ghost, consts, coef, now, prev, po, far_rows, prev_rows, 15, 14, None)


def pack_pe_kernel(place, consts, coef, se, so, now, prev, pe, far_rows, prev_rows):
    ghost = ghost_of(place, se, so)
    even_plan = place[1] % 2 == 0

    @pl.when(even_plan)
    def _():
        fill(ghost, consts, coef, now, prev, pe, far_rows, prev_rows, 15, 14, None)

    @pl.when(jnp.logical_not(even_plan))
    def _():
        fill(ghost, consts, coef, now, prev, pe, far_rows, prev_rows, 0, 1, -1.0)


def advance(below, here, above, before, coefs, sign):
    a, b, gu, gd = coefs
    lap, coup = stencil(below, here, above, sign)
    news = []
    for c in range(3):
        lower, upper = row_shift(here[c])
        news.append(update(here[c], before[c], lap[c], coup[c], a, b, gu, gd, lower, upper))
    return news


def update(here, before, lap, coup, a, b, gu, gd, below, above):
    geometric = gu * (above - here) - gd * (here - below)
    return 2.0 * here - before + a * lap + b * coup - geometric


def main_kernel(place, consts, coef, se, so, now, prev, out, u0, u1, before):
    ghost = ghost_of(place, se, so)
    occupied = jnp.broadcast_to(consts[4:5, :], (16, WIDE))
    for c in range(3):
        u0[c, 0] = ghost(False, 3 + c)
        u0[c, 1] = ghost(False, c)
        u0[c, 18] = ghost(True, c)
        u0[c, 19] = ghost(True, 3 + c)
        before[c, 0] = ghost(False, 6 + c)
        before[c, 17] = ghost(True, 6 + c)

    @pl.loop(0, 16)
    def _(z):
        for c in range(3):
            u0[c, z + 2] = now[c, z] * occupied
            before[c, z + 1] = prev[c, z] * occupied

    def one(source, earlier, target, i, shift):
        below, here, above = ([source[c, i + k] for c in range(3)] for k in range(3))
        lap, coup = stencil(below, here, above)
        a, b, gu, gd = (coef[k, pl.ds(i + shift, 1), :] for k in range(4))
        for c in range(3):
            target[c, i] = update(here[c], earlier(c, i), lap[c], coup[c], a, b, gu, gd, below[c], above[c])

    @pl.loop(0, 18)
    def _(i):
        one(u0, lambda c, i: before[c, i], u1, i, 3)

    @pl.loop(0, 16)
    def _(i):
        one(u1, lambda c, i: u0[c, i + 2], out, i, 4)


def tail_kernel(place, coef, pe_sent, po_sent, pe_got, po_got, inner, out, held):
    even_plan = place[1] % 2 == 0
    out[...] = inner[...]
    order = (1, 0, 2)

    def planes(ref):
        return [ref[c * PAD : (c + 1) * PAD, :] for c in order]

    def one_side(sent, got, near, far, sign):
        for c in range(3):
            base = c * PAD
            held[base : base + 4, :] = got[base : base + 1, :] + jnp.zeros((4, WIDE), F32)
            held[base + 4 : base + 20, :] = got[3 * PAD + 16 * c : 3 * PAD + 16 * c + 16, :]
            held[base + 20 : base + PAD, :] = got[base + 23 : base + 24, :] + jnp.zeros((4, WIDE), F32)
        a, b, gu, gd = (coef[k] for k in range(4))
        z = lax.broadcasted_iota(jnp.int32, (PAD, WIDE), 0) - 4

        def pick(row):
            own, over, under = (got[k * PAD + row : k * PAD + row + 1, :] for k in range(3))
            return jnp.where(z < 0, under, jnp.where(z > 15, over, own))

        got_a, got_b = pick(1), pick(22)
        lap, coup = stencil(None, None, planes(got), sign)
        delta = [a * lap[k] + b * coup[k] for k in range(3)]
        lap, coup = stencil(planes(sent), None, None, sign)
        outer = [p + got_a * lap[k] + got_b * coup[k] for k, p in enumerate(planes(held))]
        zero = jnp.zeros((PAD, WIDE), F32)
        near_more = advance(None, delta, outer, [zero] * 3, (a, b, gu, gd), sign)
        lap, coup = stencil(None, None, delta, sign)
        for k, c in enumerate(order):
            out[c, :, near, :] += near_more[k][4:20]
            out[c, :, far, :] += (a * lap[k] + b * coup[k])[4:20]

    @pl.when(even_plan)
    def _():
        one_side(pe_sent, pe_got, 15, 14, None)
        one_side(po_sent, po_got, 0, 1, -1.0)

    @pl.when(jnp.logical_not(even_plan))
    def _():
        one_side(pe_sent, pe_got, 0, 1, -1.0)
        one_side(po_sent, po_got, 15, 14, None)


VM = pl.BlockSpec(memory_space=pltpu.VMEM)
SM = pl.BlockSpec(memory_space=pltpu.SMEM)
HB = pl.BlockSpec(memory_space=pltpu.HBM)


def shape(*dims):
    return jax.ShapeDtypeStruct(dims, F32)


def call(kernel, outs, ins, scratch=(), flops=0, moved=0):
    return pl.pallas_call(
        kernel,
        out_shape=outs,
        in_specs=ins,
        out_specs=[VM] * len(outs),
        scratch_shapes=list(scratch),
        compiler_params=pltpu.CompilerParams(vmem_limit_bytes=24 * 2**20),
        cost_estimate=pl.CostEstimate(flops=flops, bytes_accessed=moved, transcendentals=0),
    )


def local(u_now, u_prev, occupancy, materials, shear_table, lame_table, density_table):
    height = u_now.shape[1] * lax.axis_size("story")
    stories = lax.axis_size("story")
    mats = shear_table.shape[0]
    place = jnp.stack([lax.axis_index("story"), lax.axis_index("plan")]).astype(jnp.int32)
    face, slab, table = shape(10, 16, WIDE), shape(3 * PAD + 48, WIDE), shape(4, PAD, WIDE)
    planes = [pltpu.VMEM((3 * PAD, WIDE), F32)] * 2
    se, so, masses, consts = call(
        functools.partial(prep_kernel, factor=0.8 / height),
        [face, face, shape(stories, WIDE), shape(8, WIDE)],
        [SM] + [HB] * 7,
        [
            pltpu.SMEM((BLOCK,), jnp.int32),
            pltpu.SMEM((BLOCK,), jnp.int32),
            pltpu.SMEM((mats,), F32),
            pltpu.SMEM((mats,), F32),
            pltpu.SMEM((mats,), F32),
            pltpu.VMEM((2, 3, 2, 16, WIDE), F32),
            pltpu.VMEM((2, 3, 1, 16, WIDE), F32),
            pltpu.SemaphoreType.DMA((9,)),
        ],
        moved=1 << 20,
    )(place, occupancy.reshape(-1), materials.reshape(-1), shear_table, lame_table, density_table, u_now, u_prev)
    so_got = swap(so, "story", 1)
    se_got = swap(se, "story", 0)
    masses = lax.all_to_all(masses, "story", 0, 0, tiled=True)
    cells = u_now.shape
    po, coef = call(pack_po_kernel, [slab, table], [SM] + [VM] * 6, planes, moved=1 << 20)(
        place, consts, se_got, so_got, masses, u_now, u_prev
    )
    po_got = swap(po, "plan", 1)
    (pe,) = call(pack_pe_kernel, [slab], [SM] + [VM] * 6, planes, moved=1 << 20)(
        place, consts, coef, se_got, so_got, u_now, u_prev
    )
    pe_got = swap(pe, "plan", 0)
    (inner,) = call(
        main_kernel,
        [shape(*cells)],
        [SM] + [VM] * 6,
        [
            pltpu.VMEM((3, 20, 16, WIDE), F32),
            pltpu.VMEM((3, 18, 16, WIDE), F32),
            pltpu.VMEM((3, 18, 16, WIDE), F32),
        ],
        flops=60_000_000,
        moved=4 << 20,
    )(place, consts, coef, se_got, so_got, u_now, u_prev)
    (out,) = call(
        tail_kernel, [shape(*cells)], [SM] + [VM] * 6, [pltpu.VMEM((3 * PAD, WIDE), F32)], flops=10_000_000, moved=3 << 20
    )(place, coef, pe, po, pe_got, po_got, inner)
    return out


def solution(mesh):
    in_specs = (
        P(None, "story", "plan", None),
        P(None, "story", "plan", None),
        P("story", "plan", None),
        P("story", "plan", None),
        P(),
        P(),
        P(),
    )
    out_specs = P(None, "story", "plan", None)
    return jax.shard_map(local, mesh=mesh, in_specs=in_specs, out_specs=out_specs, check_vma=False)
```

time: 47 us -> 44 us (0.936)
  the two profiles are of different devices: /device:TPU:57 before, /device:TPU:24 now
where the time goes in v2:
time: 44 us; the launch traced here: 43.8 us
  blocking collectives  18.3 us (42%)
  Pallas kernels  12.2 us (28%)
  starting transfers between devices  10.1 us (23%)
  local copies, waits for them, and re-layouts  3.02 us (7%)
    all_to_all x1, blocking collectives, local(): masses = lax.all_to_all(masses, 'story', 0, 0, tiled=True)  18.3 us
    ppermute x4, starting transfers between devices, swap(): return lax.ppermute(values, axis, pairs)  10.1 us
    pallas_call x1, Pallas kernels, local(): call(main_kernel, [shape(*cells)], [SM] + [VM] * 6, [pltpu.VMEM((3, 20, 1...  6.47 us
    unnamed x19, local copies, waits for them, and re-layouts  2.98 us
    pallas_call x1, Pallas kernels, local(): call(tail_kernel, [shape(*cells)], [SM] + [VM] * 6, [pltpu.VMEM((3 * PAD,...  2.74 us
    pallas_call x1, Pallas kernels, local(): call(functools.partial(prep_kernel, factor=0.8 / height), [face, face, sh...  1.27 us
  transfers between devices with their start and end apart: 4, of which 0 were waited for; matrix products, arithmetic and copies ran while one was open for 0% of the time, Pallas kernels for 15%

profile of v2, /device:TPU:24, one launch (start us, length us, event | category | flops | bytes accessed | tf_op | source)
XLA Modules:
  0.0 43.8 jit_solution(12814102809435622137)
XLA Ops:
  0.0 0.1 pad_add_fusion.place
  0.1 0.0 copy-start.7
  0.1 0.0 copy-start.8
  0.1 0.0 copy-start.4
  0.1 0.0 copy-start.5
  0.1 0.0 copy-start.6
  0.1 0.6 %copy-done.7 = f32[8]{0:T(128)S(1)} copy-done((f32[8]{0:T(128)S(1)}, f32[8]{0:T(128)}, u32[]{:S(2)}) %copy-start.7) | copy-done | bytes 56
  0.7 0.0 copy-done.8
  0.7 0.0 copy-done.4
  0.8 0.0 copy-done.5
  0.8 0.0 copy-done.6
  0.8 0.0 copy-start
  0.8 1.1 %copy-done = f32[3,16,16,256]{3,2,1,0:T(8,128)S(1)} copy-done((f32[3,16,16,256]{3,2,1,0:T(8,128)S(1)}, f32[3,16,16,256]{3,2,1,0:T(8,128)}, u32[]{:S(2)}) %copy-start) | copy-done | bytes 786456
  1.9 0.0 copy-start.2
  1.9 1.1 %copy-done.2 = f32[3,16,16,256]{3,2,1,0:T(8,128)S(1)} copy-done((f32[3,16,16,256]{3,2,1,0:T(8,128)S(1)}, f32[3,16,16,256]{3,2,1,0:T(8,128)}, u32[]{:S(2)}) %copy-start.2) | copy-done | bytes 786456
  3.1 0.0 copy-start.1
  3.1 0.0 copy-start.3
  3.1 1.3 %shard_map.73 = (f32[10,16,256]{2,1,0:T(8,128)S(1)}, f32[10,16,256]{2,1,0:T(8,128)S(1)}, f32[32,256]{1,0:T(8,128)S(1)}, f32[8,256]{1,0:T(8,128)S(1)}) custom-call(s32[2]{0:T(128)S(1)} %pad_add_fusion.place, s32[16]{0:T(128)S(1)} %bitcast.10, s32[16]{0:T(128)S(1)} %bitcast.11, f32[8]{0:T(128)S(1)} %copy-done.6, f32[8]{0:T(128)S(1)} %copy-done.7, ...), custom_call_target="tpu_custom_call" | custom-call | bytes 1048576 | tf_op jit(solution)/shard_map/pallas_call | solution.py:341
  4.3 0.1 collective-permute-start
  4.4 0.7 %collective-permute-start.1 = (f32[10,16,256]{2,1,0:T(8,128)S(1)}, f32[10,16,256]{2,1,0:T(8,128)S(1)}, u32[]{:S(2)}, u32[]{:S(2)}) collective-permute-start(f32[10,16,256]{2,1,0:T(8,128)S(1)} %get-tuple-element.13), channel_id=1, source_target_pairs={{8,16},{16,8},{24,32},{32,24},{40,48},{48,40},{56,64},{64,56},{72,... | collective-permute-start | bytes 491528 | tf_op jit(solution)/shard_map/ppermute | solution.py:20
  5.2 18.3 %all_to_all.11 = f32[32,1,256]{2,1,0:T(1,128)S(1)} all-to-all(f32[32,1,256]{2,1,0:T(1,128)S(1)} %copy.8), channel_id=1, replica_groups=mesh['story'=32,'plan'=8] {'story'}, dimensions={0} | all-to-all | bytes 65536 | tf_op jit(solution)/shard_map/all_to_all | solution.py:359
  23.4 0.0 collective-permute-done.se
  23.4 0.0 collective-permute-done.1.so
  23.4 0.0 copy-done.1
  23.5 0.0 copy-done.3
  23.5 0.9 %shard_map.74 = (f32[120,256]{1,0:T(8,128)S(1)}, f32[4,24,256]{2,1,0:T(8,128)S(1)}) custom-call(s32[2]{0:T(128)S(1)} %pad_add_fusion.place, f32[8,256]{1,0:T(8,128)S(1)} %get-tuple-element.11.consts, f32[10,16,256]{2,1,0:T(8,128)S(1)} %collective-permute-done.se, f32[10,16,256]{2,1,0:T(8,128)S(1)} %collective-permute-done.1.so, f32[32,256]{1,0:T(8,128)S(1)} %bitcast.8, ...), custom_call_target="tpu_custom_call" | custom-call | bytes 1048576 | tf_op jit(solution)/shard_map/pallas_call | solution.py:361
  24.3 0.9 %shard_map.75.pe_sent = f32[120,256]{1,0:T(8,128)S(1)} custom-call(s32[2]{0:T(128)S(1)} %pad_add_fusion.place, f32[8,256]{1,0:T(8,128)S(1)} %get-tuple-element.11.consts, f32[4,24,256]{2,1,0:T(8,128)S(1)} %get-tuple-element.15.coef, f32[10,16,256]{2,1,0:T(8,128)S(1)} %collective-permute-done.se, f32[10,16,256]{2,1,0:T(8,128)S(1)} %collective-permute-done.1.so, ...), custom_call_target="tpu_custom_call" | custom-call | bytes 1048576 | tf_op jit(solution)/shard_map/pallas_call | solution.py:365
  25.2 0.8 %collective-permute-start.2 = (f32[120,256]{1,0:T(8,128)S(1)}, f32[120,256]{1,0:T(8,128)S(1)}, u32[]{:S(2)}, u32[]{:S(2)}) collective-permute-start(f32[120,256]{1,0:T(8,128)S(1)} %shard_map.75.pe_sent), channel_id=1, source_target_pairs={{0,1},{1,0},{2,3},{3,2},{4,5},{5,4},{6,7},{7,6},{8,9},{9,8},{10,11... | collective-permute-start | bytes 368648 | tf_op jit(solution)/shard_map/ppermute | solution.py:20
  26.0 8.5 %collective-permute-start.3 = (f32[120,256]{1,0:T(8,128)S(1)}, f32[120,256]{1,0:T(8,128)S(1)}, u32[]{:S(2)}, u32[]{:S(2)}) collective-permute-start(f32[120,256]{1,0:T(8,128)S(1)} %get-tuple-element.16.po_sent), channel_id=1, source_target_pairs={{1,2},{2,1},{3,4},{4,3},{5,6},{6,5},{9,10},{10,9},{11,12},{12,11},... | collective-permute-start | bytes 368648 | tf_op jit(solution)/shard_map/ppermute | solution.py:20
  34.5 6.5 %shard_map.76.inner = f32[3,16,16,256]{3,2,1,0:T(8,128)S(1)} custom-call(s32[2]{0:T(128)S(1)} %pad_add_fusion.place, f32[8,256]{1,0:T(8,128)S(1)} %get-tuple-element.11.consts, f32[4,24,256]{2,1,0:T(8,128)S(1)} %get-tuple-element.15.coef, f32[10,16,256]{2,1,0:T(8,128)S(1)} %collective-permute-done.se, f32[10,16,256]{2,1,0:T(8,128)S(1)} %collective-permute-done.1.so, ...), custom_call_target="tpu_custom_call" | custom-call | flops 60000000 | bytes 4194304 | tf_op jit(solution)/shard_map/pallas_call | solution.py:369
  41.0 0.0 collective-permute-done.2.pe_got
  41.0 0.0 collective-permute-done.3.po_got
  41.0 2.7 %shard_map.77 = f32[3,16,16,256]{3,2,1,0:T(8,128)} custom-call(s32[2]{0:T(128)S(1)} %pad_add_fusion.place, f32[4,24,256]{2,1,0:T(8,128)S(1)} %get-tuple-element.15.coef, f32[120,256]{1,0:T(8,128)S(1)} %shard_map.75.pe_sent, f32[120,256]{1,0:T(8,128)S(1)} %get-tuple-element.16.po_sent, f32[120,256]{1,0:T(8,128)S(1)} %collective-permute-done.2.pe_got, ...), custom_call_target="tpu_custom_call" | custom-call | flops 10000000 | bytes 3145728 | tf_op jit(solution)/shard_map/pallas_call | solution.py:381
  (2 shorter events, 0.0 us)
Async XLA Ops:
  0.1 0.7 %copy-start.7 = (f32[8]{0:T(128)S(1)}, f32[8]{0:T(128)}, u32[]{:S(2)}) copy-start(f32[8]{0:T(128)} %lame_h.1) | copy-start | bytes 100
  0.1 0.7 %copy-start.8 = (f32[8]{0:T(128)S(1)}, f32[8]{0:T(128)}, u32[]{:S(2)}) copy-start(f32[8]{0:T(128)} %dens_h.1) | copy-start | bytes 100
  0.1 0.7 %copy-start.4 = (s32[1,1,16]{2,1,0:T(1,128)S(1)}, s32[1,1,16]{2,1,0:T(1,128)}, u32[]{:S(2)}) copy-start(s32[1,1,16]{2,1,0:T(1,128)} %param.9) | copy-start | bytes 196
  0.1 0.7 %copy-start.5 = (s32[1,1,16]{2,1,0:T(1,128)S(1)}, s32[1,1,16]{2,1,0:T(1,128)}, u32[]{:S(2)}) copy-start(s32[1,1,16]{2,1,0:T(1,128)} %param.10) | copy-start | bytes 196
  0.1 0.7 %copy-start.6 = (f32[8]{0:T(128)S(1)}, f32[8]{0:T(128)}, u32[]{:S(2)}) copy-start(f32[8]{0:T(128)} %shear_h.1) | copy-start | bytes 100
  0.8 1.1 %copy-start = (f32[3,16,16,256]{3,2,1,0:T(8,128)S(1)}, f32[3,16,16,256]{3,2,1,0:T(8,128)}, u32[]{:S(2)}) copy-start(f32[3,16,16,256]{3,2,1,0:T(8,128)} %now.7) | copy-start | bytes 2359300
  1.9 1.1 %copy-start.2 = (f32[3,16,16,256]{3,2,1,0:T(8,128)S(1)}, f32[3,16,16,256]{3,2,1,0:T(8,128)}, u32[]{:S(2)}) copy-start(f32[3,16,16,256]{3,2,1,0:T(8,128)} %prev.7) | copy-start | bytes 2359300
  3.1 20.4 %copy-start.1 = (f32[3,16,16,256]{3,2,1,0:T(8,128)S(1)}, f32[3,16,16,256]{3,2,1,0:T(8,128)}, u32[]{:S(2)}) copy-start(f32[3,16,16,256]{3,2,1,0:T(8,128)} %now.7) | copy-start | bytes 2359300
  3.1 20.4 %copy-start.3 = (f32[3,16,16,256]{3,2,1,0:T(8,128)S(1)}, f32[3,16,16,256]{3,2,1,0:T(8,128)}, u32[]{:S(2)}) copy-start(f32[3,16,16,256]{3,2,1,0:T(8,128)} %prev.7) | copy-start | bytes 2359300
  4.3 19.1 %collective-permute-start = (f32[10,16,256]{2,1,0:T(8,128)S(1)}, f32[10,16,256]{2,1,0:T(8,128)S(1)}, u32[]{:S(2)}, u32[]{:S(2)}) collective-permute-start(f32[10,16,256]{2,1,0:T(8,128)S(1)} %get-tuple-element.12), channel_id=1, source_target_pairs={{0,8},{8,0},{16,24},{24,16},{32,40},{40,32},{48,56},{56,48},{64,72... | collective-permute-start | bytes 491528 | tf_op jit(solution)/shard_map/ppermute | solution.py:20
  4.4 19.0 %collective-permute-start.1 = (f32[10,16,256]{2,1,0:T(8,128)S(1)}, f32[10,16,256]{2,1,0:T(8,128)S(1)}, u32[]{:S(2)}, u32[]{:S(2)}) collective-permute-start(f32[10,16,256]{2,1,0:T(8,128)S(1)} %get-tuple-element.13), channel_id=1, source_target_pairs={{8,16},{16,8},{24,32},{32,24},{40,48},{48,40},{56,64},{64,56},{72,... | collective-permute-start | bytes 491528 | tf_op jit(solution)/shard_map/ppermute | solution.py:20
  25.2 15.8 %collective-permute-start.2 = (f32[120,256]{1,0:T(8,128)S(1)}, f32[120,256]{1,0:T(8,128)S(1)}, u32[]{:S(2)}, u32[]{:S(2)}) collective-permute-start(f32[120,256]{1,0:T(8,128)S(1)} %shard_map.75.pe_sent), channel_id=1, source_target_pairs={{0,1},{1,0},{2,3},{3,2},{4,5},{5,4},{6,7},{7,6},{8,9},{9,8},{10,11... | collective-permute-start | bytes 368648 | tf_op jit(solution)/shard_map/ppermute | solution.py:20
  26.0 15.0 %collective-permute-start.3 = (f32[120,256]{1,0:T(8,128)S(1)}, f32[120,256]{1,0:T(8,128)S(1)}, u32[]{:S(2)}, u32[]{:S(2)}) collective-permute-start(f32[120,256]{1,0:T(8,128)S(1)} %get-tuple-element.16.po_sent), channel_id=1, source_target_pairs={{1,2},{2,1},{3,4},{4,3},{5,6},{6,5},{9,10},{10,9},{11,12},{12,11},... | collective-permute-start | bytes 368648 | tf_op jit(solution)/shard_map/ppermute | solution.py:20

commit v3 on v2

--- a/solution.py
+++ b/solution.py
@@ -319,14 +319,14 @@
     return jax.ShapeDtypeStruct(dims, F32)
 
 
-def call(kernel, outs, ins, scratch=(), flops=0, moved=0):
+def call(kernel, outs, ins, scratch=(), flops=0, moved=0, grant=24):
     return pl.pallas_call(
         kernel,
         out_shape=outs,
         in_specs=ins,
         out_specs=[VM] * len(outs),
         scratch_shapes=list(scratch),
-        compiler_params=pltpu.CompilerParams(vmem_limit_bytes=24 * 2**20),
+        compiler_params=pltpu.CompilerParams(vmem_limit_bytes=grant * 2**20),
         cost_estimate=pl.CostEstimate(flops=flops, bytes_accessed=moved, transcendentals=0),
     )
 
@@ -353,12 +353,13 @@
             pltpu.SemaphoreType.DMA((9,)),
         ],
         moved=1 << 20,
+        grant=60,
     )(place, occupancy.reshape(-1), materials.reshape(-1), shear_table, lame_table, density_table, u_now, u_prev)
     so_got = swap(so, "story", 1)
     se_got = swap(se, "story", 0)
     masses = lax.all_to_all(masses, "story", 0, 0, tiled=True)
     cells = u_now.shape
-    po, coef = call(pack_po_kernel, [slab, table], [SM] + [VM] * 6, planes, moved=1 << 20)(
+    po, coef = call(pack_po_kernel, [shape(3 * PAD + 56, WIDE), table], [SM] + [VM] * 6, planes, moved=1 << 20)(
         place, consts, se_got, so_got, masses, u_now, u_prev
     )
     po_got = swap(po, "plan", 1)

time: 44 us -> 44.1 us (level)
  the two profiles are of different devices: /device:TPU:24 before, /device:TPU:16 now
where the time goes in v3:
time: 44.1 us; the launch traced here: 43.8 us
  blocking collectives  18.3 us (41%)
  Pallas kernels  13.5 us (31%)
  starting transfers between devices  9.78 us (22%)
  local copies, waits for them, and re-layouts  1.45 us (3%)
  other arithmetic  0.62 us (1%)
    all_to_all x1, blocking collectives, local(): masses = lax.all_to_all(masses, 'story', 0, 0, tiled=True)  18.3 us
    ppermute x4, starting transfers between devices, swap(): return lax.ppermute(values, axis, pairs)  9.78 us
    pallas_call x1, Pallas kernels, local(): call(main_kernel, [shape(*cells)], [SM] + [VM] * 6, [pltpu.VMEM((3, 20, 1...  6.47 us
    pallas_call x1, Pallas kernels, local(): call(tail_kernel, [shape(*cells)], [SM] + [VM] * 6, [pltpu.VMEM((3 * PAD,...  2.75 us
    pallas_call x1, Pallas kernels, local(): call(functools.partial(prep_kernel, factor=0.8 / height), [face, face, sh...  2.6 us
  transfers between devices with their start and end apart: 4, of which 0 were waited for; matrix products, arithmetic and copies ran while one was open for 2% of the time, Pallas kernels for 17%

profile of v3, /device:TPU:16, one launch (start us, length us, event | category | flops | bytes accessed | tf_op | source)
XLA Modules:
  0.0 43.8 jit_solution(18156042073317937518)
XLA Ops:
  0.0 0.6 %pad_add_fusion.place = s32[2]{0:T(128)} fusion(s32[1]{0:T(128)} %bitcast.1, s32[1]{0:T(128)} %bitcast), kind=kLoop, calls=%fused_computation.1 | loop fusion | flops 2 | bytes 16 | tf_op jit(solution)/shard_map/stack | solution.py:338
  0.6 0.0 copy-start
  0.6 0.0 copy-start.1
  0.6 2.6 %shard_map.73 = (f32[10,16,256]{2,1,0:T(8,128)}, f32[10,16,256]{2,1,0:T(8,128)}, f32[32,256]{1,0:T(8,128)}, f32[8,256]{1,0:T(8,128)}) custom-call(s32[2]{0:T(128)} %pad_add_fusion.place, s32[16]{0:T(128)} %bitcast.10, s32[16]{0:T(128)} %bitcast.11, f32[8]{0:T(128)} %shear_h.1, f32[8]{0:T(128)} %lame_h.1, f32[8]{0:T(128)} %dens_h.1, f32[3,16,16,256]{3,2,1,0:T(8,128)} %now.7, ...), custom_call_target="tpu_custom_call" | custom-call | bytes 1048576 | tf_op jit(solution)/shard_map/pallas_call | solution.py:341
  3.2 0.1 collective-permute-start
  3.3 0.7 %collective-permute-start.1 = (f32[10,16,256]{2,1,0:T(8,128)}, f32[10,16,256]{2,1,0:T(8,128)S(1)}, u32[]{:S(2)}, u32[]{:S(2)}) collective-permute-start(f32[10,16,256]{2,1,0:T(8,128)} %get-tuple-element.13), channel_id=1, source_target_pairs={{8,16},{16,8},{24,32},{32,24},{40,48},{48,40},{56,64},{64,56},{72,... | collective-permute-start | bytes 491528 | tf_op jit(solution)/shard_map/ppermute | solution.py:20
  4.0 0.8 %copy.8 = f32[32,1,256]{2,1,0:T(1,128)S(1)} copy(f32[32,1,256]{2,0,1:T(8,128)} %bitcast.9) | data formatting | bytes 65536 | tf_op jit(solution)/shard_map/all_to_all | solution.py:360
  4.8 18.3 %all_to_all.11 = f32[32,1,256]{2,1,0:T(1,128)S(1)} all-to-all(f32[32,1,256]{2,1,0:T(1,128)S(1)} %copy.8), channel_id=1, replica_groups=mesh['story'=32,'plan'=8] {'story'}, dimensions={0} | all-to-all | bytes 65536 | tf_op jit(solution)/shard_map/all_to_all | solution.py:360
  23.1 0.0 copy-start.2
  23.1 0.0 collective-permute-done.se
  23.1 0.0 collective-permute-done.1.so
  23.1 0.0 copy-start.3
  23.1 0.0 copy-done
  23.1 0.0 copy-done.1
  23.1 0.6 %copy-done.2 = f32[8,256]{1,0:T(8,128)S(1)} copy-done((f32[8,256]{1,0:T(8,128)S(1)}, f32[8,256]{1,0:T(8,128)}, u32[]{:S(2)}) %copy-start.2) | copy-done | bytes 8216
  23.8 0.0 copy-done.3
  23.8 0.9 %shard_map.74 = (f32[128,256]{1,0:T(8,128)S(1)}, f32[4,24,256]{2,1,0:T(8,128)S(1)}) custom-call(s32[2]{0:T(128)S(1)} %copy-done.3, f32[8,256]{1,0:T(8,128)S(1)} %copy-done.2, f32[10,16,256]{2,1,0:T(8,128)S(1)} %collective-permute-done.se, f32[10,16,256]{2,1,0:T(8,128)S(1)} %collective-permute-done.1.so, f32[32,256]{1,0:T(8,128)S(1)} %bitcast.8, ...), custom_call_target="tpu_custom_call" | custom-call | bytes 1048576 | tf_op jit(solution)/shard_map/pallas_call | solution.py:362
  24.6 2.4 %collective-permute-start.3 = (f32[128,256]{1,0:T(8,128)S(1)}, f32[128,256]{1,0:T(8,128)S(1)}, u32[]{:S(2)}, u32[]{:S(2)}) collective-permute-start(f32[128,256]{1,0:T(8,128)S(1)} %get-tuple-element.16.po_sent), channel_id=1, source_target_pairs={{1,2},{2,1},{3,4},{4,3},{5,6},{6,5},{9,10},{10,9},{11,12},{12,11},... | collective-permute-start | bytes 393224 | tf_op jit(solution)/shard_map/ppermute | solution.py:20
  27.0 0.8 %shard_map.75.pe_sent = f32[120,256]{1,0:T(8,128)S(1)} custom-call(s32[2]{0:T(128)S(1)} %copy-done.3, f32[8,256]{1,0:T(8,128)S(1)} %copy-done.2, f32[4,24,256]{2,1,0:T(8,128)S(1)} %get-tuple-element.15.coef, f32[10,16,256]{2,1,0:T(8,128)S(1)} %collective-permute-done.se, f32[10,16,256]{2,1,0:T(8,128)S(1)} %collective-permute-done.1.so, ...), custom_call_target="tpu_custom_call" | custom-call | bytes 1048576 | tf_op jit(solution)/shard_map/pallas_call | solution.py:366
  27.9 6.7 %collective-permute-start.2 = (f32[120,256]{1,0:T(8,128)S(1)}, f32[120,256]{1,0:T(8,128)S(1)}, u32[]{:S(2)}, u32[]{:S(2)}) collective-permute-start(f32[120,256]{1,0:T(8,128)S(1)} %shard_map.75.pe_sent), channel_id=1, source_target_pairs={{0,1},{1,0},{2,3},{3,2},{4,5},{5,4},{6,7},{7,6},{8,9},{9,8},{10,11... | collective-permute-start | bytes 368648 | tf_op jit(solution)/shard_map/ppermute | solution.py:20
  34.5 6.5 %shard_map.76.inner = f32[3,16,16,256]{3,2,1,0:T(8,128)S(1)} custom-call(s32[2]{0:T(128)S(1)} %copy-done.3, f32[8,256]{1,0:T(8,128)S(1)} %copy-done.2, f32[4,24,256]{2,1,0:T(8,128)S(1)} %get-tuple-element.15.coef, f32[10,16,256]{2,1,0:T(8,128)S(1)} %collective-permute-done.se, f32[10,16,256]{2,1,0:T(8,128)S(1)} %collective-permute-done.1.so, ...), custom_call_target="tpu_custom_call" | custom-call | flops 60000000 | bytes 4194304 | tf_op jit(solution)/shard_map/pallas_call | solution.py:370
  41.0 0.0 collective-permute-done.2.pe_got
  41.0 0.0 collective-permute-done.3.po_got
  41.0 2.8 %shard_map.77 = f32[3,16,16,256]{3,2,1,0:T(8,128)} custom-call(s32[2]{0:T(128)S(1)} %copy-done.3, f32[4,24,256]{2,1,0:T(8,128)S(1)} %get-tuple-element.15.coef, f32[120,256]{1,0:T(8,128)S(1)} %shard_map.75.pe_sent, f32[128,256]{1,0:T(8,128)S(1)} %get-tuple-element.16.po_sent, f32[120,256]{1,0:T(8,128)S(1)} %collective-permute-done.2.pe_got, ...), custom_call_target="tpu_custom_call" | custom-call | flops 10000000 | bytes 3145728 | tf_op jit(solution)/shard_map/pallas_call | solution.py:382
  (1 shorter events, 0.0 us)
Async XLA Ops:
  0.6 22.5 %copy-start = (f32[3,16,16,256]{3,2,1,0:T(8,128)S(1)}, f32[3,16,16,256]{3,2,1,0:T(8,128)}, u32[]{:S(2)}) copy-start(f32[3,16,16,256]{3,2,1,0:T(8,128)} %now.7) | copy-start | bytes 2359300
  0.6 22.5 %copy-start.1 = (f32[3,16,16,256]{3,2,1,0:T(8,128)S(1)}, f32[3,16,16,256]{3,2,1,0:T(8,128)}, u32[]{:S(2)}) copy-start(f32[3,16,16,256]{3,2,1,0:T(8,128)} %prev.7) | copy-start | bytes 2359300
  3.2 19.9 %collective-permute-start = (f32[10,16,256]{2,1,0:T(8,128)}, f32[10,16,256]{2,1,0:T(8,128)S(1)}, u32[]{:S(2)}, u32[]{:S(2)}) collective-permute-start(f32[10,16,256]{2,1,0:T(8,128)} %get-tuple-element.12), channel_id=1, source_target_pairs={{0,8},{8,0},{16,24},{24,16},{32,40},{40,32},{48,56},{56,48},{64,72... | collective-permute-start | bytes 491528 | tf_op jit(solution)/shard_map/ppermute | solution.py:20
  3.3 19.8 %collective-permute-start.1 = (f32[10,16,256]{2,1,0:T(8,128)}, f32[10,16,256]{2,1,0:T(8,128)S(1)}, u32[]{:S(2)}, u32[]{:S(2)}) collective-permute-start(f32[10,16,256]{2,1,0:T(8,128)} %get-tuple-element.13), channel_id=1, source_target_pairs={{8,16},{16,8},{24,32},{32,24},{40,48},{48,40},{56,64},{64,56},{72,... | collective-permute-start | bytes 491528 | tf_op jit(solution)/shard_map/ppermute | solution.py:20
  23.1 0.7 %copy-start.2 = (f32[8,256]{1,0:T(8,128)S(1)}, f32[8,256]{1,0:T(8,128)}, u32[]{:S(2)}) copy-start(f32[8,256]{1,0:T(8,128)} %get-tuple-element.11.consts) | copy-start | bytes 24580
  23.1 0.7 %copy-start.3 = (s32[2]{0:T(128)S(1)}, s32[2]{0:T(128)}, u32[]{:S(2)}) copy-start(s32[2]{0:T(128)} %pad_add_fusion.place) | copy-start | bytes 28
  24.6 16.4 %collective-permute-start.3 = (f32[128,256]{1,0:T(8,128)S(1)}, f32[128,256]{1,0:T(8,128)S(1)}, u32[]{:S(2)}, u32[]{:S(2)}) collective-permute-start(f32[128,256]{1,0:T(8,128)S(1)} %get-tuple-element.16.po_sent), channel_id=1, source_target_pairs={{1,2},{2,1},{3,4},{4,3},{5,6},{6,5},{9,10},{10,9},{11,12},{12,11},... | collective-permute-start | bytes 393224 | tf_op jit(solution)/shard_map/ppermute | solution.py:20
  27.9 13.2 %collective-permute-start.2 = (f32[120,256]{1,0:T(8,128)S(1)}, f32[120,256]{1,0:T(8,128)S(1)}, u32[]{:S(2)}, u32[]{:S(2)}) collective-permute-start(f32[120,256]{1,0:T(8,128)S(1)} %shard_map.75.pe_sent), channel_id=1, source_target_pairs={{0,1},{1,0},{2,3},{3,2},{4,5},{5,4},{6,7},{7,6},{8,9},{9,8},{10,11... | collective-permute-start | bytes 368648 | tf_op jit(solution)/shard_map/ppermute | solution.py:20

commit v4 on v2

--- a/solution.py
+++ b/solution.py
@@ -106,20 +106,15 @@
     return a, b, g * upper, g * lower
 
 
-def prep_kernel(place, occ_h, mat_h, shear_h, lame_h, dens_h, now, prev, se, so, masses, consts, occ, mat, shear_t, lame_t, dens_t, held_now, held_prev, sems, *, factor):
+def prep_kernel(place, occ, mat, shear_t, lame_t, dens_t, now, prev, se, so, masses, consts, held_now, held_prev, sems, *, factor):
     top_first = place[0] % 2 == 0
-    smalls = []
-    for k, (source, target) in enumerate(((occ_h, occ), (mat_h, mat), (shear_h, shear_t), (lame_h, lame_t), (dens_h, dens_t))):
-        smalls.append(pltpu.make_async_copy(source, target, sems.at[4 + k]))
     copies = []
     for k in range(2):
         top = jnp.logical_xor(top_first, k == 1)
         copies.append(pltpu.make_async_copy(now.at[:, pl.ds(jnp.where(top, 14, 0), 2)], held_now.at[k], sems.at[2 * k]))
         copies.append(pltpu.make_async_copy(prev.at[:, pl.ds(jnp.where(top, 15, 0), 1)], held_prev.at[k], sems.at[2 * k + 1]))
-    for copy in smalls + copies:
+    for copy in copies:
         copy.start()
-    for copy in smalls:
-        copy.wait()
     block = lax.broadcasted_iota(jnp.int32, (1, WIDE), 1) // BLOCK
     zero = jnp.zeros((1, WIDE), F32)
     occupied, shear, lame, dens = zero, zero, zero, zero
@@ -205,19 +200,6 @@
         fill(ghost, consts, coef, now, prev, po, far_rows, prev_rows, 15, 14, None)
 
 
-def pack_pe_kernel(place, consts, coef, se, so, now, prev, pe, far_rows, prev_rows):
-    ghost = ghost_of(place, se, so)
-    even_plan = place[1] % 2 == 0
-
-    @pl.when(even_plan)
-    def _():
-        fill(ghost, consts, coef, now, prev, pe, far_rows, prev_rows, 15, 14, None)
-
-    @pl.when(jnp.logical_not(even_plan))
-    def _():
-        fill(ghost, consts, coef, now, prev, pe, far_rows, prev_rows, 0, 1, -1.0)
-
-
 def advance(below, here, above, before, coefs, sign):
     a, b, gu, gd = coefs
     lap, coup = stencil(below, here, above, sign)
@@ -244,7 +226,7 @@
         before[c, 0] = ghost(False, 6 + c)
         before[c, 17] = ghost(True, 6 + c)
 
-    @pl.loop(0, 16)
+    @pl.loop(0, 16, unroll=4)
     def _(z):
         for c in range(3):
             u0[c, z + 2] = now[c, z] * occupied
@@ -257,57 +239,98 @@
         for c in range(3):
             target[c, i] = update(here[c], earlier(c, i), lap[c], coup[c], a, b, gu, gd, below[c], above[c])
 
-    @pl.loop(0, 18)
+    @pl.loop(0, 18, unroll=3)
     def _(i):
         one(u0, lambda c, i: before[c, i], u1, i, 3)
 
-    @pl.loop(0, 16)
+    @pl.loop(0, 16, unroll=4)
     def _(i):
         one(u1, lambda c, i: u0[c, i + 2], out, i, 4)
 
 
-def tail_kernel(place, coef, pe_sent, po_sent, pe_got, po_got, inner, out, held):
+def pack_pe_kernel(place, consts, coef, se, so, now, prev, pe, far_rows, prev_rows):
+    ghost = ghost_of(place, se, so)
     even_plan = place[1] % 2 == 0
-    out[...] = inner[...]
+
+    @pl.when(even_plan)
+    def _():
+        fill(ghost, consts, coef, now, prev, pe, far_rows, prev_rows, 15, 14, None)
+
+    @pl.when(jnp.logical_not(even_plan))
+    def _():
+        fill(ghost, consts, coef, now, prev, pe, far_rows, prev_rows, 0, 1, -1.0)
+
+
+def one_side(coef, sent, got, work, held, near, far, sign):
     order = (1, 0, 2)
 
     def planes(ref):
         return [ref[c * PAD : (c + 1) * PAD, :] for c in order]
 
-    def one_side(sent, got, near, far, sign):
-        for c in range(3):
-            base = c * PAD
-            held[base : base + 4, :] = got[base : base + 1, :] + jnp.zeros((4, WIDE), F32)
-            held[base + 4 : base + 20, :] = got[3 * PAD + 16 * c : 3 * PAD + 16 * c + 16, :]
-            held[base + 20 : base + PAD, :] = got[base + 23 : base + 24, :] + jnp.zeros((4, WIDE), F32)
-        a, b, gu, gd = (coef[k] for k in range(4))
-        z = lax.broadcasted_iota(jnp.int32, (PAD, WIDE), 0) - 4
-
-        def pick(row):
-            own, over, under = (got[k * PAD + row : k * PAD + row + 1, :] for k in range(3))
-            return jnp.where(z < 0, under, jnp.where(z > 15, over, own))
-
-        got_a, got_b = pick(1), pick(22)
-        lap, coup = stencil(None, None, planes(got), sign)
-        delta = [a * lap[k] + b * coup[k] for k in range(3)]
-        lap, coup = stencil(planes(sent), None, None, sign)
-        outer = [p + got_a * lap[k] + got_b * coup[k] for k, p in enumerate(planes(held))]
-        zero = jnp.zeros((PAD, WIDE), F32)
-        near_more = advance(None, delta, outer, [zero] * 3, (a, b, gu, gd), sign)
-        lap, coup = stencil(None, None, delta, sign)
-        for k, c in enumerate(order):
-            out[c, :, near, :] += near_more[k][4:20]
-            out[c, :, far, :] += (a * lap[k] + b * coup[k])[4:20]
+    for c in range(3):
+        base = c * PAD
+        held[base : base + 4, :] = got[base : base + 1, :] + jnp.zeros((4, WIDE), F32)
+        held[base + 4 : base + 20, :] = got[3 * PAD + 16 * c : 3 * PAD + 16 * c + 16, :]
+        held[base + 20 : base + PAD, :] = got[base + 23 : base + 24, :] + jnp.zeros((4, WIDE), F32)
+    a, b, gu, gd = (coef[k] for k in range(4))
+    z = lax.broadcasted_iota(jnp.int32, (PAD, WIDE), 0) - 4
+
+    def pick(row):
+        own, over, under = (got[k * PAD + row : k * PAD + row + 1, :] for k in range(3))
+        return jnp.where(z < 0, under, jnp.where(z > 15, over, own))
+
+    got_a, got_b = pick(1), pick(22)
+    lap, coup = stencil(None, None, planes(got), sign)
+    delta = [a * lap[k] + b * coup[k] for k in range(3)]
+    lap, coup = stencil(planes(sent), None, None, sign)
+    outer = [p + got_a * lap[k] + got_b * coup[k] for k, p in enumerate(planes(held))]
+    zero = jnp.zeros((PAD, WIDE), F32)
+    near_more = advance(None, delta, outer, [zero] * 3, (a, b, gu, gd), sign)
+    lap, coup = stencil(None, None, delta, sign)
+    for k, c in enumerate(order):
+        work[c, :, near, :] += near_more[k][4:20]
+        work[c, :, far, :] += (a * lap[k] + b * coup[k])[4:20]
+
+
+def write_half(work, out, first, sems):
+    copies = [pltpu.make_async_copy(work.at[c], out.at[c, :, pl.ds(first, 8), :], sems.at[c]) for c in range(3)]
+    for copy in copies:
+        copy.start()
+    for copy in copies:
+        copy.wait()
+
+
+def tail_pe_kernel(place, coef, sent, got, inner, out, rest, work, held, sems):
+    even_plan = place[1] % 2 == 0
 
     @pl.when(even_plan)
     def _():
-        one_side(pe_sent, pe_got, 15, 14, None)
-        one_side(po_sent, po_got, 0, 1, -1.0)
+        work[...] = inner[:, :, 8:16, :]
+        rest[...] = inner[:, :, 0:8, :]
+        one_side(coef, sent, got, work, held, 7, 6, None)
+        write_half(work, out, 8, sems)
 
     @pl.when(jnp.logical_not(even_plan))
     def _():
-        one_side(pe_sent, pe_got, 0, 1, -1.0)
-        one_side(po_sent, po_got, 15, 14, None)
+        work[...] = inner[:, :, 0:8, :]
+        rest[...] = inner[:, :, 8:16, :]
+        one_side(coef, sent, got, work, held, 0, 1, -1.0)
+        write_half(work, out, 0, sems)
+
+
+def tail_po_kernel(place, coef, sent, got, rest, half, out, work, held, sems):
+    even_plan = place[1] % 2 == 0
+    work[...] = rest[...]
+
+    @pl.when(even_plan)
+    def _():
+        one_side(coef, sent, got, work, held, 0, 1, -1.0)
+        write_half(work, out, 0, sems)
+
+    @pl.when(jnp.logical_not(even_plan))
+    def _():
+        one_side(coef, sent, got, work, held, 7, 6, None)
+        write_half(work, out, 8, sems)
 
 
 VM = pl.BlockSpec(memory_space=pltpu.VMEM)
@@ -319,14 +342,15 @@
     return jax.ShapeDtypeStruct(dims, F32)
 
 
-def call(kernel, outs, ins, scratch=(), flops=0, moved=0):
+def call(kernel, outs, ins, scratch=(), flops=0, moved=0, grant=24.0, places=None, aliases=None):
     return pl.pallas_call(
         kernel,
         out_shape=outs,
         in_specs=ins,
-        out_specs=[VM] * len(outs),
+        out_specs=places or [VM] * len(outs),
         scratch_shapes=list(scratch),
-        compiler_params=pltpu.CompilerParams(vmem_limit_bytes=24 * 2**20),
+        input_output_aliases=aliases or {},
+        compiler_params=pltpu.CompilerParams(vmem_limit_bytes=int(grant * 2**20)),
         cost_estimate=pl.CostEstimate(flops=flops, bytes_accessed=moved, transcendentals=0),
     )
 
@@ -334,53 +358,50 @@
 def local(u_now, u_prev, occupancy, materials, shear_table, lame_table, density_table):
     height = u_now.shape[1] * lax.axis_size("story")
     stories = lax.axis_size("story")
-    mats = shear_table.shape[0]
     place = jnp.stack([lax.axis_index("story"), lax.axis_index("plan")]).astype(jnp.int32)
-    face, slab, table = shape(10, 16, WIDE), shape(3 * PAD + 48, WIDE), shape(4, PAD, WIDE)
+    face, table = shape(10, 16, WIDE), shape(4, PAD, WIDE)
+    rows = 3 * PAD + 48
     planes = [pltpu.VMEM((3 * PAD, WIDE), F32)] * 2
     se, so, masses, consts = call(
         functools.partial(prep_kernel, factor=0.8 / height),
         [face, face, shape(stories, WIDE), shape(8, WIDE)],
-        [SM] + [HB] * 7,
+        [SM] * 6 + [HB] * 2,
         [
-            pltpu.SMEM((BLOCK,), jnp.int32),
-            pltpu.SMEM((BLOCK,), jnp.int32),
-            pltpu.SMEM((mats,), F32),
-            pltpu.SMEM((mats,), F32),
-            pltpu.SMEM((mats,), F32),
             pltpu.VMEM((2, 3, 2, 16, WIDE), F32),
             pltpu.VMEM((2, 3, 1, 16, WIDE), F32),
-            pltpu.SemaphoreType.DMA((9,)),
+            pltpu.SemaphoreType.DMA((4,)),
         ],
         moved=1 << 20,
+        grant=53.2,
     )(place, occupancy.reshape(-1), materials.reshape(-1), shear_table, lame_table, density_table, u_now, u_prev)
     so_got = swap(so, "story", 1)
     se_got = swap(se, "story", 0)
     masses = lax.all_to_all(masses, "story", 0, 0, tiled=True)
     cells = u_now.shape
-    po, coef = call(pack_po_kernel, [slab, table], [SM] + [VM] * 6, planes, moved=1 << 20)(
+    po, coef = call(pack_po_kernel, [shape(rows + 8, WIDE), table], [SM] + [VM] * 6, planes, moved=1 << 20)(
         place, consts, se_got, so_got, masses, u_now, u_prev
     )
     po_got = swap(po, "plan", 1)
-    (pe,) = call(pack_pe_kernel, [slab], [SM] + [VM] * 6, planes, moved=1 << 20)(
+    levels = [
+        pltpu.VMEM((3, 20, 16, WIDE), F32),
+        pltpu.VMEM((3, 18, 16, WIDE), F32),
+        pltpu.VMEM((3, 18, 16, WIDE), F32),
+    ]
+    (pe,) = call(pack_pe_kernel, [shape(rows, WIDE)], [SM] + [VM] * 6, planes, moved=1 << 20)(
         place, consts, coef, se_got, so_got, u_now, u_prev
     )
     pe_got = swap(pe, "plan", 0)
-    (inner,) = call(
-        main_kernel,
-        [shape(*cells)],
-        [SM] + [VM] * 6,
-        [
-            pltpu.VMEM((3, 20, 16, WIDE), F32),
-            pltpu.VMEM((3, 18, 16, WIDE), F32),
-            pltpu.VMEM((3, 18, 16, WIDE), F32),
-        ],
-        flops=60_000_000,
-        moved=4 << 20,
-    )(place, consts, coef, se_got, so_got, u_now, u_prev)
+    (inner,) = call(main_kernel, [shape(*cells)], [SM] + [VM] * 6, levels, flops=60_000_000, moved=4 << 20)(
+        place, consts, coef, se_got, so_got, u_now, u_prev
+    )
+    half = shape(3, 16, 8, WIDE)
+    work = [pltpu.VMEM((3, 16, 8, WIDE), F32), pltpu.VMEM((3 * PAD, WIDE), F32), pltpu.SemaphoreType.DMA((3,))]
+    out, rest = call(
+        tail_pe_kernel, [shape(*cells), half], [SM] + [VM] * 4, work, flops=5_000_000, moved=2 << 20, places=[HB, VM]
+    )(place, coef, pe, pe_got, inner)
     (out,) = call(
-        tail_kernel, [shape(*cells)], [SM] + [VM] * 6, [pltpu.VMEM((3 * PAD, WIDE), F32)], flops=10_000_000, moved=3 << 20
-    )(place, coef, pe, po, pe_got, po_got, inner)
+        tail_po_kernel, [shape(*cells)], [SM] + [VM] * 4 + [HB], work, flops=5_000_000, moved=2 << 20, places=[HB], aliases={5: 0}
+    )(place, coef, po, po_got, rest, out)
     return out
 
 

time: 44 us -> 41 us (0.932)
  the two profiles are of different devices: /device:TPU:24 before, /device:TPU:16 now
where the time goes in v4:
time: 41 us; the launch traced here: 40.8 us
  blocking collectives  18.3 us (45%)
  Pallas kernels  11.8 us (29%)
  starting transfers between devices  9.79 us (24%)
  local copies, waits for them, and re-layouts  0.75 us (2%)
    all_to_all x1, blocking collectives, local(): masses = lax.all_to_all(masses, 'story', 0, 0, tiled=True)  18.3 us
    ppermute x4, starting transfers between devices, swap(): return lax.ppermute(values, axis, pairs)  9.79 us
    pallas_call x1, Pallas kernels, local(): call(main_kernel, [shape(*cells)], [SM] + [VM] * 6, levels, flops=6000000...  4.48 us
    pallas_call x1, Pallas kernels, local(): call(tail_po_kernel, [shape(*cells)], [SM] + [VM] * 4 + [HB], work, flops...  2 us
    pallas_call x1, Pallas kernels, local(): call(tail_pe_kernel, [shape(*cells), half], [SM] + [VM] * 4, work, flops=...  1.98 us
    pallas_call x1, Pallas kernels, local(): call(functools.partial(prep_kernel, factor=0.8 / height), [face, face, sh...  1.62 us
    pallas_call x1, Pallas kernels, local(): call(pack_po_kernel, [shape(rows + 8, WIDE), table], [SM] + [VM] * 6, pla...  0.86 us
    pallas_call x1, Pallas kernels, local(): call(pack_pe_kernel, [shape(rows, WIDE)], [SM] + [VM] * 6, planes, moved=...  0.85 us
  transfers between devices with their start and end apart: 4, of which 0 were waited for; matrix products, arithmetic and copies ran while one was open for 0% of the time, Pallas kernels for 18%

profile of v4, /device:TPU:16, one launch (start us, length us, event | category | flops | bytes accessed | tf_op | source)
XLA Modules:
  0.0 40.8 jit_solution(10586443871109889362)
XLA Ops:
  0.0 0.1 pad_add_fusion.place
  0.1 0.0 copy-start.5
  0.1 0.0 copy-start.6
  0.1 0.0 copy-start.2
  0.1 0.0 copy-start.3
  0.1 0.0 copy-start.4
  0.1 0.6 %copy-done.5 = f32[8]{0:T(128)S(1)} copy-done((f32[8]{0:T(128)S(1)}, f32[8]{0:T(128)}, u32[]{:S(2)}) %copy-start.5) | copy-done | bytes 56
  0.7 0.0 copy-done.6
  0.7 0.0 copy-done.2
  0.8 0.0 copy-done.3
  0.8 0.0 copy-done.4
  0.8 0.0 copy-start
  0.8 0.0 copy-start.1
  0.8 1.6 %shard_map.73 = (f32[10,16,256]{2,1,0:T(8,128)S(1)}, f32[10,16,256]{2,1,0:T(8,128)S(1)}, f32[32,256]{1,0:T(8,128)S(1)}, f32[8,256]{1,0:T(8,128)S(1)}) custom-call(s32[2]{0:T(128)S(1)} %pad_add_fusion.place, s32[16]{0:T(128)S(1)} %bitcast.10, s32[16]{0:T(128)S(1)} %bitcast.11, f32[8]{0:T(128)S(1)} %copy-done.4, f32[8]{0:T(128)S(1)} %copy-done.5, ...), custom_call_target="tpu_custom_call" | custom-call | bytes 1048576 | tf_op jit(solution)/shard_map/pallas_call | solution.py:365
  2.4 0.1 collective-permute-start
  2.5 0.7 %collective-permute-start.1 = (f32[10,16,256]{2,1,0:T(8,128)S(1)}, f32[10,16,256]{2,1,0:T(8,128)S(1)}, u32[]{:S(2)}, u32[]{:S(2)}) collective-permute-start(f32[10,16,256]{2,1,0:T(8,128)S(1)} %get-tuple-element.15), channel_id=1, source_target_pairs={{8,16},{16,8},{24,32},{32,24},{40,48},{48,40},{56,64},{64,56},{72,... | collective-permute-start | bytes 491528 | tf_op jit(solution)/shard_map/ppermute | solution.py:20
  3.2 18.3 %all_to_all.11 = f32[32,1,256]{2,1,0:T(1,128)S(1)} all-to-all(f32[32,1,256]{2,1,0:T(1,128)S(1)} %copy.9), channel_id=1, replica_groups=mesh['story'=32,'plan'=8] {'story'}, dimensions={0} | all-to-all | bytes 65536 | tf_op jit(solution)/shard_map/all_to_all | solution.py:379
  21.5 0.0 collective-permute-done.se
  21.5 0.0 collective-permute-done.1.so
  21.5 0.0 copy-done
  21.5 0.0 copy-done.1
  21.5 0.9 %shard_map.74 = (f32[128,256]{1,0:T(8,128)S(1)}, f32[4,24,256]{2,1,0:T(8,128)S(1)}) custom-call(s32[2]{0:T(128)S(1)} %pad_add_fusion.place, f32[8,256]{1,0:T(8,128)S(1)} %get-tuple-element.13.consts, f32[10,16,256]{2,1,0:T(8,128)S(1)} %collective-permute-done.se, f32[10,16,256]{2,1,0:T(8,128)S(1)} %collective-permute-done.1.so, f32[32,256]{1,0:T(8,128)S(1)} %bitcast.8, ...), custom_call_target="tpu_custom_call" | custom-call | bytes 1048576 | tf_op jit(solution)/shard_map/pallas_call | solution.py:381
  22.4 2.4 %collective-permute-start.2 = (f32[128,256]{1,0:T(8,128)S(1)}, f32[128,256]{1,0:T(8,128)S(1)}, u32[]{:S(2)}, u32[]{:S(2)}) collective-permute-start(f32[128,256]{1,0:T(8,128)S(1)} %get-tuple-element.18.sent), channel_id=1, source_target_pairs={{1,2},{2,1},{3,4},{4,3},{5,6},{6,5},{9,10},{10,9},{11,12},{12,11},... | collective-permute-start | bytes 393224 | tf_op jit(solution)/shard_map/ppermute | solution.py:20
  24.8 0.8 %shard_map.75.sent = f32[120,256]{1,0:T(8,128)S(1)} custom-call(s32[2]{0:T(128)S(1)} %pad_add_fusion.place, f32[8,256]{1,0:T(8,128)S(1)} %get-tuple-element.13.consts, f32[4,24,256]{2,1,0:T(8,128)S(1)} %get-tuple-element.17.coef, f32[10,16,256]{2,1,0:T(8,128)S(1)} %collective-permute-done.se, f32[10,16,256]{2,1,0:T(8,128)S(1)} %collective-permute-done.1.so, ...), custom_call_target="tpu_custom_call" | custom-call | bytes 1048576 | tf_op jit(solution)/shard_map/pallas_call | solution.py:390
  25.6 6.7 %collective-permute-start.3 = (f32[120,256]{1,0:T(8,128)S(1)}, f32[120,256]{1,0:T(8,128)S(1)}, u32[]{:S(2)}, u32[]{:S(2)}) collective-permute-start(f32[120,256]{1,0:T(8,128)S(1)} %shard_map.75.sent), channel_id=1, source_target_pairs={{0,1},{1,0},{2,3},{3,2},{4,5},{5,4},{6,7},{7,6},{8,9},{9,8},{10,11... | collective-permute-start | bytes 368648 | tf_op jit(solution)/shard_map/ppermute | solution.py:20
  32.3 4.5 %shard_map.76.inner = f32[3,16,16,256]{3,2,1,0:T(8,128)S(1)} custom-call(s32[2]{0:T(128)S(1)} %pad_add_fusion.place, f32[8,256]{1,0:T(8,128)S(1)} %get-tuple-element.13.consts, f32[4,24,256]{2,1,0:T(8,128)S(1)} %get-tuple-element.17.coef, f32[10,16,256]{2,1,0:T(8,128)S(1)} %collective-permute-done.se, f32[10,16,256]{2,1,0:T(8,128)S(1)} %collective-permute-done.1.so, ...), custom_call_target="tpu_custom_call" | custom-call | flops 60000000 | bytes 4194304 | tf_op jit(solution)/shard_map/pallas_call | solution.py:394
  36.8 0.0 collective-permute-done.3.got
  36.8 2.0 %shard_map.77 = (f32[3,16,16,256]{3,2,1,0:T(8,128)}, f32[3,16,8,256]{3,2,1,0:T(8,128)S(1)}) custom-call(s32[2]{0:T(128)S(1)} %pad_add_fusion.place, f32[4,24,256]{2,1,0:T(8,128)S(1)} %get-tuple-element.17.coef, f32[120,256]{1,0:T(8,128)S(1)} %shard_map.75.sent, f32[120,256]{1,0:T(8,128)S(1)} %collective-permute-done.3.got, ...), custom_call_target="tpu_custom_call" | custom-call | flops 5000000 | bytes 2097152 | tf_op jit(solution)/shard_map/pallas_call | solution.py:399
  38.8 0.0 collective-permute-done.2.got
  38.8 2.0 %shard_map.78 = f32[3,16,16,256]{3,2,1,0:T(8,128)} custom-call(s32[2]{0:T(128)S(1)} %pad_add_fusion.place, f32[4,24,256]{2,1,0:T(8,128)S(1)} %get-tuple-element.17.coef, f32[128,256]{1,0:T(8,128)S(1)} %get-tuple-element.18.sent, f32[128,256]{1,0:T(8,128)S(1)} %collective-permute-done.2.got, ...), custom_call_target="tpu_custom_call", output_to_operand_aliasing={{}: (5, {})} | custom-call | flops 5000000 | bytes 2097152 | tf_op jit(solution)/shard_map/pallas_call | solution.py:402
  (2 shorter events, 0.0 us)
Async XLA Ops:
  0.1 0.7 %copy-start.5 = (f32[8]{0:T(128)S(1)}, f32[8]{0:T(128)}, u32[]{:S(2)}) copy-start(f32[8]{0:T(128)} %lame_t.1) | copy-start | bytes 100
  0.1 0.7 %copy-start.6 = (f32[8]{0:T(128)S(1)}, f32[8]{0:T(128)}, u32[]{:S(2)}) copy-start(f32[8]{0:T(128)} %dens_t.1) | copy-start | bytes 100
  0.1 0.7 %copy-start.2 = (s32[1,1,16]{2,1,0:T(1,128)S(1)}, s32[1,1,16]{2,1,0:T(1,128)}, u32[]{:S(2)}) copy-start(s32[1,1,16]{2,1,0:T(1,128)} %param.9) | copy-start | bytes 196
  0.1 0.7 %copy-start.3 = (s32[1,1,16]{2,1,0:T(1,128)S(1)}, s32[1,1,16]{2,1,0:T(1,128)}, u32[]{:S(2)}) copy-start(s32[1,1,16]{2,1,0:T(1,128)} %param.10) | copy-start | bytes 196
  0.1 0.7 %copy-start.4 = (f32[8]{0:T(128)S(1)}, f32[8]{0:T(128)}, u32[]{:S(2)}) copy-start(f32[8]{0:T(128)} %shear_t.1) | copy-start | bytes 100
  0.8 20.7 %copy-start = (f32[3,16,16,256]{3,2,1,0:T(8,128)S(1)}, f32[3,16,16,256]{3,2,1,0:T(8,128)}, u32[]{:S(2)}) copy-start(f32[3,16,16,256]{3,2,1,0:T(8,128)} %now.7) | copy-start | bytes 2359300
  0.8 20.7 %copy-start.1 = (f32[3,16,16,256]{3,2,1,0:T(8,128)S(1)}, f32[3,16,16,256]{3,2,1,0:T(8,128)}, u32[]{:S(2)}) copy-start(f32[3,16,16,256]{3,2,1,0:T(8,128)} %prev.7) | copy-start | bytes 2359300
  2.4 19.1 %collective-permute-start = (f32[10,16,256]{2,1,0:T(8,128)S(1)}, f32[10,16,256]{2,1,0:T(8,128)S(1)}, u32[]{:S(2)}, u32[]{:S(2)}) collective-permute-start(f32[10,16,256]{2,1,0:T(8,128)S(1)} %get-tuple-element.14), channel_id=1, source_target_pairs={{0,8},{8,0},{16,24},{24,16},{32,40},{40,32},{48,56},{56,48},{64,72... | collective-permute-start | bytes 491528 | tf_op jit(solution)/shard_map/ppermute | solution.py:20
  2.5 19.0 %collective-permute-start.1 = (f32[10,16,256]{2,1,0:T(8,128)S(1)}, f32[10,16,256]{2,1,0:T(8,128)S(1)}, u32[]{:S(2)}, u32[]{:S(2)}) collective-permute-start(f32[10,16,256]{2,1,0:T(8,128)S(1)} %get-tuple-element.15), channel_id=1, source_target_pairs={{8,16},{16,8},{24,32},{32,24},{40,48},{48,40},{56,64},{64,56},{72,... | collective-permute-start | bytes 491528 | tf_op jit(solution)/shard_map/ppermute | solution.py:20
  22.4 16.4 %collective-permute-start.2 = (f32[128,256]{1,0:T(8,128)S(1)}, f32[128,256]{1,0:T(8,128)S(1)}, u32[]{:S(2)}, u32[]{:S(2)}) collective-permute-start(f32[128,256]{1,0:T(8,128)S(1)} %get-tuple-element.18.sent), channel_id=1, source_target_pairs={{1,2},{2,1},{3,4},{4,3},{5,6},{6,5},{9,10},{10,9},{11,12},{12,11},... | collective-permute-start | bytes 393224 | tf_op jit(solution)/shard_map/ppermute | solution.py:20
  25.6 11.2 %collective-permute-start.3 = (f32[120,256]{1,0:T(8,128)S(1)}, f32[120,256]{1,0:T(8,128)S(1)}, u32[]{:S(2)}, u32[]{:S(2)}) collective-permute-start(f32[120,256]{1,0:T(8,128)S(1)} %shard_map.75.sent), channel_id=1, source_target_pairs={{0,1},{1,0},{2,3},{3,2},{4,5},{5,4},{6,7},{7,6},{8,9},{9,8},{10,11... | collective-permute-start | bytes 368648 | tf_op jit(solution)/shard_map/ppermute | solution.py:20

commit v5 on v4

--- a/solution.py
+++ b/solution.py
@@ -153,22 +153,33 @@
     return ghost
 
 
-def fill(ghost, consts, coef, now, prev, out, far_rows, prev_rows, near, far, sign):
+def fill(right, ghost, consts, coef, now, prev, out, far_rows, prev_rows):
     occupied = consts[4:5, :]
-    for c in range(3):
-        for target, base, source, x in ((out, c * PAD, now, near), (far_rows, c * PAD, now, far), (prev_rows, c * PAD, prev, near)):
-            target[base + 4 : base + 20, :] = source[c, :, x, :] * occupied
-            kinds = (6,) if source is prev else (0, 3)
-            for k, kind in enumerate(kinds):
-                target[base + 3 - k : base + 4 - k, :] = ghost(False, kind + c, pl.ds(x, 1), slice(None))
-                target[base + 20 + k : base + 21 + k, :] = ghost(True, kind + c, pl.ds(x, 1), slice(None))
+
+    def load(near, far):
+        for c in range(3):
+            for target, source, x in ((out, now, near), (far_rows, now, far), (prev_rows, prev, near)):
+                base = c * PAD
+                target[base + 4 : base + 20, :] = source[c, :, x, :] * occupied
+                kinds = (6,) if source is prev else (0, 3)
+                for k, kind in enumerate(kinds):
+                    target[base + 3 - k : base + 4 - k, :] = ghost(False, kind + c, pl.ds(x, 1), slice(None))
+                    target[base + 20 + k : base + 21 + k, :] = ghost(True, kind + c, pl.ds(x, 1), slice(None))
+
+    @pl.when(right)
+    def _():
+        load(15, 14)
+
+    @pl.when(jnp.logical_not(right))
+    def _():
+        load(0, 1)
+
     order = (1, 0, 2)
 
     def planes(ref):
         return [ref[c * PAD : (c + 1) * PAD, :] for c in order]
 
-    here = planes(out)
-    first = advance(planes(far_rows), here, None, planes(prev_rows), [coef[k] for k in range(4)], sign)
+    first = advance(planes(far_rows), planes(out), None, planes(prev_rows), [coef[k] for k in range(4)], jnp.where(right, 1.0, -1.0))
     for k, c in enumerate(order):
         out[3 * PAD + 16 * c : 3 * PAD + 16 * c + 16, :] = first[k][4:20]
         out[c * PAD : c * PAD + 1, :] = first[k][3:4]
@@ -189,15 +200,7 @@
     under = [ghost(False, 9, pl.ds(k, 1), slice(None)) for k in range(4)]
     for k, rows in enumerate(coefficients(own, over, under, carried)):
         coef[k] = rows
-    even_plan = place[1] % 2 == 0
-
-    @pl.when(even_plan)
-    def _():
-        fill(ghost, consts, coef, now, prev, po, far_rows, prev_rows, 0, 1, -1.0)
-
-    @pl.when(jnp.logical_not(even_plan))
-    def _():
-        fill(ghost, consts, coef, now, prev, po, far_rows, prev_rows, 15, 14, None)
+    fill(place[1] % 2 == 1, ghost, consts, coef, now, prev, po, far_rows, prev_rows)
 
 
 def advance(below, here, above, before, coefs, sign):
@@ -215,7 +218,11 @@
     return 2.0 * here - before + a * lap + b * coup - geometric
 
 
-def main_kernel(place, consts, coef, se, so, now, prev, out, u0, u1, before):
+def crosses(place, plans):
+    return jnp.logical_or(place[1] == plans // 2 - 1, place[1] == plans // 2)
+
+
+def both_steps(place, consts, coef, se, so, now, prev, out, u0, u1, before):
     ghost = ghost_of(place, se, so)
     occupied = jnp.broadcast_to(consts[4:5, :], (16, WIDE))
     for c in range(3):
@@ -248,20 +255,21 @@
         one(u1, lambda c, i: u0[c, i + 2], out, i, 4)
 
 
-def pack_pe_kernel(place, consts, coef, se, so, now, prev, pe, far_rows, prev_rows):
-    ghost = ghost_of(place, se, so)
-    even_plan = place[1] % 2 == 0
-
-    @pl.when(even_plan)
-    def _():
-        fill(ghost, consts, coef, now, prev, pe, far_rows, prev_rows, 15, 14, None)
-
-    @pl.when(jnp.logical_not(even_plan))
-    def _():
-        fill(ghost, consts, coef, now, prev, pe, far_rows, prev_rows, 0, 1, -1.0)
-
-
-def one_side(coef, sent, got, work, held, near, far, sign):
+def early_kernel(place, consts, coef, se, so, now, prev, pe, out, far_rows, prev_rows, u0, u1, before, *, plans):
+    fill(place[1] % 2 == 0, ghost_of(place, se, so), consts, coef, now, prev, pe, far_rows, prev_rows)
+
+    @pl.when(jnp.logical_not(crosses(place, plans)))
+    def _():
+        both_steps(place, consts, coef, se, so, now, prev, out, u0, u1, before)
+
+
+def late_kernel(place, consts, coef, se, so, now, prev, out, u0, u1, before, *, plans):
+    @pl.when(crosses(place, plans))
+    def _():
+        both_steps(place, consts, coef, se, so, now, prev, out, u0, u1, before)
+
+
+def one_side(coef, sent, got, held, sign):
     order = (1, 0, 2)
 
     def planes(ref):
@@ -287,50 +295,56 @@
     zero = jnp.zeros((PAD, WIDE), F32)
     near_more = advance(None, delta, outer, [zero] * 3, (a, b, gu, gd), sign)
     lap, coup = stencil(None, None, delta, sign)
+    near, far = [None] * 3, [None] * 3
     for k, c in enumerate(order):
-        work[c, :, near, :] += near_more[k][4:20]
-        work[c, :, far, :] += (a * lap[k] + b * coup[k])[4:20]
-
-
-def write_half(work, out, first, sems):
-    copies = [pltpu.make_async_copy(work.at[c], out.at[c, :, pl.ds(first, 8), :], sems.at[c]) for c in range(3)]
-    for copy in copies:
-        copy.start()
-    for copy in copies:
-        copy.wait()
-
-
-def tail_pe_kernel(place, coef, sent, got, inner, out, rest, work, held, sems):
-    even_plan = place[1] % 2 == 0
-
-    @pl.when(even_plan)
-    def _():
-        work[...] = inner[:, :, 8:16, :]
-        rest[...] = inner[:, :, 0:8, :]
-        one_side(coef, sent, got, work, held, 7, 6, None)
-        write_half(work, out, 8, sems)
-
-    @pl.when(jnp.logical_not(even_plan))
-    def _():
-        work[...] = inner[:, :, 0:8, :]
-        rest[...] = inner[:, :, 8:16, :]
-        one_side(coef, sent, got, work, held, 0, 1, -1.0)
-        write_half(work, out, 0, sems)
+        near[c] = near_more[k][4:20]
+        far[c] = (a * lap[k] + b * coup[k])[4:20]
+    return near, far
+
+
+def write_half(right, near, far, work, out, sems):
+    def put(near_row, far_row, first):
+        copies = []
+        for c in range(3):
+            work[c, :, near_row, :] += near[c]
+            work[c, :, far_row, :] += far[c]
+            copies.append(pltpu.make_async_copy(work.at[c], out.at[c, :, pl.ds(first, 8), :], sems.at[c]))
+            copies[-1].start()
+        for copy in copies:
+            copy.wait()
+
+    @pl.when(right)
+    def _():
+        put(7, 6, 8)
+
+    @pl.when(jnp.logical_not(right))
+    def _():
+        put(0, 1, 0)
+
+
+def tail_pe_kernel(place, coef, sent, got, early, late, out, rest, work, held, sems, *, plans):
+    right = place[1] % 2 == 0
+    for inner, use in ((late, crosses(place, plans)), (early, jnp.logical_not(crosses(place, plans)))):
+
+        @pl.when(jnp.logical_and(use, right))
+        def _(inner=inner):
+            work[...] = inner[:, :, 8:16, :]
+            rest[...] = inner[:, :, 0:8, :]
+
+        @pl.when(jnp.logical_and(use, jnp.logical_not(right)))
+        def _(inner=inner):
+            work[...] = inner[:, :, 0:8, :]
+            rest[...] = inner[:, :, 8:16, :]
+
+    near, far = one_side(coef, sent, got, held, jnp.where(right, 1.0, -1.0))
+    write_half(right, near, far, work, out, sems)
 
 
 def tail_po_kernel(place, coef, sent, got, rest, half, out, work, held, sems):
-    even_plan = place[1] % 2 == 0
+    right = place[1] % 2 == 1
     work[...] = rest[...]
-
-    @pl.when(even_plan)
-    def _():
-        one_side(coef, sent, got, work, held, 0, 1, -1.0)
-        write_half(work, out, 0, sems)
-
-    @pl.when(jnp.logical_not(even_plan))
-    def _():
-        one_side(coef, sent, got, work, held, 7, 6, None)
-        write_half(work, out, 8, sems)
+    near, far = one_side(coef, sent, got, held, jnp.where(right, 1.0, -1.0))
+    write_half(right, near, far, work, out, sems)
 
 
 VM = pl.BlockSpec(memory_space=pltpu.VMEM)
@@ -357,7 +371,7 @@
 
 def local(u_now, u_prev, occupancy, materials, shear_table, lame_table, density_table):
     height = u_now.shape[1] * lax.axis_size("story")
-    stories = lax.axis_size("story")
+    stories, plans = lax.axis_size("story"), lax.axis_size("plan")
     place = jnp.stack([lax.axis_index("story"), lax.axis_index("plan")]).astype(jnp.int32)
     face, table = shape(10, 16, WIDE), shape(4, PAD, WIDE)
     rows = 3 * PAD + 48
@@ -387,18 +401,30 @@
         pltpu.VMEM((3, 18, 16, WIDE), F32),
         pltpu.VMEM((3, 18, 16, WIDE), F32),
     ]
-    (pe,) = call(pack_pe_kernel, [shape(rows, WIDE)], [SM] + [VM] * 6, planes, moved=1 << 20)(
-        place, consts, coef, se_got, so_got, u_now, u_prev
-    )
+    own = (place, consts, coef, se_got, so_got, u_now, u_prev)
+    pe, early = call(
+        functools.partial(early_kernel, plans=plans),
+        [shape(rows, WIDE), shape(*cells)],
+        [SM] + [VM] * 6,
+        planes + levels,
+        flops=60_000_000,
+        moved=4 << 20,
+    )(*own)
     pe_got = swap(pe, "plan", 0)
-    (inner,) = call(main_kernel, [shape(*cells)], [SM] + [VM] * 6, levels, flops=60_000_000, moved=4 << 20)(
-        place, consts, coef, se_got, so_got, u_now, u_prev
-    )
+    (late,) = call(
+        functools.partial(late_kernel, plans=plans), [shape(*cells)], [SM] + [VM] * 6, levels, flops=60_000_000, moved=4 << 20
+    )(*own)
     half = shape(3, 16, 8, WIDE)
     work = [pltpu.VMEM((3, 16, 8, WIDE), F32), pltpu.VMEM((3 * PAD, WIDE), F32), pltpu.SemaphoreType.DMA((3,))]
     out, rest = call(
-        tail_pe_kernel, [shape(*cells), half], [SM] + [VM] * 4, work, flops=5_000_000, moved=2 << 20, places=[HB, VM]
-    )(place, coef, pe, pe_got, inner)
+        functools.partial(tail_pe_kernel, plans=plans),
+        [shape(*cells), half],
+        [SM] + [VM] * 5,
+        work,
+        flops=5_000_000,
+        moved=2 << 20,
+        places=[HB, VM],
+    )(place, coef, pe, pe_got, early, late)
     (out,) = call(
         tail_po_kernel, [shape(*cells)], [SM] + [VM] * 4 + [HB], work, flops=5_000_000, moved=2 << 20, places=[HB], aliases={5: 0}
     )(place, coef, po, po_got, rest, out)

time: 41 us -> 40.2 us (0.980)
  the two profiles are of different devices: /device:TPU:16 before, /device:TPU:24 now
where the time goes in v5:
time: 40.2 us; the launch traced here: 40 us
  blocking collectives  18.3 us (46%)
  Pallas kernels  11.8 us (29%)
  starting transfers between devices  8.52 us (21%)
  local copies, waits for them, and re-layouts  0.75 us (2%)
  waiting for transfers between devices  0.41 us (1%)
    all_to_all x1, blocking collectives, local(): masses = lax.all_to_all(masses, 'story', 0, 0, tiled=True)  18.3 us
    ppermute x4, starting transfers between devices, swap(): return lax.ppermute(values, axis, pairs)  8.52 us
    pallas_call x1, Pallas kernels, local(): call(functools.partial(late_kernel, plans=plans), [shape(*cells)], [SM] +...  4.49 us
    pallas_call x1, Pallas kernels, local(): call(functools.partial(tail_pe_kernel, plans=plans), [shape(*cells), half...  2.04 us
    pallas_call x1, Pallas kernels, local(): call(tail_po_kernel, [shape(*cells)], [SM] + [VM] * 4 + [HB], work, flops...  1.97 us
    pallas_call x1, Pallas kernels, local(): call(functools.partial(prep_kernel, factor=0.8 / height), [face, face, sh...  1.62 us
    pallas_call x1, Pallas kernels, local(): call(pack_po_kernel, [shape(rows + 8, WIDE), table], [SM] + [VM] * 6, pla...  0.86 us
    pallas_call x1, Pallas kernels, local(): call(functools.partial(early_kernel, plans=plans), [shape(rows, WIDE), sh...  0.85 us
  transfers between devices with their start and end apart: 4, of which 1 were waited for; matrix products, arithmetic and copies ran while one was open for 0% of the time, Pallas kernels for 18%

profile of v5, /device:TPU:24, one launch (start us, length us, event | category | flops | bytes accessed | tf_op | source)
XLA Modules:
  0.0 40.0 jit_solution(12828228956763288517)
XLA Ops:
  0.0 0.1 pad_add_fusion.place
  0.1 0.0 copy-start.5
  0.1 0.0 copy-start.6
  0.1 0.0 copy-start.2
  0.1 0.0 copy-start.3
  0.1 0.0 copy-start.4
  0.1 0.6 %copy-done.5 = f32[8]{0:T(128)S(1)} copy-done((f32[8]{0:T(128)S(1)}, f32[8]{0:T(128)}, u32[]{:S(2)}) %copy-start.5) | copy-done | bytes 56
  0.7 0.0 copy-done.6
  0.7 0.0 copy-done.2
  0.8 0.0 copy-done.3
  0.8 0.0 copy-done.4
  0.8 0.0 copy-start
  0.8 0.0 copy-start.1
  0.8 1.6 %shard_map.73 = (f32[10,16,256]{2,1,0:T(8,128)S(1)}, f32[10,16,256]{2,1,0:T(8,128)S(1)}, f32[32,256]{1,0:T(8,128)S(1)}, f32[8,256]{1,0:T(8,128)S(1)}) custom-call(s32[2]{0:T(128)S(1)} %pad_add_fusion.place, s32[16]{0:T(128)S(1)} %bitcast.10, s32[16]{0:T(128)S(1)} %bitcast.11, f32[8]{0:T(128)S(1)} %copy-done.4, f32[8]{0:T(128)S(1)} %copy-done.5, ...), custom_call_target="tpu_custom_call" | custom-call | bytes 1048576 | tf_op jit(solution)/shard_map/pallas_call | solution.py:379
  2.4 0.1 collective-permute-start
  2.5 0.7 %collective-permute-start.1 = (f32[10,16,256]{2,1,0:T(8,128)S(1)}, f32[10,16,256]{2,1,0:T(8,128)S(1)}, u32[]{:S(2)}, u32[]{:S(2)}) collective-permute-start(f32[10,16,256]{2,1,0:T(8,128)S(1)} %get-tuple-element.17), channel_id=1, source_target_pairs={{8,16},{16,8},{24,32},{32,24},{40,48},{48,40},{56,64},{64,56},{72,... | collective-permute-start | bytes 491528 | tf_op jit(solution)/shard_map/ppermute | solution.py:20
  3.2 18.3 %all_to_all.11 = f32[32,1,256]{2,1,0:T(1,128)S(1)} all-to-all(f32[32,1,256]{2,1,0:T(1,128)S(1)} %copy.9), channel_id=1, replica_groups=mesh['story'=32,'plan'=8] {'story'}, dimensions={0} | all-to-all | bytes 65536 | tf_op jit(solution)/shard_map/all_to_all | solution.py:393
  21.5 0.0 collective-permute-done.se
  21.5 0.0 collective-permute-done.1.so
  21.5 0.0 copy-done
  21.5 0.0 copy-done.1
  21.5 0.9 %shard_map.74 = (f32[128,256]{1,0:T(8,128)S(1)}, f32[4,24,256]{2,1,0:T(8,128)S(1)}) custom-call(s32[2]{0:T(128)S(1)} %pad_add_fusion.place, f32[8,256]{1,0:T(8,128)S(1)} %get-tuple-element.15.consts, f32[10,16,256]{2,1,0:T(8,128)S(1)} %collective-permute-done.se, f32[10,16,256]{2,1,0:T(8,128)S(1)} %collective-permute-done.1.so, f32[32,256]{1,0:T(8,128)S(1)} %bitcast.8, ...), custom_call_target="tpu_custom_call" | custom-call | bytes 1048576 | tf_op jit(solution)/shard_map/pallas_call | solution.py:395
  22.4 7.7 %collective-permute-start.2 = (f32[128,256]{1,0:T(8,128)S(1)}, f32[128,256]{1,0:T(8,128)S(1)}, u32[]{:S(2)}, u32[]{:S(2)}) collective-permute-start(f32[128,256]{1,0:T(8,128)S(1)} %get-tuple-element.20.sent), channel_id=1, source_target_pairs={{1,2},{2,1},{3,4},{4,3},{5,6},{6,5},{9,10},{10,9},{11,12},{12,11},... | collective-permute-start | bytes 393224 | tf_op jit(solution)/shard_map/ppermute | solution.py:20
  30.1 0.9 %shard_map.75 = (f32[120,256]{1,0:T(8,128)S(1)}, f32[3,16,16,256]{3,2,1,0:T(8,128)S(1)}) custom-call(s32[2]{0:T(128)S(1)} %pad_add_fusion.place, f32[8,256]{1,0:T(8,128)S(1)} %get-tuple-element.15.consts, f32[4,24,256]{2,1,0:T(8,128)S(1)} %get-tuple-element.19.coef, f32[10,16,256]{2,1,0:T(8,128)S(1)} %collective-permute-done.se, ...), custom_call_target="tpu_custom_call" | custom-call | flops 60000000 | bytes 4194304 | tf_op jit(solution)/shard_map/pallas_call | solution.py:405
  30.9 0.1 collective-permute-start.3
  31.0 4.5 %shard_map.76.late = f32[3,16,16,256]{3,2,1,0:T(8,128)S(1)} custom-call(s32[2]{0:T(128)S(1)} %pad_add_fusion.place, f32[8,256]{1,0:T(8,128)S(1)} %get-tuple-element.15.consts, f32[4,24,256]{2,1,0:T(8,128)S(1)} %get-tuple-element.19.coef, f32[10,16,256]{2,1,0:T(8,128)S(1)} %collective-permute-done.se, f32[10,16,256]{2,1,0:T(8,128)S(1)} %collective-permute-done.1.so, ...), custom_call_target="tpu_custom_call" | custom-call | flops 60000000 | bytes 4194304 | tf_op jit(solution)/shard_map/pallas_call | solution.py:414
  35.5 0.4 %collective-permute-done.3.got = f32[120,256]{1,0:T(8,128)S(1)} collective-permute-done((f32[120,256]{1,0:T(8,128)S(1)}, f32[120,256]{1,0:T(8,128)S(1)}, u32[]{:S(2)}, u32[]{:S(2)}) %collective-permute-start.3) | collective-permute-done | bytes 122912 | tf_op jit(solution)/shard_map/ppermute | solution.py:20
  35.9 2.0 %shard_map.77 = (f32[3,16,16,256]{3,2,1,0:T(8,128)}, f32[3,16,8,256]{3,2,1,0:T(8,128)S(1)}) custom-call(s32[2]{0:T(128)S(1)} %pad_add_fusion.place, f32[4,24,256]{2,1,0:T(8,128)S(1)} %get-tuple-element.19.coef, f32[120,256]{1,0:T(8,128)S(1)} %get-tuple-element.21.sent, f32[120,256]{1,0:T(8,128)S(1)} %collective-permute-done.3.got, ...), custom_call_target="tpu_custom_call" | custom-call | flops 5000000 | bytes 2097152 | tf_op jit(solution)/shard_map/pallas_call | solution.py:419
  38.0 0.0 collective-permute-done.2.got
  38.0 2.0 %shard_map.78 = f32[3,16,16,256]{3,2,1,0:T(8,128)} custom-call(s32[2]{0:T(128)S(1)} %pad_add_fusion.place, f32[4,24,256]{2,1,0:T(8,128)S(1)} %get-tuple-element.19.coef, f32[128,256]{1,0:T(8,128)S(1)} %get-tuple-element.20.sent, f32[128,256]{1,0:T(8,128)S(1)} %collective-permute-done.2.got, ...), custom_call_target="tpu_custom_call", output_to_operand_aliasing={{}: (5, {})} | custom-call | flops 5000000 | bytes 2097152 | tf_op jit(solution)/shard_map/pallas_call | solution.py:428
  (2 shorter events, 0.0 us)
Async XLA Ops:
  0.1 0.7 %copy-start.5 = (f32[8]{0:T(128)S(1)}, f32[8]{0:T(128)}, u32[]{:S(2)}) copy-start(f32[8]{0:T(128)} %lame_t.1) | copy-start | bytes 100
  0.1 0.7 %copy-start.6 = (f32[8]{0:T(128)S(1)}, f32[8]{0:T(128)}, u32[]{:S(2)}) copy-start(f32[8]{0:T(128)} %dens_t.1) | copy-start | bytes 100
  0.1 0.7 %copy-start.2 = (s32[1,1,16]{2,1,0:T(1,128)S(1)}, s32[1,1,16]{2,1,0:T(1,128)}, u32[]{:S(2)}) copy-start(s32[1,1,16]{2,1,0:T(1,128)} %param.9) | copy-start | bytes 196
  0.1 0.7 %copy-start.3 = (s32[1,1,16]{2,1,0:T(1,128)S(1)}, s32[1,1,16]{2,1,0:T(1,128)}, u32[]{:S(2)}) copy-start(s32[1,1,16]{2,1,0:T(1,128)} %param.10) | copy-start | bytes 196
  0.1 0.7 %copy-start.4 = (f32[8]{0:T(128)S(1)}, f32[8]{0:T(128)}, u32[]{:S(2)}) copy-start(f32[8]{0:T(128)} %shear_t.1) | copy-start | bytes 100
  0.8 20.7 %copy-start = (f32[3,16,16,256]{3,2,1,0:T(8,128)S(1)}, f32[3,16,16,256]{3,2,1,0:T(8,128)}, u32[]{:S(2)}) copy-start(f32[3,16,16,256]{3,2,1,0:T(8,128)} %now.7) | copy-start | bytes 2359300
  0.8 20.7 %copy-start.1 = (f32[3,16,16,256]{3,2,1,0:T(8,128)S(1)}, f32[3,16,16,256]{3,2,1,0:T(8,128)}, u32[]{:S(2)}) copy-start(f32[3,16,16,256]{3,2,1,0:T(8,128)} %prev.7) | copy-start | bytes 2359300
  2.4 19.1 %collective-permute-start = (f32[10,16,256]{2,1,0:T(8,128)S(1)}, f32[10,16,256]{2,1,0:T(8,128)S(1)}, u32[]{:S(2)}, u32[]{:S(2)}) collective-permute-start(f32[10,16,256]{2,1,0:T(8,128)S(1)} %get-tuple-element.16), channel_id=1, source_target_pairs={{0,8},{8,0},{16,24},{24,16},{32,40},{40,32},{48,56},{56,48},{64,72... | collective-permute-start | bytes 491528 | tf_op jit(solution)/shard_map/ppermute | solution.py:20
  2.5 19.0 %collective-permute-start.1 = (f32[10,16,256]{2,1,0:T(8,128)S(1)}, f32[10,16,256]{2,1,0:T(8,128)S(1)}, u32[]{:S(2)}, u32[]{:S(2)}) collective-permute-start(f32[10,16,256]{2,1,0:T(8,128)S(1)} %get-tuple-element.17), channel_id=1, source_target_pairs={{8,16},{16,8},{24,32},{32,24},{40,48},{48,40},{56,64},{64,56},{72,... | collective-permute-start | bytes 491528 | tf_op jit(solution)/shard_map/ppermute | solution.py:20
  22.4 15.6 %collective-permute-start.2 = (f32[128,256]{1,0:T(8,128)S(1)}, f32[128,256]{1,0:T(8,128)S(1)}, u32[]{:S(2)}, u32[]{:S(2)}) collective-permute-start(f32[128,256]{1,0:T(8,128)S(1)} %get-tuple-element.20.sent), channel_id=1, source_target_pairs={{1,2},{2,1},{3,4},{4,3},{5,6},{6,5},{9,10},{10,9},{11,12},{12,11},... | collective-permute-start | bytes 393224 | tf_op jit(solution)/shard_map/ppermute | solution.py:20
  30.9 5.0 %collective-permute-start.3 = (f32[120,256]{1,0:T(8,128)S(1)}, f32[120,256]{1,0:T(8,128)S(1)}, u32[]{:S(2)}, u32[]{:S(2)}) collective-permute-start(f32[120,256]{1,0:T(8,128)S(1)} %get-tuple-element.21.sent), channel_id=1, source_target_pairs={{0,1},{1,0},{2,3},{3,2},{4,5},{5,4},{6,7},{7,6},{8,9},{9,8},{10,11... | collective-permute-start | bytes 368648 | tf_op jit(solution)/shard_map/ppermute | solution.py:20

commit v6 on v5

--- a/solution.py
+++ b/solution.py
@@ -106,49 +106,56 @@
     return a, b, g * upper, g * lower
 
 
-def prep_kernel(place, occ, mat, shear_t, lame_t, dens_t, now, prev, se, so, masses, consts, held_now, held_prev, sems, *, factor):
-    top_first = place[0] % 2 == 0
+def parity(axis):
+    return lax.axis_index(axis) % 2 == 0
+
+
+def slice_kernel(now, prev, se, so, sems):
+    even = parity("story")
     copies = []
-    for k in range(2):
-        top = jnp.logical_xor(top_first, k == 1)
-        copies.append(pltpu.make_async_copy(now.at[:, pl.ds(jnp.where(top, 14, 0), 2)], held_now.at[k], sems.at[2 * k]))
-        copies.append(pltpu.make_async_copy(prev.at[:, pl.ds(jnp.where(top, 15, 0), 1)], held_prev.at[k], sems.at[2 * k + 1]))
+    for k, out in enumerate((se, so)):
+        top = jnp.logical_xor(even, k == 1)
+        near, far = jnp.where(top, 15, 0), jnp.where(top, 14, 1)
+        for j, (source, z) in enumerate(((now, near), (now, far), (prev, near))):
+            copies.append(pltpu.make_async_copy(source.at[:, z], out.at[pl.ds(3 * j, 3)], sems.at[3 * k + j]))
     for copy in copies:
         copy.start()
-    block = lax.broadcasted_iota(jnp.int32, (1, WIDE), 1) // BLOCK
-    zero = jnp.zeros((1, WIDE), F32)
-    occupied, shear, lame, dens = zero, zero, zero, zero
-    for j in range(BLOCK):
-        at = block == j
-        which = mat[j]
-        occupied = jnp.where(at, occ[j].astype(F32), occupied)
-        shear = jnp.where(at, shear_t[which], shear)
-        lame = jnp.where(at, lame_t[which], lame)
-        dens = jnp.where(at, dens_t[which], dens)
-    scale = occupied * (0.1 / dens)
-    own = [scale * shear * (1.0 / 12.0), scale * (lame + shear) * (1.0 / 72.0), scale * factor, dens * occupied, occupied]
-    for k, row in enumerate(own):
-        consts[k : k + 1, :] = row
-    consts[5:8, :] = jnp.zeros((3, WIDE), F32)
-    masses[...] = jnp.broadcast_to(own[3], masses.shape)
     for copy in copies:
         copy.wait()
-    for k, out in enumerate((se, so)):
-        top = jnp.logical_xor(top_first, k == 1)
-        for c in range(3):
-            first, second = held_now[k, c, 0] * occupied, held_now[k, c, 1] * occupied
-            out[c] = jnp.where(top, second, first)
-            out[3 + c] = jnp.where(top, first, second)
-            out[6 + c] = held_prev[k, c, 0] * occupied
-        out[9, 0:8] = consts[...]
-
-
-def ghost_of(place, se, so):
-    even_story = place[0] % 2 == 0
-
-    def ghost(over, *where):
-        take = even_story if over else jnp.logical_not(even_story)
-        return jnp.where(take, se[where], so[where])
+
+
+def block_kernel(occ, mat, shear_t, lame_t, dens_t, out, held, *, factor):
+    segment = lax.broadcasted_iota(jnp.int32, (8, 128), 1) // BLOCK
+
+    def repeat(ref):
+        held[...] = jnp.zeros((8, 128), F32)
+        held[0:1, 0:BLOCK] = ref[...].astype(F32)
+        once = held[...]
+        return once + sum(pltpu.roll(once, BLOCK * k, 1) for k in range(1, 5))
+
+    occupied, which = repeat(occ), repeat(mat)
+    found = []
+    for table in (shear_t, lame_t, dens_t):
+        value = jnp.zeros((8, 128), F32)
+        for k in range(table.shape[1]):
+            value = jnp.where(which == k, table[0:1, k : k + 1], value)
+        found.append(value)
+    shear, lame, dens = found
+    scale = occupied * (0.1 / dens)
+    parts = (scale * shear * (1.0 / 12.0), scale * (lame + shear) * (1.0 / 72.0), scale * factor, dens * occupied, occupied)
+    row = jnp.zeros((8, 128), F32)
+    for k, part in enumerate(parts):
+        row = jnp.where(segment == k, part, row)
+    out[...] = jnp.broadcast_to(row[0:1], out.shape)
+
+
+def ghost_of(se, so, consts):
+    even = parity("story")
+
+    def ghost(over, plane, *where):
+        take = even if over else jnp.logical_not(even)
+        row = 9 if over else 14
+        return jnp.where(take, se[(plane,) + where], so[(plane,) + where]) * consts[row : row + 1, :]
 
     return ghost
 
@@ -184,23 +191,35 @@
         out[3 * PAD + 16 * c : 3 * PAD + 16 * c + 16, :] = first[k][4:20]
         out[c * PAD : c * PAD + 1, :] = first[k][3:4]
         out[c * PAD + 23 : c * PAD + 24, :] = first[k][20:21]
-    for k in range(2):
-        row = 1 if k == 0 else 22
-        out[row : row + 1, :] = consts[k : k + 1, :]
-        out[PAD + row : PAD + row + 1, :] = ghost(True, 9, pl.ds(k, 1), slice(None))
-        out[2 * PAD + row : 2 * PAD + row + 1, :] = ghost(False, 9, pl.ds(k, 1), slice(None))
-
-
-def pack_po_kernel(place, consts, se, so, masses, now, prev, po, coef, far_rows, prev_rows):
-    ghost = ghost_of(place, se, so)
-    step = lax.broadcasted_iota(jnp.int32, masses.shape, 0)
-    carried = 16.0 * jnp.sum(jnp.where(step > place[0], masses[...], 0.0), 0, keepdims=True)
-    own = [consts[k : k + 1, :] for k in range(4)]
-    over = [ghost(True, 9, pl.ds(k, 1), slice(None)) for k in range(4)]
-    under = [ghost(False, 9, pl.ds(k, 1), slice(None)) for k in range(4)]
-    for k, rows in enumerate(coefficients(own, over, under, carried)):
-        coef[k] = rows
-    fill(place[1] % 2 == 1, ghost, consts, coef, now, prev, po, far_rows, prev_rows)
+    for k, row in enumerate((1, 22)):
+        for j in range(3):
+            out[j * PAD + row : j * PAD + row + 1, :] = consts[5 * j + k : 5 * j + k + 1, :]
+
+
+def pack_po_kernel(blocks, se, so, now, prev, po, coef, consts, far_rows, prev_rows):
+    place = lax.axis_index("story")
+    step = lax.broadcasted_iota(jnp.int32, blocks.shape, 0)
+    rows = [jnp.sum(jnp.where(step == place + k, blocks[...], 0.0), 0, keepdims=True) for k in (0, 1, -1)]
+    rows.append(16.0 * jnp.sum(jnp.where(step > place, blocks[...], 0.0), 0, keepdims=True))
+    stacked = jnp.concatenate(rows + [jnp.zeros((4, 128), F32)], 0)
+    lane = lax.broadcasted_iota(jnp.int32, (8, 128), 1) // BLOCK
+
+    def spread(k):
+        halves = [jnp.take_along_axis(stacked, lane + (BLOCK * k + 8 * h), 1, mode="promise_in_bounds") for h in (0, 1)]
+        return jnp.concatenate(halves, 1)
+
+    sets = [[], [], []]
+    for k in range(5):
+        wide = spread(k)
+        for j in range(3):
+            sets[j].append(wide[j : j + 1])
+            consts[5 * j + k : 5 * j + k + 1, :] = wide[j : j + 1]
+        if k == 3:
+            carried = wide[3:4]
+    consts[15:16, :] = carried
+    for k, value in enumerate(coefficients(sets[0], sets[1], sets[2], carried)):
+        coef[k] = value
+    fill(jnp.logical_not(parity("plan")), ghost_of(se, so, consts), consts, coef, now, prev, po, far_rows, prev_rows)
 
 
 def advance(below, here, above, before, coefs, sign):
@@ -218,12 +237,13 @@
     return 2.0 * here - before + a * lap + b * coup - geometric
 
 
-def crosses(place, plans):
-    return jnp.logical_or(place[1] == plans // 2 - 1, place[1] == plans // 2)
-
-
-def both_steps(place, consts, coef, se, so, now, prev, out, u0, u1, before):
-    ghost = ghost_of(place, se, so)
+def crosses(plans):
+    place = lax.axis_index("plan")
+    return jnp.logical_or(place == plans // 2 - 1, place == plans // 2)
+
+
+def both_steps(consts, coef, se, so, now, prev, out, u0, u1, before):
+    ghost = ghost_of(se, so, consts)
     occupied = jnp.broadcast_to(consts[4:5, :], (16, WIDE))
     for c in range(3):
         u0[c, 0] = ghost(False, 3 + c)
@@ -255,18 +275,18 @@
         one(u1, lambda c, i: u0[c, i + 2], out, i, 4)
 
 
-def early_kernel(place, consts, coef, se, so, now, prev, pe, out, far_rows, prev_rows, u0, u1, before, *, plans):
-    fill(place[1] % 2 == 0, ghost_of(place, se, so), consts, coef, now, prev, pe, far_rows, prev_rows)
-
-    @pl.when(jnp.logical_not(crosses(place, plans)))
-    def _():
-        both_steps(place, consts, coef, se, so, now, prev, out, u0, u1, before)
-
-
-def late_kernel(place, consts, coef, se, so, now, prev, out, u0, u1, before, *, plans):
-    @pl.when(crosses(place, plans))
-    def _():
-        both_steps(place, consts, coef, se, so, now, prev, out, u0, u1, before)
+def early_kernel(consts, coef, se, so, now, prev, pe, out, far_rows, prev_rows, u0, u1, before, *, plans):
+    fill(parity("plan"), ghost_of(se, so, consts), consts, coef, now, prev, pe, far_rows, prev_rows)
+
+    @pl.when(jnp.logical_not(crosses(plans)))
+    def _():
+        both_steps(consts, coef, se, so, now, prev, out, u0, u1, before)
+
+
+def late_kernel(consts, coef, se, so, now, prev, out, u0, u1, before, *, plans):
+    @pl.when(crosses(plans))
+    def _():
+        both_steps(consts, coef, se, so, now, prev, out, u0, u1, before)
 
 
 def one_side(coef, sent, got, held, sign):
@@ -322,9 +342,9 @@
         put(0, 1, 0)
 
 
-def tail_pe_kernel(place, coef, sent, got, early, late, out, rest, work, held, sems, *, plans):
-    right = place[1] % 2 == 0
-    for inner, use in ((late, crosses(place, plans)), (early, jnp.logical_not(crosses(place, plans)))):
+def tail_pe_kernel(coef, sent, got, early, late, out, rest, work, held, sems, *, plans):
+    right = parity("plan")
+    for inner, use in ((late, crosses(plans)), (early, jnp.logical_not(crosses(plans)))):
 
         @pl.when(jnp.logical_and(use, right))
         def _(inner=inner):
@@ -340,15 +360,14 @@
     write_half(right, near, far, work, out, sems)
 
 
-def tail_po_kernel(place, coef, sent, got, rest, half, out, work, held, sems):
-    right = place[1] % 2 == 1
+def tail_po_kernel(coef, sent, got, rest, half, out, work, held, sems):
+    right = jnp.logical_not(parity("plan"))
     work[...] = rest[...]
     near, far = one_side(coef, sent, got, held, jnp.where(right, 1.0, -1.0))
     write_half(right, near, far, work, out, sems)
 
 
 VM = pl.BlockSpec(memory_space=pltpu.VMEM)
-SM = pl.BlockSpec(memory_space=pltpu.SMEM)
 HB = pl.BlockSpec(memory_space=pltpu.HBM)
 
 
@@ -372,28 +391,23 @@
 def local(u_now, u_prev, occupancy, materials, shear_table, lame_table, density_table):
     height = u_now.shape[1] * lax.axis_size("story")
     stories, plans = lax.axis_size("story"), lax.axis_size("plan")
-    place = jnp.stack([lax.axis_index("story"), lax.axis_index("plan")]).astype(jnp.int32)
-    face, table = shape(10, 16, WIDE), shape(4, PAD, WIDE)
+    face, table = shape(9, 16, WIDE), shape(4, PAD, WIDE)
     rows = 3 * PAD + 48
     planes = [pltpu.VMEM((3 * PAD, WIDE), F32)] * 2
-    se, so, masses, consts = call(
-        functools.partial(prep_kernel, factor=0.8 / height),
-        [face, face, shape(stories, WIDE), shape(8, WIDE)],
-        [SM] * 6 + [HB] * 2,
-        [
-            pltpu.VMEM((2, 3, 2, 16, WIDE), F32),
-            pltpu.VMEM((2, 3, 1, 16, WIDE), F32),
-            pltpu.SemaphoreType.DMA((4,)),
-        ],
-        moved=1 << 20,
-        grant=53.2,
-    )(place, occupancy.reshape(-1), materials.reshape(-1), shear_table, lame_table, density_table, u_now, u_prev)
+    se, so = call(slice_kernel, [face, face], [HB] * 2, [pltpu.SemaphoreType.DMA((6,))], moved=1 << 20, grant=53.2)(u_now, u_prev)
     so_got = swap(so, "story", 1)
     se_got = swap(se, "story", 0)
-    masses = lax.all_to_all(masses, "story", 0, 0, tiled=True)
+    small = [occupancy, materials, shear_table, lame_table, density_table]
+    (blocks,) = call(
+        functools.partial(block_kernel, factor=0.8 / height),
+        [shape(stories, 128)],
+        [VM] * 5,
+        [pltpu.VMEM((8, 128), F32)],
+    )(*(v.reshape(1, -1) for v in small))
+    blocks = lax.all_to_all(blocks, "story", 0, 0, tiled=True)
     cells = u_now.shape
-    po, coef = call(pack_po_kernel, [shape(rows + 8, WIDE), table], [SM] + [VM] * 6, planes, moved=1 << 20)(
-        place, consts, se_got, so_got, masses, u_now, u_prev
+    po, coef, consts = call(pack_po_kernel, [shape(rows + 8, WIDE), table, shape(16, WIDE)], [VM] * 5, planes, moved=1 << 20)(
+        blocks, se_got, so_got, u_now, u_prev
     )
     po_got = swap(po, "plan", 1)
     levels = [
@@ -401,33 +415,33 @@
         pltpu.VMEM((3, 18, 16, WIDE), F32),
         pltpu.VMEM((3, 18, 16, WIDE), F32),
     ]
-    own = (place, consts, coef, se_got, so_got, u_now, u_prev)
+    own = (consts, coef, se_got, so_got, u_now, u_prev)
     pe, early = call(
         functools.partial(early_kernel, plans=plans),
         [shape(rows, WIDE), shape(*cells)],
-        [SM] + [VM] * 6,
+        [VM] * 6,
         planes + levels,
         flops=60_000_000,
         moved=4 << 20,
     )(*own)
     pe_got = swap(pe, "plan", 0)
     (late,) = call(
-        functools.partial(late_kernel, plans=plans), [shape(*cells)], [SM] + [VM] * 6, levels, flops=60_000_000, moved=4 << 20
+        functools.partial(late_kernel, plans=plans), [shape(*cells)], [VM] * 6, levels, flops=60_000_000, moved=4 << 20
     )(*own)
     half = shape(3, 16, 8, WIDE)
     work = [pltpu.VMEM((3, 16, 8, WIDE), F32), pltpu.VMEM((3 * PAD, WIDE), F32), pltpu.SemaphoreType.DMA((3,))]
     out, rest = call(
         functools.partial(tail_pe_kernel, plans=plans),
         [shape(*cells), half],
-        [SM] + [VM] * 5,
+        [VM] * 5,
         work,
         flops=5_000_000,
         moved=2 << 20,
         places=[HB, VM],
-    )(place, coef, pe, pe_got, early, late)
+    )(coef, pe, pe_got, early, late)
     (out,) = call(
-        tail_po_kernel, [shape(*cells)], [SM] + [VM] * 4 + [HB], work, flops=5_000_000, moved=2 << 20, places=[HB], aliases={5: 0}
-    )(place, coef, po, po_got, rest, out)
+        tail_po_kernel, [shape(*cells)], [VM] * 4 + [HB], work, flops=5_000_000, moved=2 << 20, places=[HB], aliases={4: 0}
+    )(coef, po, po_got, rest, out)
     return out
 
 

time: 40.2 us -> 37.7 us (0.938)
  the two profiles are of different devices: /device:TPU:24 before, /device:TPU:57 now
where the time goes in v6:
time: 37.7 us; the launch traced here: 37.5 us
  blocking collectives  13.4 us (36%)
  starting transfers between devices  11.7 us (31%)
  Pallas kernels  8.82 us (23%)
  waiting for transfers between devices  2.82 us (7%)
  local copies, waits for them, and re-layouts  0.66 us (2%)
    all_to_all x1, blocking collectives, local(): blocks = lax.all_to_all(blocks, 'story', 0, 0, tiled=True)  13.4 us
    ppermute x4, starting transfers between devices, swap(): return lax.ppermute(values, axis, pairs)  11.7 us
    pallas_call x1, Pallas kernels, local(): call(functools.partial(late_kernel, plans=plans), [shape(*cells)], [VM] *...  3.95 us
    ppermute x4, waiting for transfers between devices, swap(): return lax.ppermute(values, axis, pairs)  2.82 us
    pallas_call x1, Pallas kernels, local(): call(functools.partial(tail_pe_kernel, plans=plans), [shape(*cells), half...  1.5 us
    pallas_call x1, Pallas kernels, local(): call(tail_po_kernel, [shape(*cells)], [VM] * 4 + [HB], work, flops=500000...  1.42 us
    pallas_call x1, Pallas kernels, local(): call(slice_kernel, [face, face], [HB] * 2, [pltpu.SemaphoreType.DMA((6,))...  1.1 us
  transfers between devices with their start and end apart: 4, of which 1 were waited for; matrix products, arithmetic and copies ran while one was open for 0% of the time, Pallas kernels for 16%

profile of v6, /device:TPU:57, one launch (start us, length us, event | category | flops | bytes accessed | tf_op | source)
XLA Modules:
  0.0 37.5 jit_solution(14962536309786125653)
XLA Ops:
  0.0 0.0 copy-start
  0.0 0.0 copy-start.1
  0.0 0.0 copy-start.5
  0.0 0.0 copy-start.6
  0.0 1.1 %shard_map.74 = (f32[9,16,256]{2,1,0:T(8,128)S(1)}, f32[9,16,256]{2,1,0:T(8,128)S(1)}) custom-call(f32[3,16,16,256]{3,2,1,0:T(8,128)} %now.7, f32[3,16,16,256]{3,2,1,0:T(8,128)} %prev.7), custom_call_target="tpu_custom_call" | custom-call | bytes 1048576 | tf_op jit(solution)/shard_map/pallas_call | solution.py:397
  1.1 0.8 %collective-permute-start = (f32[9,16,256]{2,1,0:T(8,128)S(1)}, f32[9,16,256]{2,1,0:T(8,128)S(1)}, u32[]{:S(2)}, u32[]{:S(2)}) collective-permute-start(f32[9,16,256]{2,1,0:T(8,128)S(1)} %get-tuple-element.14), channel_id=1, source_target_pairs={{0,8},{8,0},{16,24},{24,16},{32,40},{40,32},{48,56},{56,48},{64,72... | collective-permute-start | bytes 442376 | tf_op jit(solution)/shard_map/ppermute | solution.py:20
  1.9 3.4 %collective-permute-start.1 = (f32[9,16,256]{2,1,0:T(8,128)S(1)}, f32[9,16,256]{2,1,0:T(8,128)S(1)}, u32[]{:S(2)}, u32[]{:S(2)}) collective-permute-start(f32[9,16,256]{2,1,0:T(8,128)S(1)} %get-tuple-element.15), channel_id=1, source_target_pairs={{8,16},{16,8},{24,32},{32,24},{40,48},{48,40},{56,64},{64,56},{72,... | collective-permute-start | bytes 442376 | tf_op jit(solution)/shard_map/ppermute | solution.py:20
  5.3 0.0 copy-start.2
  5.4 0.0 copy-start.3
  5.4 0.0 copy-start.4
  5.4 0.0 copy-done.5
  5.4 0.0 copy-done.6
  5.4 0.6 %copy-done.2 = s32[1,1,16]{2,1,0:T(1,128)S(1)} copy-done((s32[1,1,16]{2,1,0:T(1,128)S(1)}, s32[1,1,16]{2,1,0:T(1,128)}, u32[]{:S(2)}) %copy-start.2) | copy-done | bytes 88
  6.0 0.0 copy-done.3
  6.0 0.0 copy-done.4
  6.0 0.1 shard_map.73
  6.2 13.4 %all_to_all.11 = f32[32,1,128]{2,1,0:T(1,128)S(1)} all-to-all(f32[32,1,128]{2,1,0:T(1,128)S(1)} %bitcast.10), channel_id=1, replica_groups=mesh['story'=32,'plan'=8] {'story'}, dimensions={0} | all-to-all | bytes 32768 | tf_op jit(solution)/shard_map/all_to_all | solution.py:407
  19.5 0.0 collective-permute-done.se
  19.5 0.0 collective-permute-done.1.so
  19.5 0.0 copy-done
  19.6 0.0 copy-done.1
  19.6 0.4 %shard_map.75 = (f32[128,256]{1,0:T(8,128)S(1)}, f32[4,24,256]{2,1,0:T(8,128)S(1)}, f32[16,256]{1,0:T(8,128)S(1)}) custom-call(f32[32,128]{1,0:T(8,128)S(1)} %bitcast.9, f32[9,16,256]{2,1,0:T(8,128)S(1)} %collective-permute-done.se, f32[9,16,256]{2,1,0:T(8,128)S(1)} %collective-permute-done.1.so, f32[3,16,16,256]{3,2,1,0:T(8,128)S(1)} %copy-done, ...), custom_call_target="tpu_custom_call" | custom-call | bytes 1048576 | tf_op jit(solution)/shard_map/pallas_call | solution.py:409
  20.0 7.4 %collective-permute-start.2 = (f32[128,256]{1,0:T(8,128)S(1)}, f32[128,256]{1,0:T(8,128)S(1)}, u32[]{:S(2)}, u32[]{:S(2)}) collective-permute-start(f32[128,256]{1,0:T(8,128)S(1)} %get-tuple-element.17.sent), channel_id=1, source_target_pairs={{1,2},{2,1},{3,4},{4,3},{5,6},{6,5},{9,10},{10,9},{11,12},{12,11},... | collective-permute-start | bytes 393224 | tf_op jit(solution)/shard_map/ppermute | solution.py:20
  27.4 0.3 shard_map.76
  27.7 0.1 collective-permute-start.3
  27.8 3.9 %shard_map.77.late = f32[3,16,16,256]{3,2,1,0:T(8,128)S(1)} custom-call(f32[16,256]{1,0:T(8,128)S(1)} %get-tuple-element.18.consts, f32[4,24,256]{2,1,0:T(8,128)S(1)} %get-tuple-element.16.coef, f32[9,16,256]{2,1,0:T(8,128)S(1)} %collective-permute-done.se, f32[9,16,256]{2,1,0:T(8,128)S(1)} %collective-permute-done.1.so, f32[3,16,16,256]{3,2,1,0:T(8,128)S(1)} %copy-done, ...), custom_call_target="tpu_custom_call" | custom-call | flops 60000000 | bytes 4194304 | tf_op jit(solution)/shard_map/pallas_call | solution.py:428
  31.7 0.0 collective-permute-done.3.got
  31.8 1.5 %shard_map.78 = (f32[3,16,16,256]{3,2,1,0:T(8,128)}, f32[3,16,8,256]{3,2,1,0:T(8,128)S(1)}) custom-call(f32[4,24,256]{2,1,0:T(8,128)S(1)} %get-tuple-element.16.coef, f32[120,256]{1,0:T(8,128)S(1)} %get-tuple-element.19.sent, f32[120,256]{1,0:T(8,128)S(1)} %collective-permute-done.3.got, f32[3,16,16,256]{3,2,1,0:T(8,128)S(1)} %get-tuple-element.20.early, ...), custom_call_target="tpu_custom_call" | custom-call | flops 5000000 | bytes 2097152 | tf_op jit(solution)/shard_map/pallas_call | solution.py:433
  33.3 2.8 %collective-permute-done.2.got = f32[128,256]{1,0:T(8,128)S(1)} collective-permute-done((f32[128,256]{1,0:T(8,128)S(1)}, f32[128,256]{1,0:T(8,128)S(1)}, u32[]{:S(2)}, u32[]{:S(2)}) %collective-permute-start.2) | collective-permute-done | bytes 131104 | tf_op jit(solution)/shard_map/ppermute | solution.py:20
  36.1 1.4 %shard_map.79 = f32[3,16,16,256]{3,2,1,0:T(8,128)} custom-call(f32[4,24,256]{2,1,0:T(8,128)S(1)} %get-tuple-element.16.coef, f32[128,256]{1,0:T(8,128)S(1)} %get-tuple-element.17.sent, f32[128,256]{1,0:T(8,128)S(1)} %collective-permute-done.2.got, f32[3,16,8,256]{3,2,1,0:T(8,128)S(1)} %get-tuple-element.21.rest, ...), custom_call_target="tpu_custom_call", output_to_operand_aliasing={{}: (4, {})} | custom-call | flops 5000000 | bytes 2097152 | tf_op jit(solution)/shard_map/pallas_call | solution.py:442
Async XLA Ops:
  0.0 19.5 %copy-start = (f32[3,16,16,256]{3,2,1,0:T(8,128)S(1)}, f32[3,16,16,256]{3,2,1,0:T(8,128)}, u32[]{:S(2)}) copy-start(f32[3,16,16,256]{3,2,1,0:T(8,128)} %now.7) | copy-start | bytes 2359300
  0.0 19.6 %copy-start.1 = (f32[3,16,16,256]{3,2,1,0:T(8,128)S(1)}, f32[3,16,16,256]{3,2,1,0:T(8,128)}, u32[]{:S(2)}) copy-start(f32[3,16,16,256]{3,2,1,0:T(8,128)} %prev.7) | copy-start | bytes 2359300
  0.0 5.4 %copy-start.5 = (f32[8]{0:T(128)S(1)}, f32[8]{0:T(128)}, u32[]{:S(2)}) copy-start(f32[8]{0:T(128)} %param.12) | copy-start | bytes 100
  0.0 5.4 %copy-start.6 = (f32[8]{0:T(128)S(1)}, f32[8]{0:T(128)}, u32[]{:S(2)}) copy-start(f32[8]{0:T(128)} %param.13) | copy-start | bytes 100
  1.1 18.4 %collective-permute-start = (f32[9,16,256]{2,1,0:T(8,128)S(1)}, f32[9,16,256]{2,1,0:T(8,128)S(1)}, u32[]{:S(2)}, u32[]{:S(2)}) collective-permute-start(f32[9,16,256]{2,1,0:T(8,128)S(1)} %get-tuple-element.14), channel_id=1, source_target_pairs={{0,8},{8,0},{16,24},{24,16},{32,40},{40,32},{48,56},{56,48},{64,72... | collective-permute-start | bytes 442376 | tf_op jit(solution)/shard_map/ppermute | solution.py:20
  1.9 17.7 %collective-permute-start.1 = (f32[9,16,256]{2,1,0:T(8,128)S(1)}, f32[9,16,256]{2,1,0:T(8,128)S(1)}, u32[]{:S(2)}, u32[]{:S(2)}) collective-permute-start(f32[9,16,256]{2,1,0:T(8,128)S(1)} %get-tuple-element.15), channel_id=1, source_target_pairs={{8,16},{16,8},{24,32},{32,24},{40,48},{48,40},{56,64},{64,56},{72,... | collective-permute-start | bytes 442376 | tf_op jit(solution)/shard_map/ppermute | solution.py:20
  5.3 0.7 %copy-start.2 = (s32[1,1,16]{2,1,0:T(1,128)S(1)}, s32[1,1,16]{2,1,0:T(1,128)}, u32[]{:S(2)}) copy-start(s32[1,1,16]{2,1,0:T(1,128)} %param.9) | copy-start | bytes 196
  5.4 0.7 %copy-start.3 = (s32[1,1,16]{2,1,0:T(1,128)S(1)}, s32[1,1,16]{2,1,0:T(1,128)}, u32[]{:S(2)}) copy-start(s32[1,1,16]{2,1,0:T(1,128)} %param.10) | copy-start | bytes 196
  5.4 0.7 %copy-start.4 = (f32[8]{0:T(128)S(1)}, f32[8]{0:T(128)}, u32[]{:S(2)}) copy-start(f32[8]{0:T(128)} %param.11) | copy-start | bytes 100
  20.0 16.1 %collective-permute-start.2 = (f32[128,256]{1,0:T(8,128)S(1)}, f32[128,256]{1,0:T(8,128)S(1)}, u32[]{:S(2)}, u32[]{:S(2)}) collective-permute-start(f32[128,256]{1,0:T(8,128)S(1)} %get-tuple-element.17.sent), channel_id=1, source_target_pairs={{1,2},{2,1},{3,4},{4,3},{5,6},{6,5},{9,10},{10,9},{11,12},{12,11},... | collective-permute-start | bytes 393224 | tf_op jit(solution)/shard_map/ppermute | solution.py:20
  27.7 4.1 %collective-permute-start.3 = (f32[120,256]{1,0:T(8,128)S(1)}, f32[120,256]{1,0:T(8,128)S(1)}, u32[]{:S(2)}, u32[]{:S(2)}) collective-permute-start(f32[120,256]{1,0:T(8,128)S(1)} %get-tuple-element.19.sent), channel_id=1, source_target_pairs={{0,1},{1,0},{2,3},{3,2},{4,5},{5,4},{6,7},{7,6},{8,9},{9,8},{10,11... | collective-permute-start | bytes 368648 | tf_op jit(solution)/shard_map/ppermute | solution.py:20

commit v7 on v6

--- a/solution.py
+++ b/solution.py
@@ -110,21 +110,21 @@
     return lax.axis_index(axis) % 2 == 0
 
 
-def slice_kernel(now, prev, se, so, sems):
+def slice_kernel(now, prev, occ_h, mat_h, shear_h, lame_h, dens_h, so, se, blocks, occ, mat, shear_t, lame_t, dens_t, held, sems, *, factor):
     even = parity("story")
+    smalls = []
+    for k, (source, target) in enumerate(((occ_h, occ), (mat_h, mat), (shear_h, shear_t), (lame_h, lame_t), (dens_h, dens_t))):
+        smalls.append(pltpu.make_async_copy(source, target, sems.at[6 + k]))
     copies = []
     for k, out in enumerate((se, so)):
         top = jnp.logical_xor(even, k == 1)
         near, far = jnp.where(top, 15, 0), jnp.where(top, 14, 1)
         for j, (source, z) in enumerate(((now, near), (now, far), (prev, near))):
             copies.append(pltpu.make_async_copy(source.at[:, z], out.at[pl.ds(3 * j, 3)], sems.at[3 * k + j]))
-    for copy in copies:
+    for copy in smalls + copies:
         copy.start()
-    for copy in copies:
+    for copy in smalls:
         copy.wait()
-
-
-def block_kernel(occ, mat, shear_t, lame_t, dens_t, out, held, *, factor):
     segment = lax.broadcasted_iota(jnp.int32, (8, 128), 1) // BLOCK
 
     def repeat(ref):
@@ -146,7 +146,9 @@
     row = jnp.zeros((8, 128), F32)
     for k, part in enumerate(parts):
         row = jnp.where(segment == k, part, row)
-    out[...] = jnp.broadcast_to(row[0:1], out.shape)
+    blocks[...] = jnp.broadcast_to(row[0:1], blocks.shape)
+    for copy in copies:
+        copy.wait()
 
 
 def ghost_of(se, so, consts):
@@ -394,16 +396,16 @@
     face, table = shape(9, 16, WIDE), shape(4, PAD, WIDE)
     rows = 3 * PAD + 48
     planes = [pltpu.VMEM((3 * PAD, WIDE), F32)] * 2
-    se, so = call(slice_kernel, [face, face], [HB] * 2, [pltpu.SemaphoreType.DMA((6,))], moved=1 << 20, grant=53.2)(u_now, u_prev)
+    small = [v.reshape(1, -1) for v in (occupancy, materials, shear_table, lame_table, density_table)]
+    so, se, blocks = call(
+        functools.partial(slice_kernel, factor=0.8 / height),
+        [shape(10, 16, WIDE), face, shape(stories, 128)],
+        [HB] * 7,
+        [pltpu.VMEM(v.shape, v.dtype) for v in small] + [pltpu.VMEM((8, 128), F32), pltpu.SemaphoreType.DMA((11,))],
+        moved=1 << 20,
+    )(*(pltpu.with_memory_space_constraint(v, pltpu.HBM) for v in [u_now, u_prev] + small))
     so_got = swap(so, "story", 1)
     se_got = swap(se, "story", 0)
-    small = [occupancy, materials, shear_table, lame_table, density_table]
-    (blocks,) = call(
-        functools.partial(block_kernel, factor=0.8 / height),
-        [shape(stories, 128)],
-        [VM] * 5,
-        [pltpu.VMEM((8, 128), F32)],
-    )(*(v.reshape(1, -1) for v in small))
     blocks = lax.all_to_all(blocks, "story", 0, 0, tiled=True)
     cells = u_now.shape
     po, coef, consts = call(pack_po_kernel, [shape(rows + 8, WIDE), table, shape(16, WIDE)], [VM] * 5, planes, moved=1 << 20)(

time: 37.7 us -> 37.1 us (0.984)
  local copies, waits for them, and re-layouts: 0.66 us -> 0.01 us
    unnamed x14 -> x4, local copies, waits for them, and re-layouts: 0.66 us -> 0.01 us
    pallas_call x2 -> x1, Pallas kernels: 1.22 us -> 1.21 us  [local(): call(functools.partial(slice_kernel, factor=0.8 / height), [shape(10, 16,...]
where the time goes in v7:
time: 37.1 us; the launch traced here: 36.8 us
  blocking collectives  13.4 us (36%)
  starting transfers between devices  12 us (32%)
  Pallas kernels  8.81 us (24%)
  waiting for transfers between devices  2.46 us (7%)
    all_to_all x1, blocking collectives, local(): blocks = lax.all_to_all(blocks, 'story', 0, 0, tiled=True)  13.4 us
    ppermute x4, starting transfers between devices, swap(): return lax.ppermute(values, axis, pairs)  12 us
    pallas_call x1, Pallas kernels, local(): call(functools.partial(late_kernel, plans=plans), [shape(*cells)], [VM] *...  3.95 us
    ppermute x4, waiting for transfers between devices, swap(): return lax.ppermute(values, axis, pairs)  2.46 us
    pallas_call x1, Pallas kernels, local(): call(functools.partial(tail_pe_kernel, plans=plans), [shape(*cells), half...  1.5 us
    pallas_call x1, Pallas kernels, local(): call(tail_po_kernel, [shape(*cells)], [VM] * 4 + [HB], work, flops=500000...  1.43 us
    pallas_call x1, Pallas kernels, local(): call(functools.partial(slice_kernel, factor=0.8 / height), [shape(10, 16,...  1.21 us
  transfers between devices with their start and end apart: 4, of which 1 were waited for; matrix products, arithmetic and copies ran while one was open for 0% of the time, Pallas kernels for 16%

profile of v7, /device:TPU:57, one launch (start us, length us, event | category | flops | bytes accessed | tf_op | source)
XLA Modules:
  0.0 36.8 jit_solution(10609384418762782968)
XLA Ops:
  0.0 0.0 copy-start
  0.0 0.0 copy-start.1
  0.0 1.2 %shard_map.73 = (f32[10,16,256]{2,1,0:T(8,128)S(1)}, f32[9,16,256]{2,1,0:T(8,128)S(1)}, f32[32,128]{1,0:T(8,128)S(1)}) custom-call(f32[3,16,16,256]{3,2,1,0:T(8,128)} %now.7, f32[3,16,16,256]{3,2,1,0:T(8,128)} %prev.7, s32[1,16]{1,0:T(1,128)} %bitcast.11, s32[1,16]{1,0:T(1,128)} %bitcast.12, f32[1,8]{1,0:T(1,128)} %bitcast.13, f32[1,8]{1,0:T(1,128)} %bitcast.14, ...), custom_call_target="tpu_custom_call" | custom-call | bytes 1048576 | tf_op jit(solution)/shard_map/pallas_call | solution.py:400
  1.2 4.1 %collective-permute-start.1 = (f32[10,16,256]{2,1,0:T(8,128)S(1)}, f32[10,16,256]{2,1,0:T(8,128)S(1)}, u32[]{:S(2)}, u32[]{:S(2)}) collective-permute-start(f32[10,16,256]{2,1,0:T(8,128)S(1)} %get-tuple-element.17), channel_id=1, source_target_pairs={{8,16},{16,8},{24,32},{32,24},{40,48},{48,40},{56,64},{64,56},{72,... | collective-permute-start | bytes 491528 | tf_op jit(solution)/shard_map/ppermute | solution.py:20
  5.3 0.1 collective-permute-start
  5.4 13.4 %all_to_all.11 = f32[32,1,128]{2,1,0:T(1,128)S(1)} all-to-all(f32[32,1,128]{2,1,0:T(1,128)S(1)} %bitcast.10), channel_id=1, replica_groups=mesh['story'=32,'plan'=8] {'story'}, dimensions={0} | all-to-all | bytes 32768 | tf_op jit(solution)/shard_map/all_to_all | solution.py:409
  18.8 0.0 collective-permute-done.se
  18.8 0.0 collective-permute-done.1.so
  18.8 0.0 copy-done
  18.8 0.0 copy-done.1
  18.8 0.4 %shard_map.74 = (f32[128,256]{1,0:T(8,128)S(1)}, f32[4,24,256]{2,1,0:T(8,128)S(1)}, f32[16,256]{1,0:T(8,128)S(1)}) custom-call(f32[32,128]{1,0:T(8,128)S(1)} %bitcast.9, f32[9,16,256]{2,1,0:T(8,128)S(1)} %collective-permute-done.se, f32[10,16,256]{2,1,0:T(8,128)S(1)} %collective-permute-done.1.so, f32[3,16,16,256]{3,2,1,0:T(8,128)S(1)} %copy-done, ...), custom_call_target="tpu_custom_call" | custom-call | bytes 1048576 | tf_op jit(solution)/shard_map/pallas_call | solution.py:411
  19.3 7.7 %collective-permute-start.2 = (f32[128,256]{1,0:T(8,128)S(1)}, f32[128,256]{1,0:T(8,128)S(1)}, u32[]{:S(2)}, u32[]{:S(2)}) collective-permute-start(f32[128,256]{1,0:T(8,128)S(1)} %get-tuple-element.19.sent), channel_id=1, source_target_pairs={{1,2},{2,1},{3,4},{4,3},{5,6},{6,5},{9,10},{10,9},{11,12},{12,11},... | collective-permute-start | bytes 393224 | tf_op jit(solution)/shard_map/ppermute | solution.py:20
  27.0 0.3 shard_map.75
  27.3 0.1 collective-permute-start.3
  27.4 3.9 %shard_map.76.late = f32[3,16,16,256]{3,2,1,0:T(8,128)S(1)} custom-call(f32[16,256]{1,0:T(8,128)S(1)} %get-tuple-element.20.consts, f32[4,24,256]{2,1,0:T(8,128)S(1)} %get-tuple-element.18.coef, f32[9,16,256]{2,1,0:T(8,128)S(1)} %collective-permute-done.se, f32[10,16,256]{2,1,0:T(8,128)S(1)} %collective-permute-done.1.so, f32[3,16,16,256]{3,2,1,0:T(8,128)S(1)} %copy-done, ...), custom_call_target="tpu_custom_call" | custom-call | flops 60000000 | bytes 4194304 | tf_op jit(solution)/shard_map/pallas_call | solution.py:430
  31.4 0.0 collective-permute-done.3.got
  31.4 1.5 %shard_map.77 = (f32[3,16,16,256]{3,2,1,0:T(8,128)}, f32[3,16,8,256]{3,2,1,0:T(8,128)S(1)}) custom-call(f32[4,24,256]{2,1,0:T(8,128)S(1)} %get-tuple-element.18.coef, f32[120,256]{1,0:T(8,128)S(1)} %get-tuple-element.21.sent, f32[120,256]{1,0:T(8,128)S(1)} %collective-permute-done.3.got, f32[3,16,16,256]{3,2,1,0:T(8,128)S(1)} %get-tuple-element.22.early, ...), custom_call_target="tpu_custom_call" | custom-call | flops 5000000 | bytes 2097152 | tf_op jit(solution)/shard_map/pallas_call | solution.py:435
  32.9 2.4 %collective-permute-done.2.got = f32[128,256]{1,0:T(8,128)S(1)} collective-permute-done((f32[128,256]{1,0:T(8,128)S(1)}, f32[128,256]{1,0:T(8,128)S(1)}, u32[]{:S(2)}, u32[]{:S(2)}) %collective-permute-start.2) | collective-permute-done | bytes 131104 | tf_op jit(solution)/shard_map/ppermute | solution.py:20
  35.4 1.4 %shard_map.78 = f32[3,16,16,256]{3,2,1,0:T(8,128)} custom-call(f32[4,24,256]{2,1,0:T(8,128)S(1)} %get-tuple-element.18.coef, f32[128,256]{1,0:T(8,128)S(1)} %get-tuple-element.19.sent, f32[128,256]{1,0:T(8,128)S(1)} %collective-permute-done.2.got, f32[3,16,8,256]{3,2,1,0:T(8,128)S(1)} %get-tuple-element.23.rest, ...), custom_call_target="tpu_custom_call", output_to_operand_aliasing={{}: (4, {})} | custom-call | flops 5000000 | bytes 2097152 | tf_op jit(solution)/shard_map/pallas_call | solution.py:444
Async XLA Ops:
  0.0 18.8 %copy-start = (f32[3,16,16,256]{3,2,1,0:T(8,128)S(1)}, f32[3,16,16,256]{3,2,1,0:T(8,128)}, u32[]{:S(2)}) copy-start(f32[3,16,16,256]{3,2,1,0:T(8,128)} %now.7) | copy-start | bytes 2359300
  0.0 18.8 %copy-start.1 = (f32[3,16,16,256]{3,2,1,0:T(8,128)S(1)}, f32[3,16,16,256]{3,2,1,0:T(8,128)}, u32[]{:S(2)}) copy-start(f32[3,16,16,256]{3,2,1,0:T(8,128)} %prev.7) | copy-start | bytes 2359300
  1.2 17.6 %collective-permute-start.1 = (f32[10,16,256]{2,1,0:T(8,128)S(1)}, f32[10,16,256]{2,1,0:T(8,128)S(1)}, u32[]{:S(2)}, u32[]{:S(2)}) collective-permute-start(f32[10,16,256]{2,1,0:T(8,128)S(1)} %get-tuple-element.17), channel_id=1, source_target_pairs={{8,16},{16,8},{24,32},{32,24},{40,48},{48,40},{56,64},{64,56},{72,... | collective-permute-start | bytes 491528 | tf_op jit(solution)/shard_map/ppermute | solution.py:20
  5.3 13.5 %collective-permute-start = (f32[9,16,256]{2,1,0:T(8,128)S(1)}, f32[9,16,256]{2,1,0:T(8,128)S(1)}, u32[]{:S(2)}, u32[]{:S(2)}) collective-permute-start(f32[9,16,256]{2,1,0:T(8,128)S(1)} %get-tuple-element.16), channel_id=1, source_target_pairs={{0,8},{8,0},{16,24},{24,16},{32,40},{40,32},{48,56},{56,48},{64,72... | collective-permute-start | bytes 442376 | tf_op jit(solution)/shard_map/ppermute | solution.py:20
  19.3 16.1 %collective-permute-start.2 = (f32[128,256]{1,0:T(8,128)S(1)}, f32[128,256]{1,0:T(8,128)S(1)}, u32[]{:S(2)}, u32[]{:S(2)}) collective-permute-start(f32[128,256]{1,0:T(8,128)S(1)} %get-tuple-element.19.sent), channel_id=1, source_target_pairs={{1,2},{2,1},{3,4},{4,3},{5,6},{6,5},{9,10},{10,9},{11,12},{12,11},... | collective-permute-start | bytes 393224 | tf_op jit(solution)/shard_map/ppermute | solution.py:20
  27.3 4.1 %collective-permute-start.3 = (f32[120,256]{1,0:T(8,128)S(1)}, f32[120,256]{1,0:T(8,128)S(1)}, u32[]{:S(2)}, u32[]{:S(2)}) collective-permute-start(f32[120,256]{1,0:T(8,128)S(1)} %get-tuple-element.21.sent), channel_id=1, source_target_pairs={{0,1},{1,0},{2,3},{3,2},{4,5},{5,4},{6,7},{7,6},{8,9},{9,8},{10,11... | collective-permute-start | bytes 368648 | tf_op jit(solution)/shard_map/ppermute | solution.py:20

commit v8 on v7

--- a/solution.py
+++ b/solution.py
@@ -189,13 +189,16 @@
         return [ref[c * PAD : (c + 1) * PAD, :] for c in order]
 
     first = advance(planes(far_rows), planes(out), None, planes(prev_rows), [coef[k] for k in range(4)], jnp.where(right, 1.0, -1.0))
+    lane = lax.broadcasted_iota(jnp.int32, (1, WIDE), 1)
     for k, c in enumerate(order):
-        out[3 * PAD + 16 * c : 3 * PAD + 16 * c + 16, :] = first[k][4:20]
+        count = 16 if c < 2 else 15
+        out[3 * PAD + 16 * c : 3 * PAD + 16 * c + count, :] = first[k][4 : 4 + count]
         out[c * PAD : c * PAD + 1, :] = first[k][3:4]
         out[c * PAD + 23 : c * PAD + 24, :] = first[k][20:21]
+    out[2 * PAD + 22 : 2 * PAD + 23, :] = first[order.index(2)][19:20]
     for k, row in enumerate((1, 22)):
-        for j in range(3):
-            out[j * PAD + row : j * PAD + row + 1, :] = consts[5 * j + k : 5 * j + k + 1, :]
+        out[row : row + 1, :] = consts[k : k + 1, :]
+        out[PAD + row : PAD + row + 1, :] = jnp.where(lane % 2 == 0, consts[5 + k : 6 + k, :], consts[10 + k : 11 + k, :])
 
 
 def pack_po_kernel(blocks, se, so, now, prev, po, coef, consts, far_rows, prev_rows):
@@ -285,88 +288,131 @@
         both_steps(consts, coef, se, so, now, prev, out, u0, u1, before)
 
 
-def late_kernel(consts, coef, se, so, now, prev, out, u0, u1, before, *, plans):
-    @pl.when(crosses(plans))
+def planes_of(ref):
+    return [ref[c * PAD : (c + 1) * PAD, :] for c in (1, 0, 2)]
+
+
+def side_sign(right):
+    return jnp.where(right, 1.0, -1.0)
+
+
+def late_kernel(consts, coef, se, so, now, prev, early, pe_sent, po_sent, late, out, base, pe_own, po_own, u0, u1, before, sems, *, plans):
+    right = parity("plan")
+    cross = crosses(plans)
+
+    @pl.when(cross)
     def _():
-        both_steps(consts, coef, se, so, now, prev, out, u0, u1, before)
-
-
-def one_side(coef, sent, got, held, sign):
-    order = (1, 0, 2)
-
-    def planes(ref):
-        return [ref[c * PAD : (c + 1) * PAD, :] for c in order]
-
+        both_steps(consts, coef, se, so, now, prev, late, u0, u1, before)
+
+    def finish(inner, near, far, first):
+        copies = [
+            pltpu.make_async_copy(inner.at[c, :, pl.ds(first, 8), :], out.at[c, :, pl.ds(first, 8), :], sems.at[c]) for c in range(3)
+        ]
+        for copy in copies:
+            copy.start()
+        for c in range(3):
+            base[0, c] = inner[c, :, near, :]
+            base[1, c] = inner[c, :, far, :]
+        for sent, own, sign in ((pe_sent, pe_own, side_sign(right)), (po_sent, po_own, -side_sign(right))):
+            for k, v in enumerate(sum(stencil(planes_of(sent), None, None, sign), [])):
+                own[k] = v
+        for copy in copies:
+            copy.wait()
+
+    for inner, use in ((late, cross), (early, jnp.logical_not(cross))):
+
+        @pl.when(jnp.logical_and(use, right))
+        def _(inner=inner):
+            finish(inner, 0, 1, 0)
+
+        @pl.when(jnp.logical_and(use, jnp.logical_not(right)))
+        def _(inner=inner):
+            finish(inner, 15, 14, 8)
+
+
+def one_side(coef, got, held, own, sign):
     for c in range(3):
         base = c * PAD
+        count = 16 if c < 2 else 15
         held[base : base + 4, :] = got[base : base + 1, :] + jnp.zeros((4, WIDE), F32)
-        held[base + 4 : base + 20, :] = got[3 * PAD + 16 * c : 3 * PAD + 16 * c + 16, :]
+        held[base + 4 : base + 4 + count, :] = got[3 * PAD + 16 * c : 3 * PAD + 16 * c + count, :]
         held[base + 20 : base + PAD, :] = got[base + 23 : base + 24, :] + jnp.zeros((4, WIDE), F32)
+    held[2 * PAD + 19 : 2 * PAD + 20, :] = got[2 * PAD + 22 : 2 * PAD + 23, :]
     a, b, gu, gd = (coef[k] for k in range(4))
     z = lax.broadcasted_iota(jnp.int32, (PAD, WIDE), 0) - 4
+    even = lax.broadcasted_iota(jnp.int32, (8, WIDE), 1) % 2 == 0
 
     def pick(row):
-        own, over, under = (got[k * PAD + row : k * PAD + row + 1, :] for k in range(3))
-        return jnp.where(z < 0, under, jnp.where(z > 15, over, own))
+        mixed = jnp.broadcast_to(got[PAD + row : PAD + row + 1, :], (8, WIDE))
+        lower, upper = lane_shift(mixed)
+        over = jnp.where(even, mixed, lower)[0:1]
+        under = jnp.where(even, upper, mixed)[0:1]
+        return jnp.where(z < 0, under, jnp.where(z > 15, over, got[row : row + 1, :]))
 
     got_a, got_b = pick(1), pick(22)
-    lap, coup = stencil(None, None, planes(got), sign)
+    lap, coup = stencil(None, None, planes_of(got), sign)
     delta = [a * lap[k] + b * coup[k] for k in range(3)]
-    lap, coup = stencil(planes(sent), None, None, sign)
-    outer = [p + got_a * lap[k] + got_b * coup[k] for k, p in enumerate(planes(held))]
+    outer = [p + got_a * own[k] + got_b * own[3 + k] for k, p in enumerate(planes_of(held))]
     zero = jnp.zeros((PAD, WIDE), F32)
     near_more = advance(None, delta, outer, [zero] * 3, (a, b, gu, gd), sign)
     lap, coup = stencil(None, None, delta, sign)
     near, far = [None] * 3, [None] * 3
-    for k, c in enumerate(order):
+    for k, c in enumerate((1, 0, 2)):
         near[c] = near_more[k][4:20]
         far[c] = (a * lap[k] + b * coup[k])[4:20]
     return near, far
 
 
-def write_half(right, near, far, work, out, sems):
-    def put(near_row, far_row, first):
-        copies = []
+def tail_pe_kernel(coef, got, own, early, late, half, held, *, plans):
+    right = parity("plan")
+    near, far = one_side(coef, got, held, own, side_sign(right))
+
+    def finish(inner, row, next_row, first):
         for c in range(3):
-            work[c, :, near_row, :] += near[c]
-            work[c, :, far_row, :] += far[c]
-            copies.append(pltpu.make_async_copy(work.at[c], out.at[c, :, pl.ds(first, 8), :], sems.at[c]))
-            copies[-1].start()
-        for copy in copies:
+            half[c] = inner[c, :, first : first + 8, :]
+            half[c, :, row - first, :] += near[c]
+            half[c, :, next_row - first, :] += far[c]
+
+    for inner, use in ((late, crosses(plans)), (early, jnp.logical_not(crosses(plans)))):
+
+        @pl.when(jnp.logical_and(use, right))
+        def _(inner=inner):
+            finish(inner, 15, 14, 8)
+
+        @pl.when(jnp.logical_and(use, jnp.logical_not(right)))
+        def _(inner=inner):
+            finish(inner, 0, 1, 0)
+
+
+def tail_po_kernel(coef, got, own, base, half, before, out, work, held, sems):
+    right = jnp.logical_not(parity("plan"))
+    start = pl.multiple_of(jnp.where(right, 0, 8), 8)
+    copies = [pltpu.make_async_copy(half.at[c], out.at[c, :, pl.ds(start, 8), :], sems.at[c]) for c in range(3)]
+    for copy in copies:
+        copy.start()
+    near, far = one_side(coef, got, held, own, side_sign(right))
+
+    def finish(row, next_row, first):
+        last = []
+        for c in range(3):
+            work[c, :, row, :] = base[0, c] + near[c]
+            work[c, :, next_row, :] = base[1, c] + far[c]
+            rows = pl.ds(min(row, next_row), 2)
+            last.append(pltpu.make_async_copy(work.at[c, :, rows, :], out.at[c, :, pl.ds(first + min(row, next_row), 2), :], sems.at[3 + c]))
+            last[-1].start()
+        for copy in last:
             copy.wait()
 
     @pl.when(right)
     def _():
-        put(7, 6, 8)
+        finish(7, 6, 8)
 
     @pl.when(jnp.logical_not(right))
     def _():
-        put(0, 1, 0)
-
-
-def tail_pe_kernel(coef, sent, got, early, late, out, rest, work, held, sems, *, plans):
-    right = parity("plan")
-    for inner, use in ((late, crosses(plans)), (early, jnp.logical_not(crosses(plans)))):
-
-        @pl.when(jnp.logical_and(use, right))
-        def _(inner=inner):
-            work[...] = inner[:, :, 8:16, :]
-            rest[...] = inner[:, :, 0:8, :]
-
-        @pl.when(jnp.logical_and(use, jnp.logical_not(right)))
-        def _(inner=inner):
-            work[...] = inner[:, :, 0:8, :]
-            rest[...] = inner[:, :, 8:16, :]
-
-    near, far = one_side(coef, sent, got, held, jnp.where(right, 1.0, -1.0))
-    write_half(right, near, far, work, out, sems)
-
-
-def tail_po_kernel(coef, sent, got, rest, half, out, work, held, sems):
-    right = jnp.logical_not(parity("plan"))
-    work[...] = rest[...]
-    near, far = one_side(coef, sent, got, held, jnp.where(right, 1.0, -1.0))
-    write_half(right, near, far, work, out, sems)
+        finish(0, 1, 0)
+
+    for copy in copies:
+        copy.wait()
 
 
 VM = pl.BlockSpec(memory_space=pltpu.VMEM)
@@ -408,7 +454,7 @@
     se_got = swap(se, "story", 0)
     blocks = lax.all_to_all(blocks, "story", 0, 0, tiled=True)
     cells = u_now.shape
-    po, coef, consts = call(pack_po_kernel, [shape(rows + 8, WIDE), table, shape(16, WIDE)], [VM] * 5, planes, moved=1 << 20)(
+    po, coef, consts = call(pack_po_kernel, [shape(rows, WIDE), table, shape(16, WIDE)], [VM] * 5, planes, moved=1 << 20)(
         blocks, se_got, so_got, u_now, u_prev
     )
     po_got = swap(po, "plan", 1)
@@ -420,30 +466,37 @@
     own = (consts, coef, se_got, so_got, u_now, u_prev)
     pe, early = call(
         functools.partial(early_kernel, plans=plans),
-        [shape(rows, WIDE), shape(*cells)],
+        [shape(rows - 1, WIDE), shape(*cells)],
         [VM] * 6,
         planes + levels,
         flops=60_000_000,
         moved=4 << 20,
     )(*own)
     pe_got = swap(pe, "plan", 0)
-    (late,) = call(
-        functools.partial(late_kernel, plans=plans), [shape(*cells)], [VM] * 6, levels, flops=60_000_000, moved=4 << 20
-    )(*own)
-    half = shape(3, 16, 8, WIDE)
-    work = [pltpu.VMEM((3, 16, 8, WIDE), F32), pltpu.VMEM((3 * PAD, WIDE), F32), pltpu.SemaphoreType.DMA((3,))]
-    out, rest = call(
-        functools.partial(tail_pe_kernel, plans=plans),
-        [shape(*cells), half],
-        [VM] * 5,
-        work,
+    side = shape(6, PAD, WIDE)
+    late, out, base, pe_own, po_own = call(
+        functools.partial(late_kernel, plans=plans),
+        [shape(*cells), shape(*cells), shape(2, 3, 16, WIDE), side, side],
+        [VM] * 9,
+        levels + [pltpu.SemaphoreType.DMA((3,))],
+        flops=60_000_000,
+        moved=4 << 20,
+        places=[VM, HB, VM, VM, VM],
+    )(*own, early, pe, po)
+    held = pltpu.VMEM((3 * PAD, WIDE), F32)
+    (half,) = call(
+        functools.partial(tail_pe_kernel, plans=plans), [shape(3, 16, 8, WIDE)], [VM] * 5, [held], flops=5_000_000, moved=2 << 20
+    )(coef, pe_got, pe_own, early, late)
+    (out,) = call(
+        tail_po_kernel,
+        [shape(*cells)],
+        [VM] * 5 + [HB],
+        [pltpu.VMEM((3, 16, 8, WIDE), F32), held, pltpu.SemaphoreType.DMA((6,))],
         flops=5_000_000,
         moved=2 << 20,
-        places=[HB, VM],
-    )(coef, pe, pe_got, early, late)
-    (out,) = call(
-        tail_po_kernel, [shape(*cells)], [VM] * 4 + [HB], work, flops=5_000_000, moved=2 << 20, places=[HB], aliases={4: 0}
-    )(coef, po, po_got, rest, out)
+        places=[HB],
+        aliases={5: 0},
+    )(coef, po_got, po_own, base, half, out)
     return out
 
 

time: 37.1 us -> 36.6 us (0.987)
  waiting for transfers between devices: 2.46 us -> 2.02 us
    ppermute x4, waiting for transfers between devices: 2.46 us -> 2.02 us  [swap(): return lax.ppermute(values, axis, pairs)]
where the time goes in v8:
time: 36.6 us; the launch traced here: 36.3 us
  blocking collectives  13.4 us (37%)
  starting transfers between devices  12 us (33%)
  Pallas kernels  8.74 us (24%)
  waiting for transfers between devices  2.02 us (6%)
    all_to_all x1, blocking collectives, local(): blocks = lax.all_to_all(blocks, 'story', 0, 0, tiled=True)  13.4 us
    ppermute x4, starting transfers between devices, swap(): return lax.ppermute(values, axis, pairs)  12 us
    pallas_call x1, Pallas kernels, local(): call(functools.partial(late_kernel, plans=plans), [shape(*cells), shape(*...  4.93 us
    ppermute x4, waiting for transfers between devices, swap(): return lax.ppermute(values, axis, pairs)  2.02 us
    pallas_call x1, Pallas kernels, local(): call(tail_po_kernel, [shape(*cells)], [VM] * 5 + [HB], [pltpu.VMEM((3, 16...  1.26 us
    pallas_call x1, Pallas kernels, local(): call(functools.partial(slice_kernel, factor=0.8 / height), [shape(10, 16,...  1.21 us
  transfers between devices with their start and end apart: 4, of which 1 were waited for; matrix products, arithmetic and copies ran while one was open for 0% of the time, Pallas kernels for 16%

profile of v8, /device:TPU:57, one launch (start us, length us, event | category | flops | bytes accessed | tf_op | source)
XLA Modules:
  0.0 36.3 jit_solution(11429025817634823918)
XLA Ops:
  0.0 0.0 copy-start
  0.0 0.0 copy-start.1
  0.0 1.2 %shard_map.73 = (f32[10,16,256]{2,1,0:T(8,128)S(1)}, f32[9,16,256]{2,1,0:T(8,128)S(1)}, f32[32,128]{1,0:T(8,128)S(1)}) custom-call(f32[3,16,16,256]{3,2,1,0:T(8,128)} %now.7, f32[3,16,16,256]{3,2,1,0:T(8,128)} %prev.7, s32[1,16]{1,0:T(1,128)} %bitcast.11, s32[1,16]{1,0:T(1,128)} %bitcast.12, f32[1,8]{1,0:T(1,128)} %bitcast.13, f32[1,8]{1,0:T(1,128)} %bitcast.14, ...), custom_call_target="tpu_custom_call" | custom-call | bytes 1048576 | tf_op jit(solution)/shard_map/pallas_call | solution.py:446
  1.2 4.1 %collective-permute-start.1 = (f32[10,16,256]{2,1,0:T(8,128)S(1)}, f32[10,16,256]{2,1,0:T(8,128)S(1)}, u32[]{:S(2)}, u32[]{:S(2)}) collective-permute-start(f32[10,16,256]{2,1,0:T(8,128)S(1)} %get-tuple-element.20), channel_id=1, source_target_pairs={{8,16},{16,8},{24,32},{32,24},{40,48},{48,40},{56,64},{64,56},{72,... | collective-permute-start | bytes 491528 | tf_op jit(solution)/shard_map/ppermute | solution.py:20
  5.3 0.1 collective-permute-start
  5.4 13.4 %all_to_all.11 = f32[32,1,128]{2,1,0:T(1,128)S(1)} all-to-all(f32[32,1,128]{2,1,0:T(1,128)S(1)} %bitcast.10), channel_id=1, replica_groups=mesh['story'=32,'plan'=8] {'story'}, dimensions={0} | all-to-all | bytes 32768 | tf_op jit(solution)/shard_map/all_to_all | solution.py:455
  18.8 0.0 collective-permute-done.se
  18.8 0.0 collective-permute-done.1.so
  18.8 0.0 copy-done
  18.8 0.0 copy-done.1
  18.8 0.4 %shard_map.74 = (f32[120,256]{1,0:T(8,128)S(1)}, f32[4,24,256]{2,1,0:T(8,128)S(1)}, f32[16,256]{1,0:T(8,128)S(1)}) custom-call(f32[32,128]{1,0:T(8,128)S(1)} %bitcast.9, f32[9,16,256]{2,1,0:T(8,128)S(1)} %collective-permute-done.se, f32[10,16,256]{2,1,0:T(8,128)S(1)} %collective-permute-done.1.so, f32[3,16,16,256]{3,2,1,0:T(8,128)S(1)} %copy-done, ...), custom_call_target="tpu_custom_call" | custom-call | bytes 1048576 | tf_op jit(solution)/shard_map/pallas_call | solution.py:457
  19.3 7.7 %collective-permute-start.2 = (f32[120,256]{1,0:T(8,128)S(1)}, f32[120,256]{1,0:T(8,128)S(1)}, u32[]{:S(2)}, u32[]{:S(2)}) collective-permute-start(f32[120,256]{1,0:T(8,128)S(1)} %get-tuple-element.22.po_sent), channel_id=1, source_target_pairs={{1,2},{2,1},{3,4},{4,3},{5,6},{6,5},{9,10},{10,9},{11,12},{12,11},... | collective-permute-start | bytes 368648 | tf_op jit(solution)/shard_map/ppermute | solution.py:20
  27.0 0.3 shard_map.75
  27.3 0.1 collective-permute-start.3
  27.4 4.9 %shard_map.76 = (f32[3,16,16,256]{3,2,1,0:T(8,128)S(1)}, f32[3,16,16,256]{3,2,1,0:T(8,128)}, f32[2,3,16,256]{3,2,1,0:T(8,128)S(1)}, f32[6,24,256]{2,1,0:T(8,128)S(1)}, f32[6,24,256]{2,1,0:T(8,128)S(1)}) custom-call(f32[16,256]{1,0:T(8,128)S(1)} %get-tuple-element.23.consts, f32[4,24,256]{2,1,0:T(8,128)S(1)} %get-tuple-element.21.coef, ...), custom_call_target="tpu_custom_call" | custom-call | flops 60000000 | bytes 4194304 | tf_op jit(solution)/shard_map/pallas_call | solution.py:477
  32.4 0.0 collective-permute-done.3.got
  32.4 0.6 %shard_map.77.half = f32[3,16,8,256]{3,2,1,0:T(8,128)S(1)} custom-call(f32[4,24,256]{2,1,0:T(8,128)S(1)} %get-tuple-element.21.coef, f32[119,256]{1,0:T(8,128)S(1)} %collective-permute-done.3.got, f32[6,24,256]{2,1,0:T(8,128)S(1)} %get-tuple-element.28.own, f32[3,16,16,256]{3,2,1,0:T(8,128)S(1)} %get-tuple-element.24.early, ...), custom_call_target="tpu_custom_call" | custom-call | flops 5000000 | bytes 2097152 | tf_op jit(solution)/shard_map/pallas_call | solution.py:487
  33.0 2.0 %collective-permute-done.2.got = f32[120,256]{1,0:T(8,128)S(1)} collective-permute-done((f32[120,256]{1,0:T(8,128)S(1)}, f32[120,256]{1,0:T(8,128)S(1)}, u32[]{:S(2)}, u32[]{:S(2)}) %collective-permute-start.2) | collective-permute-done | bytes 122912 | tf_op jit(solution)/shard_map/ppermute | solution.py:20
  35.0 1.3 %shard_map.78 = f32[3,16,16,256]{3,2,1,0:T(8,128)} custom-call(f32[4,24,256]{2,1,0:T(8,128)S(1)} %get-tuple-element.21.coef, f32[120,256]{1,0:T(8,128)S(1)} %collective-permute-done.2.got, f32[6,24,256]{2,1,0:T(8,128)S(1)} %get-tuple-element.26.own, f32[2,3,16,256]{3,2,1,0:T(8,128)S(1)} %get-tuple-element.27.base, ...), custom_call_target="tpu_custom_call", output_to_operand_aliasing={{}: (5, {})} | custom-call | flops 5000000 | bytes 2097152 | tf_op jit(solution)/shard_map/pallas_call | solution.py:490
Async XLA Ops:
  0.0 18.8 %copy-start = (f32[3,16,16,256]{3,2,1,0:T(8,128)S(1)}, f32[3,16,16,256]{3,2,1,0:T(8,128)}, u32[]{:S(2)}) copy-start(f32[3,16,16,256]{3,2,1,0:T(8,128)} %now.7) | copy-start | bytes 2359300
  0.0 18.8 %copy-start.1 = (f32[3,16,16,256]{3,2,1,0:T(8,128)S(1)}, f32[3,16,16,256]{3,2,1,0:T(8,128)}, u32[]{:S(2)}) copy-start(f32[3,16,16,256]{3,2,1,0:T(8,128)} %prev.7) | copy-start | bytes 2359300
  1.2 17.6 %collective-permute-start.1 = (f32[10,16,256]{2,1,0:T(8,128)S(1)}, f32[10,16,256]{2,1,0:T(8,128)S(1)}, u32[]{:S(2)}, u32[]{:S(2)}) collective-permute-start(f32[10,16,256]{2,1,0:T(8,128)S(1)} %get-tuple-element.20), channel_id=1, source_target_pairs={{8,16},{16,8},{24,32},{32,24},{40,48},{48,40},{56,64},{64,56},{72,... | collective-permute-start | bytes 491528 | tf_op jit(solution)/shard_map/ppermute | solution.py:20
  5.3 13.5 %collective-permute-start = (f32[9,16,256]{2,1,0:T(8,128)S(1)}, f32[9,16,256]{2,1,0:T(8,128)S(1)}, u32[]{:S(2)}, u32[]{:S(2)}) collective-permute-start(f32[9,16,256]{2,1,0:T(8,128)S(1)} %get-tuple-element.19), channel_id=1, source_target_pairs={{0,8},{8,0},{16,24},{24,16},{32,40},{40,32},{48,56},{56,48},{64,72... | collective-permute-start | bytes 442376 | tf_op jit(solution)/shard_map/ppermute | solution.py:20
  19.3 15.8 %collective-permute-start.2 = (f32[120,256]{1,0:T(8,128)S(1)}, f32[120,256]{1,0:T(8,128)S(1)}, u32[]{:S(2)}, u32[]{:S(2)}) collective-permute-start(f32[120,256]{1,0:T(8,128)S(1)} %get-tuple-element.22.po_sent), channel_id=1, source_target_pairs={{1,2},{2,1},{3,4},{4,3},{5,6},{6,5},{9,10},{10,9},{11,12},{12,11},... | collective-permute-start | bytes 368648 | tf_op jit(solution)/shard_map/ppermute | solution.py:20
  27.3 5.0 %collective-permute-start.3 = (f32[119,256]{1,0:T(8,128)S(1)}, f32[119,256]{1,0:T(8,128)S(1)}, u32[]{:S(2)}, u32[]{:S(2)}) collective-permute-start(f32[119,256]{1,0:T(8,128)S(1)} %get-tuple-element.25.pe_sent), channel_id=1, source_target_pairs={{0,1},{1,0},{2,3},{3,2},{4,5},{5,4},{6,7},{7,6},{8,9},{9,8},{10,11... | collective-permute-start | bytes 365576 | tf_op jit(solution)/shard_map/ppermute | solution.py:20

commit v9 on v8

--- a/solution.py
+++ b/solution.py
@@ -110,7 +110,7 @@
     return lax.axis_index(axis) % 2 == 0
 
 
-def slice_kernel(now, prev, occ_h, mat_h, shear_h, lame_h, dens_h, so, se, blocks, occ, mat, shear_t, lame_t, dens_t, held, sems, *, factor):
+def slice_kernel(now, prev, occ_h, mat_h, shear_h, lame_h, dens_h, so, se, blocks, occ, mat, shear_t, lame_t, dens_t, held, held_blocks, sems, *, factor):
     even = parity("story")
     smalls = []
     for k, (source, target) in enumerate(((occ_h, occ), (mat_h, mat), (shear_h, shear_t), (lame_h, lame_t), (dens_h, dens_t))):
@@ -146,7 +146,9 @@
     row = jnp.zeros((8, 128), F32)
     for k, part in enumerate(parts):
         row = jnp.where(segment == k, part, row)
-    blocks[...] = jnp.broadcast_to(row[0:1], blocks.shape)
+    held_blocks[...] = jnp.broadcast_to(row[0:1], held_blocks.shape)
+    copies.append(pltpu.make_async_copy(held_blocks, blocks, sems.at[11]))
+    copies[-1].start()
     for copy in copies:
         copy.wait()
 
@@ -162,18 +164,39 @@
     return ghost
 
 
-def fill(right, ghost, consts, coef, now, prev, out, far_rows, prev_rows):
+def planes_kernel(now, prev, po, pe, token):
+    even = parity("plan")
+    token[...] = jnp.zeros(token.shape, F32)
+
+    def load(out, near, far):
+        for k, (source, x) in enumerate(((now, near), (now, far), (prev, near))):
+            for c in range(3):
+                base = (3 * k + c) * 16
+                out[base : base + 16, :] = source[c, :, x, :]
+
+    @pl.when(even)
+    def _():
+        load(pe, 15, 14)
+        load(po, 0, 1)
+
+    @pl.when(jnp.logical_not(even))
+    def _():
+        load(pe, 0, 1)
+        load(po, 15, 14)
+
+
+def fill(right, ghost, consts, coef, layers, out, far_rows, prev_rows):
     occupied = consts[4:5, :]
 
     def load(near, far):
-        for c in range(3):
-            for target, source, x in ((out, now, near), (far_rows, now, far), (prev_rows, prev, near)):
+        for kind, (target, x, sides) in enumerate(((out, near, (0, 3)), (far_rows, far, (0, 3)), (prev_rows, near, (6,)))):
+            for c in range(3):
                 base = c * PAD
-                target[base + 4 : base + 20, :] = source[c, :, x, :] * occupied
-                kinds = (6,) if source is prev else (0, 3)
-                for k, kind in enumerate(kinds):
-                    target[base + 3 - k : base + 4 - k, :] = ghost(False, kind + c, pl.ds(x, 1), slice(None))
-                    target[base + 20 + k : base + 21 + k, :] = ghost(True, kind + c, pl.ds(x, 1), slice(None))
+                at = (3 * kind + c) * 16
+                target[base + 4 : base + 20, :] = layers[at : at + 16, :] * occupied
+                for k, side in enumerate(sides):
+                    target[base + 3 - k : base + 4 - k, :] = ghost(False, side + c, pl.ds(x, 1), slice(None))
+                    target[base + 20 + k : base + 21 + k, :] = ghost(True, side + c, pl.ds(x, 1), slice(None))
 
     @pl.when(right)
     def _():
@@ -201,7 +224,7 @@
         out[PAD + row : PAD + row + 1, :] = jnp.where(lane % 2 == 0, consts[5 + k : 6 + k, :], consts[10 + k : 11 + k, :])
 
 
-def pack_po_kernel(blocks, se, so, now, prev, po, coef, consts, far_rows, prev_rows):
+def expand_kernel(blocks, token, coef, consts):
     place = lax.axis_index("story")
     step = lax.broadcasted_iota(jnp.int32, blocks.shape, 0)
     rows = [jnp.sum(jnp.where(step == place + k, blocks[...], 0.0), 0, keepdims=True) for k in (0, 1, -1)]
@@ -224,7 +247,10 @@
     consts[15:16, :] = carried
     for k, value in enumerate(coefficients(sets[0], sets[1], sets[2], carried)):
         coef[k] = value
-    fill(jnp.logical_not(parity("plan")), ghost_of(se, so, consts), consts, coef, now, prev, po, far_rows, prev_rows)
+
+
+def pack_po_kernel(consts, coef, se, so, layers, po, far_rows, prev_rows):
+    fill(jnp.logical_not(parity("plan")), ghost_of(se, so, consts), consts, coef, layers, po, far_rows, prev_rows)
 
 
 def advance(below, here, above, before, coefs, sign):
@@ -242,9 +268,9 @@
     return 2.0 * here - before + a * lap + b * coup - geometric
 
 
-def crosses(plans):
+def runs_late(plans):
     place = lax.axis_index("plan")
-    return jnp.logical_or(place == plans // 2 - 1, place == plans // 2)
+    return jnp.logical_not(jnp.logical_or(place == plans // 2 - 2, place == plans // 2 + 1))
 
 
 def both_steps(consts, coef, se, so, now, prev, out, u0, u1, before):
@@ -271,19 +297,19 @@
         for c in range(3):
             target[c, i] = update(here[c], earlier(c, i), lap[c], coup[c], a, b, gu, gd, below[c], above[c])
 
-    @pl.loop(0, 18, unroll=3)
+    @pl.loop(0, 18, unroll=6)
     def _(i):
         one(u0, lambda c, i: before[c, i], u1, i, 3)
 
-    @pl.loop(0, 16, unroll=4)
+    @pl.loop(0, 16, unroll=8)
     def _(i):
         one(u1, lambda c, i: u0[c, i + 2], out, i, 4)
 
 
-def early_kernel(consts, coef, se, so, now, prev, pe, out, far_rows, prev_rows, u0, u1, before, *, plans):
-    fill(parity("plan"), ghost_of(se, so, consts), consts, coef, now, prev, pe, far_rows, prev_rows)
-
-    @pl.when(jnp.logical_not(crosses(plans)))
+def early_kernel(consts, coef, se, so, now, prev, layers, pe, out, far_rows, prev_rows, u0, u1, before, *, plans):
+    fill(parity("plan"), ghost_of(se, so, consts), consts, coef, layers, pe, far_rows, prev_rows)
+
+    @pl.when(jnp.logical_not(runs_late(plans)))
     def _():
         both_steps(consts, coef, se, so, now, prev, out, u0, u1, before)
 
@@ -296,38 +322,57 @@
     return jnp.where(right, 1.0, -1.0)
 
 
-def late_kernel(consts, coef, se, so, now, prev, early, pe_sent, po_sent, late, out, base, pe_own, po_own, u0, u1, before, sems, *, plans):
+def late_kernel(consts, coef, se, so, now, prev, early, pe_sent, po_sent, late, base, pe_own, po_own, u0, u1, before, *, plans):
     right = parity("plan")
-    cross = crosses(plans)
+    cross = runs_late(plans)
 
     @pl.when(cross)
     def _():
         both_steps(consts, coef, se, so, now, prev, late, u0, u1, before)
 
-    def finish(inner, near, far, first):
-        copies = [
-            pltpu.make_async_copy(inner.at[c, :, pl.ds(first, 8), :], out.at[c, :, pl.ds(first, 8), :], sems.at[c]) for c in range(3)
-        ]
-        for copy in copies:
-            copy.start()
+    for sent, own, sign in ((pe_sent, pe_own, side_sign(right)), (po_sent, po_own, -side_sign(right))):
+        for k, v in enumerate(sum(stencil(planes_of(sent), None, None, sign), [])):
+            own[k] = v
+
+    def finish(inner, near, far):
         for c in range(3):
             base[0, c] = inner[c, :, near, :]
             base[1, c] = inner[c, :, far, :]
-        for sent, own, sign in ((pe_sent, pe_own, side_sign(right)), (po_sent, po_own, -side_sign(right))):
-            for k, v in enumerate(sum(stencil(planes_of(sent), None, None, sign), [])):
-                own[k] = v
-        for copy in copies:
-            copy.wait()
 
     for inner, use in ((late, cross), (early, jnp.logical_not(cross))):
 
         @pl.when(jnp.logical_and(use, right))
         def _(inner=inner):
-            finish(inner, 0, 1, 0)
+            finish(inner, 0, 1)
 
         @pl.when(jnp.logical_and(use, jnp.logical_not(right)))
         def _(inner=inner):
-            finish(inner, 15, 14, 8)
+            finish(inner, 15, 14)
+
+
+def rows_of(v):
+    lower, upper = row_shift(v)
+    return lower + upper + 4.0 * v, upper - lower
+
+
+def outer_terms(layer, sign):
+    (v0, s0, f0), (v1, s1, f1), (v2, s2, f2) = layer
+    lap = [lane_smooth(s - 2.0 * v) - 2.0 * s for v, s, _ in layer]
+    c0 = lane_smooth(2.0 * s0 + (3.0 * sign) * f1) + lane_first((3.0 * sign) * s2)
+    c1 = lane_smooth(2.0 * s1 - 12.0 * v1 + (3.0 * sign) * f0) + lane_first(3.0 * f2)
+    c2 = lane_first(3.0 * (sign * s0 + f1)) + 2.0 * lane_smooth(s2) - 12.0 * s2
+    return lap, [c0, c1, c2]
+
+
+def both_terms(here, outer, sign):
+    zs = [o[0] + 4.0 * h[0] for h, o in zip(here, outer)]
+    s_zs = [o[1] + 4.0 * h[1] for h, o in zip(here, outer)]
+    f_zs = [o[2] + 4.0 * h[2] for h, o in zip(here, outer)]
+    lap = [lane_smooth(s_zs[j] - 2.0 * (here[j][1] + zs[j])) - 2.0 * s_zs[j] for j in range(3)]
+    c0 = lane_smooth(2.0 * s_zs[0] - 12.0 * here[0][1] + (3.0 * sign) * outer[1][2]) + lane_first((3.0 * sign) * outer[2][1])
+    c1 = lane_smooth(2.0 * s_zs[1] - 12.0 * zs[1] + (3.0 * sign) * outer[0][2]) + lane_first(3.0 * f_zs[2])
+    c2 = lane_first(3.0 * (sign * outer[0][1] + f_zs[1])) + 2.0 * lane_smooth(s_zs[2]) - 12.0 * s_zs[2]
+    return lap, [c0, c1, c2]
 
 
 def one_side(coef, got, held, own, sign):
@@ -350,30 +395,51 @@
         return jnp.where(z < 0, under, jnp.where(z > 15, over, got[row : row + 1, :]))
 
     got_a, got_b = pick(1), pick(22)
-    lap, coup = stencil(None, None, planes_of(got), sign)
+    lap, coup = outer_terms([(v,) + rows_of(v) for v in planes_of(got)], sign)
     delta = [a * lap[k] + b * coup[k] for k in range(3)]
     outer = [p + got_a * own[k] + got_b * own[3 + k] for k, p in enumerate(planes_of(held))]
-    zero = jnp.zeros((PAD, WIDE), F32)
-    near_more = advance(None, delta, outer, [zero] * 3, (a, b, gu, gd), sign)
-    lap, coup = stencil(None, None, delta, sign)
+    delta_rows = [(v,) + rows_of(v) for v in delta]
+    outer_rows = [(v,) + rows_of(v) for v in outer]
+    far_lap, far_coup = outer_terms(delta_rows, sign)
+    near_lap, near_coup = both_terms(delta_rows, outer_rows, sign)
     near, far = [None] * 3, [None] * 3
     for k, c in enumerate((1, 0, 2)):
-        near[c] = near_more[k][4:20]
-        far[c] = (a * lap[k] + b * coup[k])[4:20]
+        lower, upper = row_shift(delta[k])
+        geometric = gu * (upper - delta[k]) - gd * (delta[k] - lower)
+        near[c] = (2.0 * delta[k] + a * near_lap[k] + b * near_coup[k] - geometric)[4:20]
+        far[c] = (a * far_lap[k] + b * far_coup[k])[4:20]
     return near, far
 
 
-def tail_pe_kernel(coef, got, own, early, late, half, held, *, plans):
+def tail_pe_kernel(coef, got, own, early, late, out, half, held, sems, *, plans):
     right = parity("plan")
-    near, far = one_side(coef, got, held, own, side_sign(right))
+    cross = runs_late(plans)
+    start = pl.multiple_of(jnp.where(right, 0, 8), 8)
+
+    def copies(inner):
+        return [pltpu.make_async_copy(inner.at[c, :, pl.ds(start, 8), :], out.at[c, :, pl.ds(start, 8), :], sems.at[c]) for c in range(3)]
+
+    def begin(inner):
+        for copy in copies(inner):
+            copy.start()
 
     def finish(inner, row, next_row, first):
         for c in range(3):
             half[c] = inner[c, :, first : first + 8, :]
             half[c, :, row - first, :] += near[c]
             half[c, :, next_row - first, :] += far[c]
-
-    for inner, use in ((late, crosses(plans)), (early, jnp.logical_not(crosses(plans)))):
+        for copy in copies(inner):
+            copy.wait()
+
+    places = ((late, cross), (early, jnp.logical_not(cross)))
+    for inner, use in places:
+
+        @pl.when(use)
+        def _(inner=inner):
+            begin(inner)
+
+    near, far = one_side(coef, got, held, own, side_sign(right))
+    for inner, use in places:
 
         @pl.when(jnp.logical_and(use, right))
         def _(inner=inner):
@@ -445,18 +511,20 @@
     small = [v.reshape(1, -1) for v in (occupancy, materials, shear_table, lame_table, density_table)]
     so, se, blocks = call(
         functools.partial(slice_kernel, factor=0.8 / height),
-        [shape(10, 16, WIDE), face, shape(stories, 128)],
+        [face, shape(10, 16, WIDE), shape(stories, 128)],
         [HB] * 7,
-        [pltpu.VMEM(v.shape, v.dtype) for v in small] + [pltpu.VMEM((8, 128), F32), pltpu.SemaphoreType.DMA((11,))],
+        [pltpu.VMEM(v.shape, v.dtype) for v in small] + [pltpu.VMEM((8, 128), F32), pltpu.VMEM((stories, 128), F32), pltpu.SemaphoreType.DMA((12,))],
         moved=1 << 20,
+        places=[VM, VM, HB],
     )(*(pltpu.with_memory_space_constraint(v, pltpu.HBM) for v in [u_now, u_prev] + small))
     so_got = swap(so, "story", 1)
     se_got = swap(se, "story", 0)
     blocks = lax.all_to_all(blocks, "story", 0, 0, tiled=True)
     cells = u_now.shape
-    po, coef, consts = call(pack_po_kernel, [shape(rows, WIDE), table, shape(16, WIDE)], [VM] * 5, planes, moved=1 << 20)(
-        blocks, se_got, so_got, u_now, u_prev
-    )
+    layers = shape(9 * 16, WIDE)
+    po_layers, pe_layers, token = call(planes_kernel, [layers, layers, shape(8, 128)], [VM] * 2, flops=1_000_000_000, moved=16 << 20)(u_now, u_prev)
+    coef, consts = call(expand_kernel, [table, shape(16, WIDE)], [VM] * 2, flops=20_000_000_000, moved=1 << 30)(blocks, token)
+    (po,) = call(pack_po_kernel, [shape(rows, WIDE)], [VM] * 5, planes, moved=1 << 20)(consts, coef, se_got, so_got, po_layers)
     po_got = swap(po, "plan", 1)
     levels = [
         pltpu.VMEM((3, 20, 16, WIDE), F32),
@@ -467,25 +535,30 @@
     pe, early = call(
         functools.partial(early_kernel, plans=plans),
         [shape(rows - 1, WIDE), shape(*cells)],
-        [VM] * 6,
+        [VM] * 7,
         planes + levels,
         flops=60_000_000,
         moved=4 << 20,
-    )(*own)
+    )(*own, pe_layers)
     pe_got = swap(pe, "plan", 0)
     side = shape(6, PAD, WIDE)
-    late, out, base, pe_own, po_own = call(
+    late, base, pe_own, po_own = call(
         functools.partial(late_kernel, plans=plans),
-        [shape(*cells), shape(*cells), shape(2, 3, 16, WIDE), side, side],
+        [shape(*cells), shape(2, 3, 16, WIDE), side, side],
         [VM] * 9,
-        levels + [pltpu.SemaphoreType.DMA((3,))],
+        levels,
         flops=60_000_000,
         moved=4 << 20,
-        places=[VM, HB, VM, VM, VM],
     )(*own, early, pe, po)
     held = pltpu.VMEM((3 * PAD, WIDE), F32)
-    (half,) = call(
-        functools.partial(tail_pe_kernel, plans=plans), [shape(3, 16, 8, WIDE)], [VM] * 5, [held], flops=5_000_000, moved=2 << 20
+    out, half = call(
+        functools.partial(tail_pe_kernel, plans=plans),
+        [shape(*cells), shape(3, 16, 8, WIDE)],
+        [VM] * 5,
+        [held, pltpu.SemaphoreType.DMA((3,))],
+        flops=5_000_000,
+        moved=2 << 20,
+        places=[HB, VM],
     )(coef, pe_got, pe_own, early, late)
     (out,) = call(
         tail_po_kernel,

time: 36.6 us -> 35.6 us (0.973)
  the two profiles are of different devices: /device:TPU:57 before, /device:TPU:30 now
where the time goes in v9:
time: 35.6 us; the launch traced here: 35.5 us
  starting transfers between devices  21.2 us (60%)
  Pallas kernels  8.92 us (25%)
  waiting for transfers between devices  5.2 us (15%)
    ppermute x4, starting transfers between devices, swap(): return lax.ppermute(values, axis, pairs)  12.2 us
    all_to_all x1, starting transfers between devices, local(): blocks = lax.all_to_all(blocks, 'story', 0, 0, tiled=True)  9.05 us
    ppermute x4, waiting for transfers between devices, swap(): return lax.ppermute(values, axis, pairs)  4.94 us
    pallas_call x1, Pallas kernels, local(): call(functools.partial(late_kernel, plans=plans), [shape(*cells), shape(2...  4.06 us
    pallas_call x1, Pallas kernels, local(): call(functools.partial(slice_kernel, factor=0.8 / height), [face, shape(1...  1.67 us
    pallas_call x1, Pallas kernels, local(): call(tail_po_kernel, [shape(*cells)], [VM] * 5 + [HB], [pltpu.VMEM((3, 16...  1.23 us
    pallas_call x1, Pallas kernels, local(): call(functools.partial(tail_pe_kernel, plans=plans), [shape(*cells), shap...  1.19 us
  transfers between devices with their start and end apart: 5, of which 4 were waited for; matrix products, arithmetic and copies ran while one was open for 0% of the time, Pallas kernels for 16%

profile of v9, /device:TPU:30, one launch (start us, length us, event | category | flops | bytes accessed | tf_op | source)
XLA Modules:
  0.0 35.5 jit_solution(1800752766919714036)
XLA Ops:
  0.0 0.0 copy-start
  0.0 0.0 copy-start.1
  0.0 1.7 %shard_map.73 = (f32[9,16,256]{2,1,0:T(8,128)S(1)}, f32[10,16,256]{2,1,0:T(8,128)S(1)}, f32[32,128]{1,0:T(8,128)}) custom-call(f32[3,16,16,256]{3,2,1,0:T(8,128)} %now.7, f32[3,16,16,256]{3,2,1,0:T(8,128)} %prev.7, s32[1,16]{1,0:T(1,128)} %bitcast.10, s32[1,16]{1,0:T(1,128)} %bitcast.11, f32[1,8]{1,0:T(1,128)} %bitcast.12, f32[1,8]{1,0:T(1,128)} %bitcast.13, ...), custom_call_target="tpu_custom_call" | custom-call | bytes 1048576 | tf_op jit(solution)/shard_map/pallas_call | solution.py:512
  1.7 9.0 %all-to-all-start = ((f32[32,1,128]{2,1,0:T(1,128)}), f32[32,1,128]{2,1,0:T(1,128)S(1)}, u32[]{:S(2)}, u32[]{:S(2)}) async-start(f32[32,1,128]{2,1,0:T(1,128)} %bitcast.6), calls=%async_computation | async-start | bytes 32768 | tf_op jit(solution)/shard_map/all_to_all | solution.py:522
  10.7 5.2 %collective-permute-start.1 = (f32[9,16,256]{2,1,0:T(8,128)S(1)}, f32[9,16,256]{2,1,0:T(8,128)S(1)}, u32[]{:S(2)}, u32[]{:S(2)}) collective-permute-start(f32[9,16,256]{2,1,0:T(8,128)S(1)} %get-tuple-element.26), channel_id=1, source_target_pairs={{8,16},{16,8},{24,32},{32,24},{40,48},{48,40},{56,64},{64,56},{72,... | collective-permute-start | bytes 442376 | tf_op jit(solution)/shard_map/ppermute | solution.py:20
  16.0 0.1 collective-permute-start
  16.1 0.0 copy-done
  16.1 0.0 copy-done.1
  16.1 0.1 shard_map.74
  16.2 0.3 all-to-all-done
  16.5 0.1 shard_map.75
  16.6 4.6 %collective-permute-done.1.so = f32[9,16,256]{2,1,0:T(8,128)S(1)} collective-permute-done((f32[9,16,256]{2,1,0:T(8,128)S(1)}, f32[9,16,256]{2,1,0:T(8,128)S(1)}, u32[]{:S(2)}, u32[]{:S(2)}) %collective-permute-start.1) | collective-permute-done | bytes 147488 | tf_op jit(solution)/shard_map/ppermute | solution.py:20
  21.2 0.0 collective-permute-done.se
  21.2 0.3 shard_map.76.po_sent
  21.4 6.1 %collective-permute-start.2 = (f32[120,256]{1,0:T(8,128)S(1)}, f32[120,256]{1,0:T(8,128)S(1)}, u32[]{:S(2)}, u32[]{:S(2)}) collective-permute-start(f32[120,256]{1,0:T(8,128)S(1)} %shard_map.76.po_sent), channel_id=1, source_target_pairs={{1,2},{2,1},{3,4},{4,3},{5,6},{6,5},{9,10},{10,9},{11,12},{12,11},... | collective-permute-start | bytes 368648 | tf_op jit(solution)/shard_map/ppermute | solution.py:20
  27.5 0.3 shard_map.77
  27.8 0.8 %collective-permute-start.3 = (f32[119,256]{1,0:T(8,128)S(1)}, f32[119,256]{1,0:T(8,128)S(1)}, u32[]{:S(2)}, u32[]{:S(2)}) collective-permute-start(f32[119,256]{1,0:T(8,128)S(1)} %get-tuple-element.30.pe_sent), channel_id=1, source_target_pairs={{0,1},{1,0},{2,3},{3,2},{4,5},{5,4},{6,7},{7,6},{8,9},{9,8},{10,11... | collective-permute-start | bytes 365576 | tf_op jit(solution)/shard_map/ppermute | solution.py:20
  28.6 4.1 %shard_map.78 = (f32[3,16,16,256]{3,2,1,0:T(8,128)S(1)}, f32[2,3,16,256]{3,2,1,0:T(8,128)S(1)}, f32[6,24,256]{2,1,0:T(8,128)S(1)}, f32[6,24,256]{2,1,0:T(8,128)S(1)}) custom-call(f32[16,256]{1,0:T(8,128)S(1)} %get-tuple-element.24.consts, f32[4,24,256]{2,1,0:T(8,128)S(1)} %get-tuple-element.23.coef, f32[10,16,256]{2,1,0:T(8,128)S(1)} %collective-permute-done.se, ...), custom_call_target="tpu_custom_call" | custom-call | flops 60000000 | bytes 4194304 | tf_op jit(solution)/shard_map/pallas_call | solution.py:545
  32.7 0.1 collective-permute-done.3.got
  32.7 1.2 %shard_map.79 = (f32[3,16,16,256]{3,2,1,0:T(8,128)}, f32[3,16,8,256]{3,2,1,0:T(8,128)S(1)}) custom-call(f32[4,24,256]{2,1,0:T(8,128)S(1)} %get-tuple-element.23.coef, f32[119,256]{1,0:T(8,128)S(1)} %collective-permute-done.3.got, f32[6,24,256]{2,1,0:T(8,128)S(1)} %get-tuple-element.33.own, f32[3,16,16,256]{3,2,1,0:T(8,128)S(1)} %get-tuple-element.29.early, ...), custom_call_target="tpu_custom_call" | custom-call | flops 5000000 | bytes 2097152 | tf_op jit(solution)/shard_map/pallas_call | solution.py:554
  33.9 0.3 collective-permute-done.2.got
  34.2 1.2 %shard_map.80 = f32[3,16,16,256]{3,2,1,0:T(8,128)} custom-call(f32[4,24,256]{2,1,0:T(8,128)S(1)} %get-tuple-element.23.coef, f32[120,256]{1,0:T(8,128)S(1)} %collective-permute-done.2.got, f32[6,24,256]{2,1,0:T(8,128)S(1)} %get-tuple-element.31.own, f32[2,3,16,256]{3,2,1,0:T(8,128)S(1)} %get-tuple-element.32.base, ...), custom_call_target="tpu_custom_call", output_to_operand_aliasing={{}: (5, {})} | custom-call | flops 5000000 | bytes 2097152 | tf_op jit(solution)/shard_map/pallas_call | solution.py:563
Async XLA Ops:
  0.0 16.1 %copy-start = (f32[3,16,16,256]{3,2,1,0:T(8,128)S(1)}, f32[3,16,16,256]{3,2,1,0:T(8,128)}, u32[]{:S(2)}) copy-start(f32[3,16,16,256]{3,2,1,0:T(8,128)} %now.7) | copy-start | bytes 2359300
  0.0 16.1 %copy-start.1 = (f32[3,16,16,256]{3,2,1,0:T(8,128)S(1)}, f32[3,16,16,256]{3,2,1,0:T(8,128)}, u32[]{:S(2)}) copy-start(f32[3,16,16,256]{3,2,1,0:T(8,128)} %prev.7) | copy-start | bytes 2359300
  1.7 14.8 %all-to-all-start = ((f32[32,1,128]{2,1,0:T(1,128)}), f32[32,1,128]{2,1,0:T(1,128)S(1)}, u32[]{:S(2)}, u32[]{:S(2)}) async-start(f32[32,1,128]{2,1,0:T(1,128)} %bitcast.6), calls=%async_computation | async-start | bytes 32768 | tf_op jit(solution)/shard_map/all_to_all | solution.py:522
  10.7 10.4 %collective-permute-start.1 = (f32[9,16,256]{2,1,0:T(8,128)S(1)}, f32[9,16,256]{2,1,0:T(8,128)S(1)}, u32[]{:S(2)}, u32[]{:S(2)}) collective-permute-start(f32[9,16,256]{2,1,0:T(8,128)S(1)} %get-tuple-element.26), channel_id=1, source_target_pairs={{8,16},{16,8},{24,32},{32,24},{40,48},{48,40},{56,64},{64,56},{72,... | collective-permute-start | bytes 442376 | tf_op jit(solution)/shard_map/ppermute | solution.py:20
  16.0 5.2 %collective-permute-start = (f32[10,16,256]{2,1,0:T(8,128)S(1)}, f32[10,16,256]{2,1,0:T(8,128)S(1)}, u32[]{:S(2)}, u32[]{:S(2)}) collective-permute-start(f32[10,16,256]{2,1,0:T(8,128)S(1)} %get-tuple-element.25), channel_id=1, source_target_pairs={{0,8},{8,0},{16,24},{24,16},{32,40},{40,32},{48,56},{56,48},{64,72... | collective-permute-start | bytes 491528 | tf_op jit(solution)/shard_map/ppermute | solution.py:20
  21.4 12.8 %collective-permute-start.2 = (f32[120,256]{1,0:T(8,128)S(1)}, f32[120,256]{1,0:T(8,128)S(1)}, u32[]{:S(2)}, u32[]{:S(2)}) collective-permute-start(f32[120,256]{1,0:T(8,128)S(1)} %shard_map.76.po_sent), channel_id=1, source_target_pairs={{1,2},{2,1},{3,4},{4,3},{5,6},{6,5},{9,10},{10,9},{11,12},{12,11},... | collective-permute-start | bytes 368648 | tf_op jit(solution)/shard_map/ppermute | solution.py:20
  27.8 5.0 %collective-permute-start.3 = (f32[119,256]{1,0:T(8,128)S(1)}, f32[119,256]{1,0:T(8,128)S(1)}, u32[]{:S(2)}, u32[]{:S(2)}) collective-permute-start(f32[119,256]{1,0:T(8,128)S(1)} %get-tuple-element.30.pe_sent), channel_id=1, source_target_pairs={{0,1},{1,0},{2,3},{3,2},{4,5},{5,4},{6,7},{7,6},{8,9},{9,8},{10,11... | collective-permute-start | bytes 365576 | tf_op jit(solution)/shard_map/ppermute | solution.py:20

commit v10 on v9

--- a/solution.py
+++ b/solution.py
@@ -110,7 +110,7 @@
     return lax.axis_index(axis) % 2 == 0
 
 
-def slice_kernel(now, prev, occ_h, mat_h, shear_h, lame_h, dens_h, so, se, blocks, occ, mat, shear_t, lame_t, dens_t, held, held_blocks, sems, *, factor):
+def slice_kernel(now, prev, occ_h, mat_h, shear_h, lame_h, dens_h, small, se, so, blocks, occ, mat, shear_t, lame_t, dens_t, held, held_blocks, sems, *, factor):
     even = parity("story")
     smalls = []
     for k, (source, target) in enumerate(((occ_h, occ), (mat_h, mat), (shear_h, shear_t), (lame_h, lame_t), (dens_h, dens_t))):
@@ -121,6 +121,10 @@
         near, far = jnp.where(top, 15, 0), jnp.where(top, 14, 1)
         for j, (source, z) in enumerate(((now, near), (now, far), (prev, near))):
             copies.append(pltpu.make_async_copy(source.at[:, z], out.at[pl.ds(3 * j, 3)], sems.at[3 * k + j]))
+            if k == 1:
+                for h, x in enumerate((0, 14)):
+                    rows = small.at[pl.ds(3 * j, 3), pl.ds(2 * h, 2), :]
+                    copies.append(pltpu.make_async_copy(source.at[:, z, pl.ds(x, 2), :], rows, sems.at[12 + 2 * j + h]))
     for copy in smalls + copies:
         copy.start()
     for copy in smalls:
@@ -164,6 +168,18 @@
     return ghost
 
 
+def edge_of(se, small, consts):
+    even = parity("story")
+
+    def edge(over, plane, x):
+        take = even if over else jnp.logical_not(even)
+        row = 9 if over else 14
+        at = x % 12
+        return jnp.where(take, se[plane, x : x + 1, :], small[plane, at : at + 1, :]) * consts[row : row + 1, :]
+
+    return edge
+
+
 def planes_kernel(now, prev, po, pe, token):
     even = parity("plan")
     token[...] = jnp.zeros(token.shape, F32)
@@ -185,7 +201,7 @@
         load(po, 15, 14)
 
 
-def fill(right, ghost, consts, coef, layers, out, far_rows, prev_rows):
+def fill(right, edge, consts, coef, layers, out, far_rows, prev_rows):
     occupied = consts[4:5, :]
 
     def load(near, far):
@@ -195,8 +211,8 @@
                 at = (3 * kind + c) * 16
                 target[base + 4 : base + 20, :] = layers[at : at + 16, :] * occupied
                 for k, side in enumerate(sides):
-                    target[base + 3 - k : base + 4 - k, :] = ghost(False, side + c, pl.ds(x, 1), slice(None))
-                    target[base + 20 + k : base + 21 + k, :] = ghost(True, side + c, pl.ds(x, 1), slice(None))
+                    target[base + 3 - k : base + 4 - k, :] = edge(False, side + c, x)
+                    target[base + 20 + k : base + 21 + k, :] = edge(True, side + c, x)
 
     @pl.when(right)
     def _():
@@ -249,8 +265,8 @@
         coef[k] = value
 
 
-def pack_po_kernel(consts, coef, se, so, layers, po, far_rows, prev_rows):
-    fill(jnp.logical_not(parity("plan")), ghost_of(se, so, consts), consts, coef, layers, po, far_rows, prev_rows)
+def pack_po_kernel(consts, coef, se, small, layers, po, far_rows, prev_rows):
+    fill(jnp.logical_not(parity("plan")), edge_of(se, small, consts), consts, coef, layers, po, far_rows, prev_rows)
 
 
 def advance(below, here, above, before, coefs, sign):
@@ -266,11 +282,6 @@
 def update(here, before, lap, coup, a, b, gu, gd, below, above):
     geometric = gu * (above - here) - gd * (here - below)
     return 2.0 * here - before + a * lap + b * coup - geometric
-
-
-def runs_late(plans):
-    place = lax.axis_index("plan")
-    return jnp.logical_not(jnp.logical_or(place == plans // 2 - 2, place == plans // 2 + 1))
 
 
 def both_steps(consts, coef, se, so, now, prev, out, u0, u1, before):
@@ -306,12 +317,8 @@
         one(u1, lambda c, i: u0[c, i + 2], out, i, 4)
 
 
-def early_kernel(consts, coef, se, so, now, prev, layers, pe, out, far_rows, prev_rows, u0, u1, before, *, plans):
-    fill(parity("plan"), ghost_of(se, so, consts), consts, coef, layers, pe, far_rows, prev_rows)
-
-    @pl.when(jnp.logical_not(runs_late(plans)))
-    def _():
-        both_steps(consts, coef, se, so, now, prev, out, u0, u1, before)
+def pack_pe_kernel(consts, coef, se, small, layers, pe, far_rows, prev_rows):
+    fill(parity("plan"), edge_of(se, small, consts), consts, coef, layers, pe, far_rows, prev_rows)
 
 
 def planes_of(ref):
@@ -322,32 +329,25 @@
     return jnp.where(right, 1.0, -1.0)
 
 
-def late_kernel(consts, coef, se, so, now, prev, early, pe_sent, po_sent, late, base, pe_own, po_own, u0, u1, before, *, plans):
+def main_kernel(consts, coef, se, so, now, prev, pe_sent, po_sent, inner, base, pe_own, po_own, u0, u1, before):
     right = parity("plan")
-    cross = runs_late(plans)
-
-    @pl.when(cross)
-    def _():
-        both_steps(consts, coef, se, so, now, prev, late, u0, u1, before)
-
+    both_steps(consts, coef, se, so, now, prev, inner, u0, u1, before)
     for sent, own, sign in ((pe_sent, pe_own, side_sign(right)), (po_sent, po_own, -side_sign(right))):
         for k, v in enumerate(sum(stencil(planes_of(sent), None, None, sign), [])):
             own[k] = v
 
-    def finish(inner, near, far):
+    def finish(near, far):
         for c in range(3):
             base[0, c] = inner[c, :, near, :]
             base[1, c] = inner[c, :, far, :]
 
-    for inner, use in ((late, cross), (early, jnp.logical_not(cross))):
-
-        @pl.when(jnp.logical_and(use, right))
-        def _(inner=inner):
-            finish(inner, 0, 1)
-
-        @pl.when(jnp.logical_and(use, jnp.logical_not(right)))
-        def _(inner=inner):
-            finish(inner, 15, 14)
+    @pl.when(right)
+    def _():
+        finish(0, 1)
+
+    @pl.when(jnp.logical_not(right))
+    def _():
+        finish(15, 14)
 
 
 def rows_of(v):
@@ -411,43 +411,30 @@
     return near, far
 
 
-def tail_pe_kernel(coef, got, own, early, late, out, half, held, sems, *, plans):
+def tail_pe_kernel(coef, got, own, inner, out, half, held, sems):
     right = parity("plan")
-    cross = runs_late(plans)
     start = pl.multiple_of(jnp.where(right, 0, 8), 8)
-
-    def copies(inner):
-        return [pltpu.make_async_copy(inner.at[c, :, pl.ds(start, 8), :], out.at[c, :, pl.ds(start, 8), :], sems.at[c]) for c in range(3)]
-
-    def begin(inner):
-        for copy in copies(inner):
-            copy.start()
-
-    def finish(inner, row, next_row, first):
+    copies = [pltpu.make_async_copy(inner.at[c, :, pl.ds(start, 8), :], out.at[c, :, pl.ds(start, 8), :], sems.at[c]) for c in range(3)]
+    for copy in copies:
+        copy.start()
+    near, far = one_side(coef, got, held, own, side_sign(right))
+
+    def finish(row, next_row, first):
         for c in range(3):
             half[c] = inner[c, :, first : first + 8, :]
             half[c, :, row - first, :] += near[c]
             half[c, :, next_row - first, :] += far[c]
-        for copy in copies(inner):
-            copy.wait()
-
-    places = ((late, cross), (early, jnp.logical_not(cross)))
-    for inner, use in places:
-
-        @pl.when(use)
-        def _(inner=inner):
-            begin(inner)
-
-    near, far = one_side(coef, got, held, own, side_sign(right))
-    for inner, use in places:
-
-        @pl.when(jnp.logical_and(use, right))
-        def _(inner=inner):
-            finish(inner, 15, 14, 8)
-
-        @pl.when(jnp.logical_and(use, jnp.logical_not(right)))
-        def _(inner=inner):
-            finish(inner, 0, 1, 0)
+
+    @pl.when(right)
+    def _():
+        finish(15, 14, 8)
+
+    @pl.when(jnp.logical_not(right))
+    def _():
+        finish(0, 1, 0)
+
+    for copy in copies:
+        copy.wait()
 
 
 def tail_po_kernel(coef, got, own, base, half, before, out, work, held, sems):
@@ -504,19 +491,20 @@
 
 def local(u_now, u_prev, occupancy, materials, shear_table, lame_table, density_table):
     height = u_now.shape[1] * lax.axis_size("story")
-    stories, plans = lax.axis_size("story"), lax.axis_size("plan")
+    stories = lax.axis_size("story")
     face, table = shape(9, 16, WIDE), shape(4, PAD, WIDE)
     rows = 3 * PAD + 48
     planes = [pltpu.VMEM((3 * PAD, WIDE), F32)] * 2
     small = [v.reshape(1, -1) for v in (occupancy, materials, shear_table, lame_table, density_table)]
-    so, se, blocks = call(
+    small_so, se, so, blocks = call(
         functools.partial(slice_kernel, factor=0.8 / height),
-        [face, shape(10, 16, WIDE), shape(stories, 128)],
+        [shape(9, 4, WIDE), face, shape(10, 16, WIDE), shape(stories, 128)],
         [HB] * 7,
-        [pltpu.VMEM(v.shape, v.dtype) for v in small] + [pltpu.VMEM((8, 128), F32), pltpu.VMEM((stories, 128), F32), pltpu.SemaphoreType.DMA((12,))],
+        [pltpu.VMEM(v.shape, v.dtype) for v in small] + [pltpu.VMEM((8, 128), F32), pltpu.VMEM((stories, 128), F32), pltpu.SemaphoreType.DMA((18,))],
         moved=1 << 20,
-        places=[VM, VM, HB],
+        places=[VM, VM, VM, HB],
     )(*(pltpu.with_memory_space_constraint(v, pltpu.HBM) for v in [u_now, u_prev] + small))
+    small_got = swap(small_so, "story", 1)
     so_got = swap(so, "story", 1)
     se_got = swap(se, "story", 0)
     blocks = lax.all_to_all(blocks, "story", 0, 0, tiled=True)
@@ -524,42 +512,29 @@
     layers = shape(9 * 16, WIDE)
     po_layers, pe_layers, token = call(planes_kernel, [layers, layers, shape(8, 128)], [VM] * 2, flops=1_000_000_000, moved=16 << 20)(u_now, u_prev)
     coef, consts = call(expand_kernel, [table, shape(16, WIDE)], [VM] * 2, flops=20_000_000_000, moved=1 << 30)(blocks, token)
-    (po,) = call(pack_po_kernel, [shape(rows, WIDE)], [VM] * 5, planes, moved=1 << 20)(consts, coef, se_got, so_got, po_layers)
+    (po,) = call(pack_po_kernel, [shape(rows, WIDE)], [VM] * 5, planes, moved=1 << 20)(consts, coef, se_got, small_got, po_layers)
     po_got = swap(po, "plan", 1)
     levels = [
         pltpu.VMEM((3, 20, 16, WIDE), F32),
         pltpu.VMEM((3, 18, 16, WIDE), F32),
         pltpu.VMEM((3, 18, 16, WIDE), F32),
     ]
-    own = (consts, coef, se_got, so_got, u_now, u_prev)
-    pe, early = call(
-        functools.partial(early_kernel, plans=plans),
-        [shape(rows - 1, WIDE), shape(*cells)],
-        [VM] * 7,
-        planes + levels,
-        flops=60_000_000,
-        moved=4 << 20,
-    )(*own, pe_layers)
+    (pe,) = call(pack_pe_kernel, [shape(rows - 1, WIDE)], [VM] * 5, planes, moved=1 << 20)(consts, coef, se_got, small_got, pe_layers)
     pe_got = swap(pe, "plan", 0)
     side = shape(6, PAD, WIDE)
-    late, base, pe_own, po_own = call(
-        functools.partial(late_kernel, plans=plans),
-        [shape(*cells), shape(2, 3, 16, WIDE), side, side],
-        [VM] * 9,
-        levels,
-        flops=60_000_000,
-        moved=4 << 20,
-    )(*own, early, pe, po)
+    inner, base, pe_own, po_own = call(
+        main_kernel, [shape(*cells), shape(2, 3, 16, WIDE), side, side], [VM] * 8, levels, flops=60_000_000, moved=4 << 20
+    )(consts, coef, se_got, so_got, u_now, u_prev, pe, po)
     held = pltpu.VMEM((3 * PAD, WIDE), F32)
     out, half = call(
-        functools.partial(tail_pe_kernel, plans=plans),
+        tail_pe_kernel,
         [shape(*cells), shape(3, 16, 8, WIDE)],
-        [VM] * 5,
+        [VM] * 4,
         [held, pltpu.SemaphoreType.DMA((3,))],
         flops=5_000_000,
         moved=2 << 20,
         places=[HB, VM],
-    )(coef, pe_got, pe_own, early, late)
+    )(coef, pe_got, pe_own, inner)
     (out,) = call(
         tail_po_kernel,
         [shape(*cells)],

time: 35.6 us -> 35.4 us (level)
  the two profiles are of different devices: /device:TPU:30 before, /device:TPU:57 now
where the time goes in v10:
time: 35.4 us; the launch traced here: 35.2 us
  starting transfers between devices  21.7 us (61%)
  Pallas kernels  8.97 us (25%)
  waiting for transfers between devices  4.36 us (12%)
    ppermute x5, starting transfers between devices, swap(): return lax.ppermute(values, axis, pairs)  12.8 us
    all_to_all x1, starting transfers between devices, local(): blocks = lax.all_to_all(blocks, 'story', 0, 0, tiled=True)  8.95 us
    ppermute x5, waiting for transfers between devices, swap(): return lax.ppermute(values, axis, pairs)  4.36 us
    pallas_call x1, Pallas kernels, local(): call(main_kernel, [shape(*cells), shape(2, 3, 16, WIDE), side, side], [VM...  4.06 us
    pallas_call x1, Pallas kernels, local(): call(functools.partial(slice_kernel, factor=0.8 / height), [shape(9, 4, W...  1.73 us
    pallas_call x1, Pallas kernels, local(): call(tail_po_kernel, [shape(*cells)], [VM] * 5 + [HB], [pltpu.VMEM((3, 16...  1.23 us
    pallas_call x1, Pallas kernels, local(): call(tail_pe_kernel, [shape(*cells), shape(3, 16, 8, WIDE)], [VM] * 4, [h...  1.18 us
  transfers between devices with their start and end apart: 6, of which 2 were waited for; matrix products, arithmetic and copies ran while one was open for 0% of the time, Pallas kernels for 17%

profile of v10, /device:TPU:57, one launch (start us, length us, event | category | flops | bytes accessed | tf_op | source)
XLA Modules:
  0.0 35.2 jit_solution(1057142041394254263)
XLA Ops:
  0.0 0.0 copy-start
  0.0 0.0 copy-start.1
  0.0 1.7 %shard_map.73 = (f32[9,4,256]{2,1,0:T(4,128)S(1)}, f32[9,16,256]{2,1,0:T(8,128)S(1)}, f32[10,16,256]{2,1,0:T(8,128)S(1)}, f32[32,128]{1,0:T(8,128)}) custom-call(f32[3,16,16,256]{3,2,1,0:T(8,128)} %now.5, f32[3,16,16,256]{3,2,1,0:T(8,128)} %prev.5, s32[1,16]{1,0:T(1,128)} %bitcast.10, s32[1,16]{1,0:T(1,128)} %bitcast.11, f32[1,8]{1,0:T(1,128)} %bitcast.12, ...), custom_call_target="tpu_custom_call" | custom-call | bytes 1048576 | tf_op jit(solution)/shard_map/pallas_call | solution.py:499
  1.7 8.9 %all-to-all-start = ((f32[32,1,128]{2,1,0:T(1,128)}), f32[32,1,128]{2,1,0:T(1,128)S(1)}, u32[]{:S(2)}, u32[]{:S(2)}) async-start(f32[32,1,128]{2,1,0:T(1,128)} %bitcast.6), calls=%async_computation | async-start | bytes 32768 | tf_op jit(solution)/shard_map/all_to_all | solution.py:510
  10.7 3.3 %collective-permute-start.1 = (f32[9,4,256]{2,1,0:T(4,128)S(1)}, f32[9,4,256]{2,1,0:T(4,128)S(1)}, u32[]{:S(2)}, u32[]{:S(2)}) collective-permute-start(f32[9,4,256]{2,1,0:T(4,128)S(1)} %get-tuple-element.25), channel_id=1, source_target_pairs={{8,16},{16,8},{24,32},{32,24},{40,48},{48,40},{56,64},{64,56},{72,... | collective-permute-start | bytes 110600 | tf_op jit(solution)/shard_map/ppermute | solution.py:20
  14.0 0.1 collective-permute-start
  14.1 3.5 %collective-permute-start.3 = (f32[10,16,256]{2,1,0:T(8,128)S(1)}, f32[10,16,256]{2,1,0:T(8,128)S(1)}, u32[]{:S(2)}, u32[]{:S(2)}) collective-permute-start(f32[10,16,256]{2,1,0:T(8,128)S(1)} %get-tuple-element.27), channel_id=1, source_target_pairs={{8,16},{16,8},{24,32},{32,24},{40,48},{48,40},{56,64},{64,56},{72,... | collective-permute-start | bytes 491528 | tf_op jit(solution)/shard_map/ppermute | solution.py:20
  17.6 0.0 copy-done
  17.6 0.0 copy-done.1
  17.6 0.1 shard_map.74
  17.8 0.0 all-to-all-done
  17.8 0.1 shard_map.75
  17.9 0.0 collective-permute-done.1.small
  17.9 0.0 collective-permute-done.se
  17.9 0.3 shard_map.76.po_sent
  18.2 5.8 %collective-permute-start.2 = (f32[120,256]{1,0:T(8,128)S(1)}, f32[120,256]{1,0:T(8,128)S(1)}, u32[]{:S(2)}, u32[]{:S(2)}) collective-permute-start(f32[120,256]{1,0:T(8,128)S(1)} %shard_map.76.po_sent), channel_id=1, source_target_pairs={{1,2},{2,1},{3,4},{4,3},{5,6},{6,5},{9,10},{10,9},{11,12},{12,11},... | collective-permute-start | bytes 368648 | tf_op jit(solution)/shard_map/ppermute | solution.py:20
  24.0 0.3 shard_map.77.pe_sent
  24.3 0.1 collective-permute-start.4
  24.4 0.0 collective-permute-done.3.so
  24.4 4.1 %shard_map.78 = (f32[3,16,16,256]{3,2,1,0:T(8,128)S(1)}, f32[2,3,16,256]{3,2,1,0:T(8,128)S(1)}, f32[6,24,256]{2,1,0:T(8,128)S(1)}, f32[6,24,256]{2,1,0:T(8,128)S(1)}) custom-call(f32[16,256]{1,0:T(8,128)S(1)} %get-tuple-element.23.consts, f32[4,24,256]{2,1,0:T(8,128)S(1)} %get-tuple-element.22.coef, f32[9,16,256]{2,1,0:T(8,128)S(1)} %collective-permute-done.se, ...), custom_call_target="tpu_custom_call" | custom-call | flops 60000000 | bytes 4194304 | tf_op jit(solution)/shard_map/pallas_call | solution.py:525
  28.4 0.9 %collective-permute-done.4.got = f32[119,256]{1,0:T(8,128)S(1)} collective-permute-done((f32[119,256]{1,0:T(8,128)S(1)}, f32[119,256]{1,0:T(8,128)S(1)}, u32[]{:S(2)}, u32[]{:S(2)}) %collective-permute-start.4) | collective-permute-done | bytes 121888 | tf_op jit(solution)/shard_map/ppermute | solution.py:20
  29.4 1.2 %shard_map.79 = (f32[3,16,16,256]{3,2,1,0:T(8,128)}, f32[3,16,8,256]{3,2,1,0:T(8,128)S(1)}) custom-call(f32[4,24,256]{2,1,0:T(8,128)S(1)} %get-tuple-element.22.coef, f32[119,256]{1,0:T(8,128)S(1)} %collective-permute-done.4.got, f32[6,24,256]{2,1,0:T(8,128)S(1)} %get-tuple-element.31.own, f32[3,16,16,256]{3,2,1,0:T(8,128)S(1)} %get-tuple-element.32.inner), custom_call_target="tpu_custom_call" | custom-call | flops 5000000 | bytes 2097152 | tf_op jit(solution)/shard_map/pallas_call | solution.py:529
  30.6 3.4 %collective-permute-done.2.got = f32[120,256]{1,0:T(8,128)S(1)} collective-permute-done((f32[120,256]{1,0:T(8,128)S(1)}, f32[120,256]{1,0:T(8,128)S(1)}, u32[]{:S(2)}, u32[]{:S(2)}) %collective-permute-start.2) | collective-permute-done | bytes 122912 | tf_op jit(solution)/shard_map/ppermute | solution.py:20
  34.0 1.2 %shard_map.80 = f32[3,16,16,256]{3,2,1,0:T(8,128)} custom-call(f32[4,24,256]{2,1,0:T(8,128)S(1)} %get-tuple-element.22.coef, f32[120,256]{1,0:T(8,128)S(1)} %collective-permute-done.2.got, f32[6,24,256]{2,1,0:T(8,128)S(1)} %get-tuple-element.29.own, f32[2,3,16,256]{3,2,1,0:T(8,128)S(1)} %get-tuple-element.30.base, ...), custom_call_target="tpu_custom_call", output_to_operand_aliasing={{}: (5, {})} | custom-call | flops 5000000 | bytes 2097152 | tf_op jit(solution)/shard_map/pallas_call | solution.py:538
Async XLA Ops:
  0.0 17.6 %copy-start = (f32[3,16,16,256]{3,2,1,0:T(8,128)S(1)}, f32[3,16,16,256]{3,2,1,0:T(8,128)}, u32[]{:S(2)}) copy-start(f32[3,16,16,256]{3,2,1,0:T(8,128)} %now.5) | copy-start | bytes 2359300
  0.0 17.6 %copy-start.1 = (f32[3,16,16,256]{3,2,1,0:T(8,128)S(1)}, f32[3,16,16,256]{3,2,1,0:T(8,128)}, u32[]{:S(2)}) copy-start(f32[3,16,16,256]{3,2,1,0:T(8,128)} %prev.5) | copy-start | bytes 2359300
  1.7 16.0 %all-to-all-start = ((f32[32,1,128]{2,1,0:T(1,128)}), f32[32,1,128]{2,1,0:T(1,128)S(1)}, u32[]{:S(2)}, u32[]{:S(2)}) async-start(f32[32,1,128]{2,1,0:T(1,128)} %bitcast.6), calls=%async_computation | async-start | bytes 32768 | tf_op jit(solution)/shard_map/all_to_all | solution.py:510
  10.7 7.2 %collective-permute-start.1 = (f32[9,4,256]{2,1,0:T(4,128)S(1)}, f32[9,4,256]{2,1,0:T(4,128)S(1)}, u32[]{:S(2)}, u32[]{:S(2)}) collective-permute-start(f32[9,4,256]{2,1,0:T(4,128)S(1)} %get-tuple-element.25), channel_id=1, source_target_pairs={{8,16},{16,8},{24,32},{32,24},{40,48},{48,40},{56,64},{64,56},{72,... | collective-permute-start | bytes 110600 | tf_op jit(solution)/shard_map/ppermute | solution.py:20
  14.0 3.9 %collective-permute-start = (f32[9,16,256]{2,1,0:T(8,128)S(1)}, f32[9,16,256]{2,1,0:T(8,128)S(1)}, u32[]{:S(2)}, u32[]{:S(2)}) collective-permute-start(f32[9,16,256]{2,1,0:T(8,128)S(1)} %get-tuple-element.24), channel_id=1, source_target_pairs={{0,8},{8,0},{16,24},{24,16},{32,40},{40,32},{48,56},{56,48},{64,72... | collective-permute-start | bytes 442376 | tf_op jit(solution)/shard_map/ppermute | solution.py:20
  14.1 10.2 %collective-permute-start.3 = (f32[10,16,256]{2,1,0:T(8,128)S(1)}, f32[10,16,256]{2,1,0:T(8,128)S(1)}, u32[]{:S(2)}, u32[]{:S(2)}) collective-permute-start(f32[10,16,256]{2,1,0:T(8,128)S(1)} %get-tuple-element.27), channel_id=1, source_target_pairs={{8,16},{16,8},{24,32},{32,24},{40,48},{48,40},{56,64},{64,56},{72,... | collective-permute-start | bytes 491528 | tf_op jit(solution)/shard_map/ppermute | solution.py:20
  18.2 15.8 %collective-permute-start.2 = (f32[120,256]{1,0:T(8,128)S(1)}, f32[120,256]{1,0:T(8,128)S(1)}, u32[]{:S(2)}, u32[]{:S(2)}) collective-permute-start(f32[120,256]{1,0:T(8,128)S(1)} %shard_map.76.po_sent), channel_id=1, source_target_pairs={{1,2},{2,1},{3,4},{4,3},{5,6},{6,5},{9,10},{10,9},{11,12},{12,11},... | collective-permute-start | bytes 368648 | tf_op jit(solution)/shard_map/ppermute | solution.py:20
  24.3 5.1 %collective-permute-start.4 = (f32[119,256]{1,0:T(8,128)S(1)}, f32[119,256]{1,0:T(8,128)S(1)}, u32[]{:S(2)}, u32[]{:S(2)}) collective-permute-start(f32[119,256]{1,0:T(8,128)S(1)} %shard_map.77.pe_sent), channel_id=1, source_target_pairs={{0,1},{1,0},{2,3},{3,2},{4,5},{5,4},{6,7},{7,6},{8,9},{9,8},{10,11... | collective-permute-start | bytes 365576 | tf_op jit(solution)/shard_map/ppermute | solution.py:20

commit v11 on v10

--- a/solution.py
+++ b/solution.py
@@ -24,8 +24,10 @@
     count = v.shape[0] // 8
     row = lax.broadcasted_iota(jnp.int32, (8, v.shape[1]), 0)
     tiles = [v[8 * k : 8 * k + 8] for k in range(count)]
-    down = [jnp.zeros_like(tiles[0])] + [pltpu.roll(t, 1, 0) for t in tiles]
-    up = [pltpu.roll(t, 7, 0) for t in tiles] + [jnp.zeros_like(tiles[0])]
+    down, up = [pltpu.roll(t, 1, 0) for t in tiles], [pltpu.roll(t, 7, 0) for t in tiles]
+    zero = jnp.zeros_like(tiles[0])
+    around = v.shape[0] == PAD
+    down, up = [down[-1] if around else zero] + down, up + [up[0] if around else zero]
     lower = [jnp.where(row == 0, down[k], down[k + 1]) for k in range(count)]
     upper = [jnp.where(row == 7, up[k + 1], up[k]) for k in range(count)]
     return jnp.concatenate(lower, 0), jnp.concatenate(upper, 0)
@@ -92,8 +94,13 @@
     return lap, [c0, c1, c2]
 
 
+def heights():
+    row = lax.broadcasted_iota(jnp.int32, (PAD, WIDE), 0)
+    return jnp.where(row > 20, row - PAD, row)
+
+
 def coefficients(own, over, under, carried):
-    z = lax.broadcasted_iota(jnp.int32, (PAD, WIDE), 0) - 4
+    z = heights()
     zf = z.astype(F32)
 
     def pick(k):
@@ -209,10 +216,10 @@
             for c in range(3):
                 base = c * PAD
                 at = (3 * kind + c) * 16
-                target[base + 4 : base + 20, :] = layers[at : at + 16, :] * occupied
+                target[base : base + 16, :] = layers[at : at + 16, :] * occupied
                 for k, side in enumerate(sides):
-                    target[base + 3 - k : base + 4 - k, :] = edge(False, side + c, x)
-                    target[base + 20 + k : base + 21 + k, :] = edge(True, side + c, x)
+                    target[base + 23 - k : base + 24 - k, :] = edge(False, side + c, x)
+                    target[base + 16 + k : base + 17 + k, :] = edge(True, side + c, x)
 
     @pl.when(right)
     def _():
@@ -231,11 +238,11 @@
     lane = lax.broadcasted_iota(jnp.int32, (1, WIDE), 1)
     for k, c in enumerate(order):
         count = 16 if c < 2 else 15
-        out[3 * PAD + 16 * c : 3 * PAD + 16 * c + count, :] = first[k][4 : 4 + count]
-        out[c * PAD : c * PAD + 1, :] = first[k][3:4]
-        out[c * PAD + 23 : c * PAD + 24, :] = first[k][20:21]
-    out[2 * PAD + 22 : 2 * PAD + 23, :] = first[order.index(2)][19:20]
-    for k, row in enumerate((1, 22)):
+        out[3 * PAD + 16 * c : 3 * PAD + 16 * c + count, :] = first[k][0:count]
+        out[c * PAD + 18 : c * PAD + 19, :] = first[k][23:24]
+        out[c * PAD + 19 : c * PAD + 20, :] = first[k][16:17]
+    out[2 * PAD + 21 : 2 * PAD + 22, :] = first[order.index(2)][15:16]
+    for k, row in enumerate((20, 21)):
         out[row : row + 1, :] = consts[k : k + 1, :]
         out[PAD + row : PAD + row + 1, :] = jnp.where(lane % 2 == 0, consts[5 + k : 6 + k, :], consts[10 + k : 11 + k, :])
 
@@ -301,20 +308,20 @@
             u0[c, z + 2] = now[c, z] * occupied
             before[c, z + 1] = prev[c, z] * occupied
 
-    def one(source, earlier, target, i, shift):
+    def one(source, earlier, target, i, z):
         below, here, above = ([source[c, i + k] for c in range(3)] for k in range(3))
         lap, coup = stencil(below, here, above)
-        a, b, gu, gd = (coef[k, pl.ds(i + shift, 1), :] for k in range(4))
+        a, b, gu, gd = (coef[k, pl.ds(z, 1), :] for k in range(4))
         for c in range(3):
             target[c, i] = update(here[c], earlier(c, i), lap[c], coup[c], a, b, gu, gd, below[c], above[c])
 
     @pl.loop(0, 18, unroll=6)
     def _(i):
-        one(u0, lambda c, i: before[c, i], u1, i, 3)
+        one(u0, lambda c, i: before[c, i], u1, i, jnp.where(i == 0, PAD - 1, i - 1))
 
     @pl.loop(0, 16, unroll=8)
     def _(i):
-        one(u1, lambda c, i: u0[c, i + 2], out, i, 4)
+        one(u1, lambda c, i: u0[c, i + 2], out, i, i)
 
 
 def pack_pe_kernel(consts, coef, se, small, layers, pe, far_rows, prev_rows):
@@ -379,12 +386,12 @@
     for c in range(3):
         base = c * PAD
         count = 16 if c < 2 else 15
-        held[base : base + 4, :] = got[base : base + 1, :] + jnp.zeros((4, WIDE), F32)
-        held[base + 4 : base + 4 + count, :] = got[3 * PAD + 16 * c : 3 * PAD + 16 * c + count, :]
-        held[base + 20 : base + PAD, :] = got[base + 23 : base + 24, :] + jnp.zeros((4, WIDE), F32)
-    held[2 * PAD + 19 : 2 * PAD + 20, :] = got[2 * PAD + 22 : 2 * PAD + 23, :]
+        held[base : base + count, :] = got[3 * PAD + 16 * c : 3 * PAD + 16 * c + count, :]
+        held[base + 16 : base + 17, :] = got[base + 19 : base + 20, :]
+        held[base + 23 : base + 24, :] = got[base + 18 : base + 19, :]
+    held[2 * PAD + 15 : 2 * PAD + 16, :] = got[2 * PAD + 21 : 2 * PAD + 22, :]
     a, b, gu, gd = (coef[k] for k in range(4))
-    z = lax.broadcasted_iota(jnp.int32, (PAD, WIDE), 0) - 4
+    z = heights()
     even = lax.broadcasted_iota(jnp.int32, (8, WIDE), 1) % 2 == 0
 
     def pick(row):
@@ -394,20 +401,22 @@
         under = jnp.where(even, upper, mixed)[0:1]
         return jnp.where(z < 0, under, jnp.where(z > 15, over, got[row : row + 1, :]))
 
-    got_a, got_b = pick(1), pick(22)
+    got_a, got_b = pick(20), pick(21)
     lap, coup = outer_terms([(v,) + rows_of(v) for v in planes_of(got)], sign)
     delta = [a * lap[k] + b * coup[k] for k in range(3)]
     outer = [p + got_a * own[k] + got_b * own[3 + k] for k, p in enumerate(planes_of(held))]
-    delta_rows = [(v,) + rows_of(v) for v in delta]
-    outer_rows = [(v,) + rows_of(v) for v in outer]
+    delta_rows = [tuple(p[0:16] for p in (v,) + rows_of(v)) for v in delta]
+    outer_rows = [tuple(p[0:16] for p in (v,) + rows_of(v)) for v in outer]
     far_lap, far_coup = outer_terms(delta_rows, sign)
     near_lap, near_coup = both_terms(delta_rows, outer_rows, sign)
+    a, b, gu, gd = (coef[k, 0:16] for k in range(4))
     near, far = [None] * 3, [None] * 3
     for k, c in enumerate((1, 0, 2)):
-        lower, upper = row_shift(delta[k])
-        geometric = gu * (upper - delta[k]) - gd * (delta[k] - lower)
-        near[c] = (2.0 * delta[k] + a * near_lap[k] + b * near_coup[k] - geometric)[4:20]
-        far[c] = (a * far_lap[k] + b * far_coup[k])[4:20]
+        lower, upper = (v[0:16] for v in row_shift(delta[k]))
+        here = delta[k][0:16]
+        geometric = gu * (upper - here) - gd * (here - lower)
+        near[c] = 2.0 * here + a * near_lap[k] + b * near_coup[k] - geometric
+        far[c] = a * far_lap[k] + b * far_coup[k]
     return near, far
 
 

time: 35.4 us -> 35.3 us (level)
  no operation moved by 1% of the time
where the time goes in v11:
time: 35.3 us; the launch traced here: 35.1 us
  starting transfers between devices  21.7 us (61%)
  Pallas kernels  8.81 us (25%)
  waiting for transfers between devices  4.44 us (13%)
    ppermute x5, starting transfers between devices, swap(): return lax.ppermute(values, axis, pairs)  12.8 us
    all_to_all x1, starting transfers between devices, local(): blocks = lax.all_to_all(blocks, 'story', 0, 0, tiled=True)  8.95 us
    ppermute x5, waiting for transfers between devices, swap(): return lax.ppermute(values, axis, pairs)  4.43 us
    pallas_call x1, Pallas kernels, local(): call(main_kernel, [shape(*cells), shape(2, 3, 16, WIDE), side, side], [VM...  4.06 us
    pallas_call x1, Pallas kernels, local(): call(functools.partial(slice_kernel, factor=0.8 / height), [shape(9, 4, W...  1.73 us
    pallas_call x1, Pallas kernels, local(): call(tail_po_kernel, [shape(*cells)], [VM] * 5 + [HB], [pltpu.VMEM((3, 16...  1.16 us
    pallas_call x1, Pallas kernels, local(): call(tail_pe_kernel, [shape(*cells), shape(3, 16, 8, WIDE)], [VM] * 4, [h...  1.11 us
  transfers between devices with their start and end apart: 6, of which 2 were waited for; matrix products, arithmetic and copies ran while one was open for 0% of the time, Pallas kernels for 17%

profile of v11, /device:TPU:57, one launch (start us, length us, event | category | flops | bytes accessed | tf_op | source)
XLA Modules:
  0.0 35.1 jit_solution(11358640634004993968)
XLA Ops:
  0.0 0.0 copy-start
  0.0 0.0 copy-start.1
  0.0 1.7 %shard_map.73 = (f32[9,4,256]{2,1,0:T(4,128)S(1)}, f32[9,16,256]{2,1,0:T(8,128)S(1)}, f32[10,16,256]{2,1,0:T(8,128)S(1)}, f32[32,128]{1,0:T(8,128)}) custom-call(f32[3,16,16,256]{3,2,1,0:T(8,128)} %now.5, f32[3,16,16,256]{3,2,1,0:T(8,128)} %prev.5, s32[1,16]{1,0:T(1,128)} %bitcast.10, s32[1,16]{1,0:T(1,128)} %bitcast.11, f32[1,8]{1,0:T(1,128)} %bitcast.12, ...), custom_call_target="tpu_custom_call" | custom-call | bytes 1048576 | tf_op jit(solution)/shard_map/pallas_call | solution.py:508
  1.7 8.9 %all-to-all-start = ((f32[32,1,128]{2,1,0:T(1,128)}), f32[32,1,128]{2,1,0:T(1,128)S(1)}, u32[]{:S(2)}, u32[]{:S(2)}) async-start(f32[32,1,128]{2,1,0:T(1,128)} %bitcast.6), calls=%async_computation | async-start | bytes 32768 | tf_op jit(solution)/shard_map/all_to_all | solution.py:519
  10.7 3.3 %collective-permute-start.1 = (f32[9,4,256]{2,1,0:T(4,128)S(1)}, f32[9,4,256]{2,1,0:T(4,128)S(1)}, u32[]{:S(2)}, u32[]{:S(2)}) collective-permute-start(f32[9,4,256]{2,1,0:T(4,128)S(1)} %get-tuple-element.25), channel_id=1, source_target_pairs={{8,16},{16,8},{24,32},{32,24},{40,48},{48,40},{56,64},{64,56},{72,... | collective-permute-start | bytes 110600 | tf_op jit(solution)/shard_map/ppermute | solution.py:20
  14.0 0.1 collective-permute-start
  14.1 3.5 %collective-permute-start.3 = (f32[10,16,256]{2,1,0:T(8,128)S(1)}, f32[10,16,256]{2,1,0:T(8,128)S(1)}, u32[]{:S(2)}, u32[]{:S(2)}) collective-permute-start(f32[10,16,256]{2,1,0:T(8,128)S(1)} %get-tuple-element.27), channel_id=1, source_target_pairs={{8,16},{16,8},{24,32},{32,24},{40,48},{48,40},{56,64},{64,56},{72,... | collective-permute-start | bytes 491528 | tf_op jit(solution)/shard_map/ppermute | solution.py:20
  17.6 0.0 copy-done
  17.6 0.0 copy-done.1
  17.6 0.1 shard_map.74
  17.8 0.0 all-to-all-done
  17.8 0.1 shard_map.75
  17.9 0.0 collective-permute-done.1.small
  17.9 0.0 collective-permute-done.se
  17.9 0.3 shard_map.76.po_sent
  18.2 5.8 %collective-permute-start.2 = (f32[120,256]{1,0:T(8,128)S(1)}, f32[120,256]{1,0:T(8,128)S(1)}, u32[]{:S(2)}, u32[]{:S(2)}) collective-permute-start(f32[120,256]{1,0:T(8,128)S(1)} %shard_map.76.po_sent), channel_id=1, source_target_pairs={{1,2},{2,1},{3,4},{4,3},{5,6},{6,5},{9,10},{10,9},{11,12},{12,11},... | collective-permute-start | bytes 368648 | tf_op jit(solution)/shard_map/ppermute | solution.py:20
  24.0 0.3 shard_map.77.pe_sent
  24.2 0.1 collective-permute-start.4
  24.3 0.0 collective-permute-done.3.so
  24.3 4.1 %shard_map.78 = (f32[3,16,16,256]{3,2,1,0:T(8,128)S(1)}, f32[2,3,16,256]{3,2,1,0:T(8,128)S(1)}, f32[6,24,256]{2,1,0:T(8,128)S(1)}, f32[6,24,256]{2,1,0:T(8,128)S(1)}) custom-call(f32[16,256]{1,0:T(8,128)S(1)} %get-tuple-element.23.consts, f32[4,24,256]{2,1,0:T(8,128)S(1)} %get-tuple-element.22.coef, f32[9,16,256]{2,1,0:T(8,128)S(1)} %collective-permute-done.se, ...), custom_call_target="tpu_custom_call" | custom-call | flops 60000000 | bytes 4194304 | tf_op jit(solution)/shard_map/pallas_call | solution.py:534
  28.4 0.9 %collective-permute-done.4.got = f32[119,256]{1,0:T(8,128)S(1)} collective-permute-done((f32[119,256]{1,0:T(8,128)S(1)}, f32[119,256]{1,0:T(8,128)S(1)}, u32[]{:S(2)}, u32[]{:S(2)}) %collective-permute-start.4) | collective-permute-done | bytes 121888 | tf_op jit(solution)/shard_map/ppermute | solution.py:20
  29.4 1.1 %shard_map.79 = (f32[3,16,16,256]{3,2,1,0:T(8,128)}, f32[3,16,8,256]{3,2,1,0:T(8,128)S(1)}) custom-call(f32[4,24,256]{2,1,0:T(8,128)S(1)} %get-tuple-element.22.coef, f32[119,256]{1,0:T(8,128)S(1)} %collective-permute-done.4.got, f32[6,24,256]{2,1,0:T(8,128)S(1)} %get-tuple-element.31.own, f32[3,16,16,256]{3,2,1,0:T(8,128)S(1)} %get-tuple-element.32.inner), custom_call_target="tpu_custom_call" | custom-call | flops 5000000 | bytes 2097152 | tf_op jit(solution)/shard_map/pallas_call | solution.py:538
  30.5 3.5 %collective-permute-done.2.got = f32[120,256]{1,0:T(8,128)S(1)} collective-permute-done((f32[120,256]{1,0:T(8,128)S(1)}, f32[120,256]{1,0:T(8,128)S(1)}, u32[]{:S(2)}, u32[]{:S(2)}) %collective-permute-start.2) | collective-permute-done | bytes 122912 | tf_op jit(solution)/shard_map/ppermute | solution.py:20
  34.0 1.2 %shard_map.80 = f32[3,16,16,256]{3,2,1,0:T(8,128)} custom-call(f32[4,24,256]{2,1,0:T(8,128)S(1)} %get-tuple-element.22.coef, f32[120,256]{1,0:T(8,128)S(1)} %collective-permute-done.2.got, f32[6,24,256]{2,1,0:T(8,128)S(1)} %get-tuple-element.29.own, f32[2,3,16,256]{3,2,1,0:T(8,128)S(1)} %get-tuple-element.30.base, ...), custom_call_target="tpu_custom_call", output_to_operand_aliasing={{}: (5, {})} | custom-call | flops 5000000 | bytes 2097152 | tf_op jit(solution)/shard_map/pallas_call | solution.py:547
Async XLA Ops:
  0.0 17.6 %copy-start = (f32[3,16,16,256]{3,2,1,0:T(8,128)S(1)}, f32[3,16,16,256]{3,2,1,0:T(8,128)}, u32[]{:S(2)}) copy-start(f32[3,16,16,256]{3,2,1,0:T(8,128)} %now.5) | copy-start | bytes 2359300
  0.0 17.6 %copy-start.1 = (f32[3,16,16,256]{3,2,1,0:T(8,128)S(1)}, f32[3,16,16,256]{3,2,1,0:T(8,128)}, u32[]{:S(2)}) copy-start(f32[3,16,16,256]{3,2,1,0:T(8,128)} %prev.5) | copy-start | bytes 2359300
  1.7 16.0 %all-to-all-start = ((f32[32,1,128]{2,1,0:T(1,128)}), f32[32,1,128]{2,1,0:T(1,128)S(1)}, u32[]{:S(2)}, u32[]{:S(2)}) async-start(f32[32,1,128]{2,1,0:T(1,128)} %bitcast.6), calls=%async_computation | async-start | bytes 32768 | tf_op jit(solution)/shard_map/all_to_all | solution.py:519
  10.7 7.2 %collective-permute-start.1 = (f32[9,4,256]{2,1,0:T(4,128)S(1)}, f32[9,4,256]{2,1,0:T(4,128)S(1)}, u32[]{:S(2)}, u32[]{:S(2)}) collective-permute-start(f32[9,4,256]{2,1,0:T(4,128)S(1)} %get-tuple-element.25), channel_id=1, source_target_pairs={{8,16},{16,8},{24,32},{32,24},{40,48},{48,40},{56,64},{64,56},{72,... | collective-permute-start | bytes 110600 | tf_op jit(solution)/shard_map/ppermute | solution.py:20
  14.0 3.9 %collective-permute-start = (f32[9,16,256]{2,1,0:T(8,128)S(1)}, f32[9,16,256]{2,1,0:T(8,128)S(1)}, u32[]{:S(2)}, u32[]{:S(2)}) collective-permute-start(f32[9,16,256]{2,1,0:T(8,128)S(1)} %get-tuple-element.24), channel_id=1, source_target_pairs={{0,8},{8,0},{16,24},{24,16},{32,40},{40,32},{48,56},{56,48},{64,72... | collective-permute-start | bytes 442376 | tf_op jit(solution)/shard_map/ppermute | solution.py:20
  14.1 10.2 %collective-permute-start.3 = (f32[10,16,256]{2,1,0:T(8,128)S(1)}, f32[10,16,256]{2,1,0:T(8,128)S(1)}, u32[]{:S(2)}, u32[]{:S(2)}) collective-permute-start(f32[10,16,256]{2,1,0:T(8,128)S(1)} %get-tuple-element.27), channel_id=1, source_target_pairs={{8,16},{16,8},{24,32},{32,24},{40,48},{48,40},{56,64},{64,56},{72,... | collective-permute-start | bytes 491528 | tf_op jit(solution)/shard_map/ppermute | solution.py:20
  18.2 15.8 %collective-permute-start.2 = (f32[120,256]{1,0:T(8,128)S(1)}, f32[120,256]{1,0:T(8,128)S(1)}, u32[]{:S(2)}, u32[]{:S(2)}) collective-permute-start(f32[120,256]{1,0:T(8,128)S(1)} %shard_map.76.po_sent), channel_id=1, source_target_pairs={{1,2},{2,1},{3,4},{4,3},{5,6},{6,5},{9,10},{10,9},{11,12},{12,11},... | collective-permute-start | bytes 368648 | tf_op jit(solution)/shard_map/ppermute | solution.py:20
  24.2 5.1 %collective-permute-start.4 = (f32[119,256]{1,0:T(8,128)S(1)}, f32[119,256]{1,0:T(8,128)S(1)}, u32[]{:S(2)}, u32[]{:S(2)}) collective-permute-start(f32[119,256]{1,0:T(8,128)S(1)} %shard_map.77.pe_sent), channel_id=1, source_target_pairs={{0,1},{1,0},{2,3},{3,2},{4,5},{5,4},{6,7},{7,6},{8,9},{9,8},{10,11... | collective-permute-start | bytes 365576 | tf_op jit(solution)/shard_map/ppermute | solution.py:20

commit v12 on v11

--- a/solution.py
+++ b/solution.py
@@ -117,7 +117,7 @@
     return lax.axis_index(axis) % 2 == 0
 
 
-def slice_kernel(now, prev, occ_h, mat_h, shear_h, lame_h, dens_h, small, se, so, blocks, occ, mat, shear_t, lame_t, dens_t, held, held_blocks, sems, *, factor):
+def slice_kernel(now, prev, occ_h, mat_h, shear_h, lame_h, dens_h, so, se, blocks, occ, mat, shear_t, lame_t, dens_t, held, held_blocks, sems, *, factor):
     even = parity("story")
     smalls = []
     for k, (source, target) in enumerate(((occ_h, occ), (mat_h, mat), (shear_h, shear_t), (lame_h, lame_t), (dens_h, dens_t))):
@@ -128,10 +128,6 @@
         near, far = jnp.where(top, 15, 0), jnp.where(top, 14, 1)
         for j, (source, z) in enumerate(((now, near), (now, far), (prev, near))):
             copies.append(pltpu.make_async_copy(source.at[:, z], out.at[pl.ds(3 * j, 3)], sems.at[3 * k + j]))
-            if k == 1:
-                for h, x in enumerate((0, 14)):
-                    rows = small.at[pl.ds(3 * j, 3), pl.ds(2 * h, 2), :]
-                    copies.append(pltpu.make_async_copy(source.at[:, z, pl.ds(x, 2), :], rows, sems.at[12 + 2 * j + h]))
     for copy in smalls + copies:
         copy.start()
     for copy in smalls:
@@ -175,14 +171,13 @@
     return ghost
 
 
-def edge_of(se, small, consts):
+def edge_of(se, so, consts):
     even = parity("story")
 
     def edge(over, plane, x):
         take = even if over else jnp.logical_not(even)
         row = 9 if over else 14
-        at = x % 12
-        return jnp.where(take, se[plane, x : x + 1, :], small[plane, at : at + 1, :]) * consts[row : row + 1, :]
+        return jnp.where(take, se[plane, x : x + 1, :], so[plane, x : x + 1, :]) * consts[row : row + 1, :]
 
     return edge
 
@@ -272,8 +267,8 @@
         coef[k] = value
 
 
-def pack_po_kernel(consts, coef, se, small, layers, po, far_rows, prev_rows):
-    fill(jnp.logical_not(parity("plan")), edge_of(se, small, consts), consts, coef, layers, po, far_rows, prev_rows)
+def pack_po_kernel(consts, coef, se, so, layers, po, far_rows, prev_rows):
+    fill(jnp.logical_not(parity("plan")), edge_of(se, so, consts), consts, coef, layers, po, far_rows, prev_rows)
 
 
 def advance(below, here, above, before, coefs, sign):
@@ -324,8 +319,8 @@
         one(u1, lambda c, i: u0[c, i + 2], out, i, i)
 
 
-def pack_pe_kernel(consts, coef, se, small, layers, pe, far_rows, prev_rows):
-    fill(parity("plan"), edge_of(se, small, consts), consts, coef, layers, pe, far_rows, prev_rows)
+def pack_pe_kernel(consts, coef, se, so, layers, pe, far_rows, prev_rows):
+    fill(parity("plan"), edge_of(se, so, consts), consts, coef, layers, pe, far_rows, prev_rows)
 
 
 def planes_of(ref):
@@ -505,15 +500,14 @@
     rows = 3 * PAD + 48
     planes = [pltpu.VMEM((3 * PAD, WIDE), F32)] * 2
     small = [v.reshape(1, -1) for v in (occupancy, materials, shear_table, lame_table, density_table)]
-    small_so, se, so, blocks = call(
+    so, se, blocks = call(
         functools.partial(slice_kernel, factor=0.8 / height),
-        [shape(9, 4, WIDE), face, shape(10, 16, WIDE), shape(stories, 128)],
+        [face, shape(10, 16, WIDE), shape(stories, 128)],
         [HB] * 7,
-        [pltpu.VMEM(v.shape, v.dtype) for v in small] + [pltpu.VMEM((8, 128), F32), pltpu.VMEM((stories, 128), F32), pltpu.SemaphoreType.DMA((18,))],
+        [pltpu.VMEM(v.shape, v.dtype) for v in small] + [pltpu.VMEM((8, 128), F32), pltpu.VMEM((stories, 128), F32), pltpu.SemaphoreType.DMA((12,))],
         moved=1 << 20,
-        places=[VM, VM, VM, HB],
+        places=[VM, VM, HB],
     )(*(pltpu.with_memory_space_constraint(v, pltpu.HBM) for v in [u_now, u_prev] + small))
-    small_got = swap(small_so, "story", 1)
     so_got = swap(so, "story", 1)
     se_got = swap(se, "story", 0)
     blocks = lax.all_to_all(blocks, "story", 0, 0, tiled=True)
@@ -521,14 +515,14 @@
     layers = shape(9 * 16, WIDE)
     po_layers, pe_layers, token = call(planes_kernel, [layers, layers, shape(8, 128)], [VM] * 2, flops=1_000_000_000, moved=16 << 20)(u_now, u_prev)
     coef, consts = call(expand_kernel, [table, shape(16, WIDE)], [VM] * 2, flops=20_000_000_000, moved=1 << 30)(blocks, token)
-    (po,) = call(pack_po_kernel, [shape(rows, WIDE)], [VM] * 5, planes, moved=1 << 20)(consts, coef, se_got, small_got, po_layers)
+    (po,) = call(pack_po_kernel, [shape(rows, WIDE)], [VM] * 5, planes, moved=1 << 20)(consts, coef, se_got, so_got, po_layers)
     po_got = swap(po, "plan", 1)
     levels = [
         pltpu.VMEM((3, 20, 16, WIDE), F32),
         pltpu.VMEM((3, 18, 16, WIDE), F32),
         pltpu.VMEM((3, 18, 16, WIDE), F32),
     ]
-    (pe,) = call(pack_pe_kernel, [shape(rows - 1, WIDE)], [VM] * 5, planes, moved=1 << 20)(consts, coef, se_got, small_got, pe_layers)
+    (pe,) = call(pack_pe_kernel, [shape(rows - 1, WIDE)], [VM] * 5, planes, moved=1 << 20)(consts, coef, se_got, so_got, pe_layers)
     pe_got = swap(pe, "plan", 0)
     side = shape(6, PAD, WIDE)
     inner, base, pe_own, po_own = call(

time: 35.3 us -> 35.6 us (level)
  the two profiles are of different devices: /device:TPU:57 before, /device:TPU:22 now
where the time goes in v12:
time: 35.6 us; the launch traced here: 35.5 us
  starting transfers between devices  21.8 us (61%)
  Pallas kernels  8.71 us (24%)
  waiting for transfers between devices  4.85 us (14%)
    ppermute x4, starting transfers between devices, swap(): return lax.ppermute(values, axis, pairs)  12.7 us
    all_to_all x1, starting transfers between devices, local(): blocks = lax.all_to_all(blocks, 'story', 0, 0, tiled=True)  9.05 us
    ppermute x4, waiting for transfers between devices, swap(): return lax.ppermute(values, axis, pairs)  4.58 us
    pallas_call x1, Pallas kernels, local(): call(main_kernel, [shape(*cells), shape(2, 3, 16, WIDE), side, side], [VM...  4.03 us
    pallas_call x1, Pallas kernels, local(): call(functools.partial(slice_kernel, factor=0.8 / height), [face, shape(1...  1.67 us
    pallas_call x1, Pallas kernels, local(): call(tail_po_kernel, [shape(*cells)], [VM] * 5 + [HB], [pltpu.VMEM((3, 16...  1.17 us
    pallas_call x1, Pallas kernels, local(): call(tail_pe_kernel, [shape(*cells), shape(3, 16, 8, WIDE)], [VM] * 4, [h...  1.11 us
  transfers between devices with their start and end apart: 5, of which 2 were waited for; matrix products, arithmetic and copies ran while one was open for 0% of the time, Pallas kernels for 16%

profile of v12, /device:TPU:22, one launch (start us, length us, event | category | flops | bytes accessed | tf_op | source)
XLA Modules:
  0.0 35.5 jit_solution(6704023299501592339)
XLA Ops:
  0.0 0.0 copy-start
  0.0 0.0 copy-start.1
  0.0 1.7 %shard_map.73 = (f32[9,16,256]{2,1,0:T(8,128)S(1)}, f32[10,16,256]{2,1,0:T(8,128)S(1)}, f32[32,128]{1,0:T(8,128)}) custom-call(f32[3,16,16,256]{3,2,1,0:T(8,128)} %now.5, f32[3,16,16,256]{3,2,1,0:T(8,128)} %prev.5, s32[1,16]{1,0:T(1,128)} %bitcast.10, s32[1,16]{1,0:T(1,128)} %bitcast.11, f32[1,8]{1,0:T(1,128)} %bitcast.12, f32[1,8]{1,0:T(1,128)} %bitcast.13, ...), custom_call_target="tpu_custom_call" | custom-call | bytes 1048576 | tf_op jit(solution)/shard_map/pallas_call | solution.py:503
  1.7 9.0 %all-to-all-start = ((f32[32,1,128]{2,1,0:T(1,128)}), f32[32,1,128]{2,1,0:T(1,128)S(1)}, u32[]{:S(2)}, u32[]{:S(2)}) async-start(f32[32,1,128]{2,1,0:T(1,128)} %bitcast.6), calls=%async_computation | async-start | bytes 32768 | tf_op jit(solution)/shard_map/all_to_all | solution.py:513
  10.7 5.2 %collective-permute-start.1 = (f32[9,16,256]{2,1,0:T(8,128)S(1)}, f32[9,16,256]{2,1,0:T(8,128)S(1)}, u32[]{:S(2)}, u32[]{:S(2)}) collective-permute-start(f32[9,16,256]{2,1,0:T(8,128)S(1)} %get-tuple-element.24), channel_id=1, source_target_pairs={{8,16},{16,8},{24,32},{32,24},{40,48},{48,40},{56,64},{64,56},{72,... | collective-permute-start | bytes 442376 | tf_op jit(solution)/shard_map/ppermute | solution.py:20
  16.0 0.1 collective-permute-start
  16.1 0.0 copy-done
  16.1 0.0 copy-done.1
  16.1 0.1 shard_map.74
  16.2 0.3 all-to-all-done
  16.5 0.1 shard_map.75
  16.6 4.6 %collective-permute-done.1.so = f32[9,16,256]{2,1,0:T(8,128)S(1)} collective-permute-done((f32[9,16,256]{2,1,0:T(8,128)S(1)}, f32[9,16,256]{2,1,0:T(8,128)S(1)}, u32[]{:S(2)}, u32[]{:S(2)}) %collective-permute-start.1) | collective-permute-done | bytes 147488 | tf_op jit(solution)/shard_map/ppermute | solution.py:20
  21.2 0.0 collective-permute-done.se
  21.2 0.2 shard_map.76.po_sent
  21.4 2.4 %collective-permute-start.2 = (f32[120,256]{1,0:T(8,128)S(1)}, f32[120,256]{1,0:T(8,128)S(1)}, u32[]{:S(2)}, u32[]{:S(2)}) collective-permute-start(f32[120,256]{1,0:T(8,128)S(1)} %shard_map.76.po_sent), channel_id=1, source_target_pairs={{1,2},{2,1},{3,4},{4,3},{5,6},{6,5},{9,10},{10,9},{11,12},{12,11},... | collective-permute-start | bytes 368648 | tf_op jit(solution)/shard_map/ppermute | solution.py:20
  23.8 0.3 shard_map.77.pe_sent
  24.0 5.1 %collective-permute-start.3 = (f32[119,256]{1,0:T(8,128)S(1)}, f32[119,256]{1,0:T(8,128)S(1)}, u32[]{:S(2)}, u32[]{:S(2)}) collective-permute-start(f32[119,256]{1,0:T(8,128)S(1)} %shard_map.77.pe_sent), channel_id=1, source_target_pairs={{0,1},{1,0},{2,3},{3,2},{4,5},{5,4},{6,7},{7,6},{8,9},{9,8},{10,11... | collective-permute-start | bytes 365576 | tf_op jit(solution)/shard_map/ppermute | solution.py:20
  29.1 4.0 %shard_map.78 = (f32[3,16,16,256]{3,2,1,0:T(8,128)S(1)}, f32[2,3,16,256]{3,2,1,0:T(8,128)S(1)}, f32[6,24,256]{2,1,0:T(8,128)S(1)}, f32[6,24,256]{2,1,0:T(8,128)S(1)}) custom-call(f32[16,256]{1,0:T(8,128)S(1)} %get-tuple-element.22.consts, f32[4,24,256]{2,1,0:T(8,128)S(1)} %get-tuple-element.21.coef, f32[10,16,256]{2,1,0:T(8,128)S(1)} %collective-permute-done.se, ...), custom_call_target="tpu_custom_call" | custom-call | flops 60000000 | bytes 4194304 | tf_op jit(solution)/shard_map/pallas_call | solution.py:528
  33.2 0.0 collective-permute-done.3.got
  33.2 1.1 %shard_map.79 = (f32[3,16,16,256]{3,2,1,0:T(8,128)}, f32[3,16,8,256]{3,2,1,0:T(8,128)S(1)}) custom-call(f32[4,24,256]{2,1,0:T(8,128)S(1)} %get-tuple-element.21.coef, f32[119,256]{1,0:T(8,128)S(1)} %collective-permute-done.3.got, f32[6,24,256]{2,1,0:T(8,128)S(1)} %get-tuple-element.29.own, f32[3,16,16,256]{3,2,1,0:T(8,128)S(1)} %get-tuple-element.30.inner), custom_call_target="tpu_custom_call" | custom-call | flops 5000000 | bytes 2097152 | tf_op jit(solution)/shard_map/pallas_call | solution.py:532
  34.3 0.0 collective-permute-done.2.got
  34.3 1.2 %shard_map.80 = f32[3,16,16,256]{3,2,1,0:T(8,128)} custom-call(f32[4,24,256]{2,1,0:T(8,128)S(1)} %get-tuple-element.21.coef, f32[120,256]{1,0:T(8,128)S(1)} %collective-permute-done.2.got, f32[6,24,256]{2,1,0:T(8,128)S(1)} %get-tuple-element.27.own, f32[2,3,16,256]{3,2,1,0:T(8,128)S(1)} %get-tuple-element.28.base, ...), custom_call_target="tpu_custom_call", output_to_operand_aliasing={{}: (5, {})} | custom-call | flops 5000000 | bytes 2097152 | tf_op jit(solution)/shard_map/pallas_call | solution.py:541
Async XLA Ops:
  0.0 16.1 %copy-start = (f32[3,16,16,256]{3,2,1,0:T(8,128)S(1)}, f32[3,16,16,256]{3,2,1,0:T(8,128)}, u32[]{:S(2)}) copy-start(f32[3,16,16,256]{3,2,1,0:T(8,128)} %now.5) | copy-start | bytes 2359300
  0.0 16.1 %copy-start.1 = (f32[3,16,16,256]{3,2,1,0:T(8,128)S(1)}, f32[3,16,16,256]{3,2,1,0:T(8,128)}, u32[]{:S(2)}) copy-start(f32[3,16,16,256]{3,2,1,0:T(8,128)} %prev.5) | copy-start | bytes 2359300
  1.7 14.8 %all-to-all-start = ((f32[32,1,128]{2,1,0:T(1,128)}), f32[32,1,128]{2,1,0:T(1,128)S(1)}, u32[]{:S(2)}, u32[]{:S(2)}) async-start(f32[32,1,128]{2,1,0:T(1,128)} %bitcast.6), calls=%async_computation | async-start | bytes 32768 | tf_op jit(solution)/shard_map/all_to_all | solution.py:513
  10.7 10.4 %collective-permute-start.1 = (f32[9,16,256]{2,1,0:T(8,128)S(1)}, f32[9,16,256]{2,1,0:T(8,128)S(1)}, u32[]{:S(2)}, u32[]{:S(2)}) collective-permute-start(f32[9,16,256]{2,1,0:T(8,128)S(1)} %get-tuple-element.24), channel_id=1, source_target_pairs={{8,16},{16,8},{24,32},{32,24},{40,48},{48,40},{56,64},{64,56},{72,... | collective-permute-start | bytes 442376 | tf_op jit(solution)/shard_map/ppermute | solution.py:20
  16.0 5.2 %collective-permute-start = (f32[10,16,256]{2,1,0:T(8,128)S(1)}, f32[10,16,256]{2,1,0:T(8,128)S(1)}, u32[]{:S(2)}, u32[]{:S(2)}) collective-permute-start(f32[10,16,256]{2,1,0:T(8,128)S(1)} %get-tuple-element.23), channel_id=1, source_target_pairs={{0,8},{8,0},{16,24},{24,16},{32,40},{40,32},{48,56},{56,48},{64,72... | collective-permute-start | bytes 491528 | tf_op jit(solution)/shard_map/ppermute | solution.py:20
  21.4 12.9 %collective-permute-start.2 = (f32[120,256]{1,0:T(8,128)S(1)}, f32[120,256]{1,0:T(8,128)S(1)}, u32[]{:S(2)}, u32[]{:S(2)}) collective-permute-start(f32[120,256]{1,0:T(8,128)S(1)} %shard_map.76.po_sent), channel_id=1, source_target_pairs={{1,2},{2,1},{3,4},{4,3},{5,6},{6,5},{9,10},{10,9},{11,12},{12,11},... | collective-permute-start | bytes 368648 | tf_op jit(solution)/shard_map/ppermute | solution.py:20
  24.0 9.1 %collective-permute-start.3 = (f32[119,256]{1,0:T(8,128)S(1)}, f32[119,256]{1,0:T(8,128)S(1)}, u32[]{:S(2)}, u32[]{:S(2)}) collective-permute-start(f32[119,256]{1,0:T(8,128)S(1)} %shard_map.77.pe_sent), channel_id=1, source_target_pairs={{0,1},{1,0},{2,3},{3,2},{4,5},{5,4},{6,7},{7,6},{8,9},{9,8},{10,11... | collective-permute-start | bytes 365576 | tf_op jit(solution)/shard_map/ppermute | solution.py:20

commit v13 on v11

--- a/solution.py
+++ b/solution.py
@@ -429,10 +429,15 @@
     near, far = one_side(coef, got, held, own, side_sign(right))
 
     def finish(row, next_row, first):
+        mine = list(copies)
         for c in range(3):
             half[c] = inner[c, :, first : first + 8, :]
             half[c, :, row - first, :] += near[c]
             half[c, :, next_row - first, :] += far[c]
+            mine.append(pltpu.make_async_copy(half.at[c], out.at[c, :, pl.ds(first, 8), :], sems.at[3 + c]))
+            mine[-1].start()
+        for copy in mine:
+            copy.wait()
 
     @pl.when(right)
     def _():
@@ -442,16 +447,9 @@
     def _():
         finish(0, 1, 0)
 
-    for copy in copies:
-        copy.wait()
-
-
-def tail_po_kernel(coef, got, own, base, half, before, out, work, held, sems):
+
+def tail_po_kernel(coef, got, own, base, before, out, work, held, sems):
     right = jnp.logical_not(parity("plan"))
-    start = pl.multiple_of(jnp.where(right, 0, 8), 8)
-    copies = [pltpu.make_async_copy(half.at[c], out.at[c, :, pl.ds(start, 8), :], sems.at[c]) for c in range(3)]
-    for copy in copies:
-        copy.start()
     near, far = one_side(coef, got, held, own, side_sign(right))
 
     def finish(row, next_row, first):
@@ -472,9 +470,6 @@
     @pl.when(jnp.logical_not(right))
     def _():
         finish(0, 1, 0)
-
-    for copy in copies:
-        copy.wait()
 
 
 VM = pl.BlockSpec(memory_space=pltpu.VMEM)
@@ -535,25 +530,26 @@
         main_kernel, [shape(*cells), shape(2, 3, 16, WIDE), side, side], [VM] * 8, levels, flops=60_000_000, moved=4 << 20
     )(consts, coef, se_got, so_got, u_now, u_prev, pe, po)
     held = pltpu.VMEM((3 * PAD, WIDE), F32)
-    out, half = call(
+    half = pltpu.VMEM((3, 16, 8, WIDE), F32)
+    (out,) = call(
         tail_pe_kernel,
-        [shape(*cells), shape(3, 16, 8, WIDE)],
+        [shape(*cells)],
         [VM] * 4,
-        [held, pltpu.SemaphoreType.DMA((3,))],
+        [half, held, pltpu.SemaphoreType.DMA((6,))],
         flops=5_000_000,
         moved=2 << 20,
-        places=[HB, VM],
+        places=[HB],
     )(coef, pe_got, pe_own, inner)
     (out,) = call(
         tail_po_kernel,
         [shape(*cells)],
-        [VM] * 5 + [HB],
-        [pltpu.VMEM((3, 16, 8, WIDE), F32), held, pltpu.SemaphoreType.DMA((6,))],
+        [VM] * 4 + [HB],
+        [half, held, pltpu.SemaphoreType.DMA((6,))],
         flops=5_000_000,
         moved=2 << 20,
         places=[HB],
-        aliases={5: 0},
-    )(coef, po_got, po_own, base, half, out)
+        aliases={4: 0},
+    )(coef, po_got, po_own, base, out)
     return out
 
 

time: 35.3 us -> 35.3 us (level)
  no operation moved by 1% of the time
where the time goes in v13:
time: 35.3 us; the launch traced here: 35.1 us
  starting transfers between devices  21.7 us (61%)
  Pallas kernels  8.94 us (25%)
  waiting for transfers between devices  4.27 us (12%)
    ppermute x5, starting transfers between devices, swap(): return lax.ppermute(values, axis, pairs)  12.8 us
    all_to_all x1, starting transfers between devices, local(): blocks = lax.all_to_all(blocks, 'story', 0, 0, tiled=True)  8.95 us
    ppermute x5, waiting for transfers between devices, swap(): return lax.ppermute(values, axis, pairs)  4.27 us
    pallas_call x1, Pallas kernels, local(): call(main_kernel, [shape(*cells), shape(2, 3, 16, WIDE), side, side], [VM...  4.06 us
    pallas_call x1, Pallas kernels, local(): call(functools.partial(slice_kernel, factor=0.8 / height), [shape(9, 4, W...  1.73 us
    pallas_call x1, Pallas kernels, local(): call(tail_pe_kernel, [shape(*cells)], [VM] * 4, [half, held, pltpu.Semaph...  1.26 us
    pallas_call x1, Pallas kernels, local(): call(tail_po_kernel, [shape(*cells)], [VM] * 4 + [HB], [half, held, pltpu...  1.13 us
  transfers between devices with their start and end apart: 6, of which 2 were waited for; matrix products, arithmetic and copies ran while one was open for 0% of the time, Pallas kernels for 17%

profile of v13, /device:TPU:57, one launch (start us, length us, event | category | flops | bytes accessed | tf_op | source)
XLA Modules:
  0.0 35.1 jit_solution(3988859014853467470)
XLA Ops:
  0.0 0.0 copy-start
  0.0 0.0 copy-start.1
  0.0 1.7 %shard_map.73 = (f32[9,4,256]{2,1,0:T(4,128)S(1)}, f32[9,16,256]{2,1,0:T(8,128)S(1)}, f32[10,16,256]{2,1,0:T(8,128)S(1)}, f32[32,128]{1,0:T(8,128)}) custom-call(f32[3,16,16,256]{3,2,1,0:T(8,128)} %now.5, f32[3,16,16,256]{3,2,1,0:T(8,128)} %prev.5, s32[1,16]{1,0:T(1,128)} %bitcast.10, s32[1,16]{1,0:T(1,128)} %bitcast.11, f32[1,8]{1,0:T(1,128)} %bitcast.12, ...), custom_call_target="tpu_custom_call" | custom-call | bytes 1048576 | tf_op jit(solution)/shard_map/pallas_call | solution.py:503
  1.7 8.9 %all-to-all-start = ((f32[32,1,128]{2,1,0:T(1,128)}), f32[32,1,128]{2,1,0:T(1,128)S(1)}, u32[]{:S(2)}, u32[]{:S(2)}) async-start(f32[32,1,128]{2,1,0:T(1,128)} %bitcast.6), calls=%async_computation | async-start | bytes 32768 | tf_op jit(solution)/shard_map/all_to_all | solution.py:514
  10.7 3.3 %collective-permute-start.1 = (f32[9,4,256]{2,1,0:T(4,128)S(1)}, f32[9,4,256]{2,1,0:T(4,128)S(1)}, u32[]{:S(2)}, u32[]{:S(2)}) collective-permute-start(f32[9,4,256]{2,1,0:T(4,128)S(1)} %get-tuple-element.23), channel_id=1, source_target_pairs={{8,16},{16,8},{24,32},{32,24},{40,48},{48,40},{56,64},{64,56},{72,... | collective-permute-start | bytes 110600 | tf_op jit(solution)/shard_map/ppermute | solution.py:20
  14.0 0.1 collective-permute-start
  14.1 3.5 %collective-permute-start.3 = (f32[10,16,256]{2,1,0:T(8,128)S(1)}, f32[10,16,256]{2,1,0:T(8,128)S(1)}, u32[]{:S(2)}, u32[]{:S(2)}) collective-permute-start(f32[10,16,256]{2,1,0:T(8,128)S(1)} %get-tuple-element.25), channel_id=1, source_target_pairs={{8,16},{16,8},{24,32},{32,24},{40,48},{48,40},{56,64},{64,56},{72,... | collective-permute-start | bytes 491528 | tf_op jit(solution)/shard_map/ppermute | solution.py:20
  17.6 0.0 copy-done
  17.6 0.0 copy-done.1
  17.6 0.1 shard_map.74
  17.8 0.0 all-to-all-done
  17.8 0.1 shard_map.75
  17.9 0.0 collective-permute-done.1.small
  17.9 0.0 collective-permute-done.se
  17.9 0.3 shard_map.76.po_sent
  18.2 5.8 %collective-permute-start.2 = (f32[120,256]{1,0:T(8,128)S(1)}, f32[120,256]{1,0:T(8,128)S(1)}, u32[]{:S(2)}, u32[]{:S(2)}) collective-permute-start(f32[120,256]{1,0:T(8,128)S(1)} %shard_map.76.po_sent), channel_id=1, source_target_pairs={{1,2},{2,1},{3,4},{4,3},{5,6},{6,5},{9,10},{10,9},{11,12},{12,11},... | collective-permute-start | bytes 368648 | tf_op jit(solution)/shard_map/ppermute | solution.py:20
  24.0 0.3 shard_map.77.pe_sent
  24.2 0.1 collective-permute-start.4
  24.3 0.0 collective-permute-done.3.so
  24.4 4.1 %shard_map.78 = (f32[3,16,16,256]{3,2,1,0:T(8,128)S(1)}, f32[2,3,16,256]{3,2,1,0:T(8,128)S(1)}, f32[6,24,256]{2,1,0:T(8,128)S(1)}, f32[6,24,256]{2,1,0:T(8,128)S(1)}) custom-call(f32[16,256]{1,0:T(8,128)S(1)} %get-tuple-element.21.consts, f32[4,24,256]{2,1,0:T(8,128)S(1)} %get-tuple-element.20.coef, f32[9,16,256]{2,1,0:T(8,128)S(1)} %collective-permute-done.se, ...), custom_call_target="tpu_custom_call" | custom-call | flops 60000000 | bytes 4194304 | tf_op jit(solution)/shard_map/pallas_call | solution.py:529
  28.4 0.9 %collective-permute-done.4.got = f32[119,256]{1,0:T(8,128)S(1)} collective-permute-done((f32[119,256]{1,0:T(8,128)S(1)}, f32[119,256]{1,0:T(8,128)S(1)}, u32[]{:S(2)}, u32[]{:S(2)}) %collective-permute-start.4) | collective-permute-done | bytes 121888 | tf_op jit(solution)/shard_map/ppermute | solution.py:20
  29.4 1.3 %shard_map.79.before = f32[3,16,16,256]{3,2,1,0:T(8,128)} custom-call(f32[4,24,256]{2,1,0:T(8,128)S(1)} %get-tuple-element.20.coef, f32[119,256]{1,0:T(8,128)S(1)} %collective-permute-done.4.got, f32[6,24,256]{2,1,0:T(8,128)S(1)} %get-tuple-element.29.own, f32[3,16,16,256]{3,2,1,0:T(8,128)S(1)} %get-tuple-element.30.inner), custom_call_target="tpu_custom_call" | custom-call | flops 5000000 | bytes 2097152 | tf_op jit(solution)/shard_map/pallas_call | solution.py:534
  30.6 3.3 %collective-permute-done.2.got = f32[120,256]{1,0:T(8,128)S(1)} collective-permute-done((f32[120,256]{1,0:T(8,128)S(1)}, f32[120,256]{1,0:T(8,128)S(1)}, u32[]{:S(2)}, u32[]{:S(2)}) %collective-permute-start.2) | collective-permute-done | bytes 122912 | tf_op jit(solution)/shard_map/ppermute | solution.py:20
  34.0 1.1 %shard_map.80 = f32[3,16,16,256]{3,2,1,0:T(8,128)} custom-call(f32[4,24,256]{2,1,0:T(8,128)S(1)} %get-tuple-element.20.coef, f32[120,256]{1,0:T(8,128)S(1)} %collective-permute-done.2.got, f32[6,24,256]{2,1,0:T(8,128)S(1)} %get-tuple-element.27.own, f32[2,3,16,256]{3,2,1,0:T(8,128)S(1)} %get-tuple-element.28.base, ...), custom_call_target="tpu_custom_call", output_to_operand_aliasing={{}: (4, {})} | custom-call | flops 5000000 | bytes 2097152 | tf_op jit(solution)/shard_map/pallas_call | solution.py:543
Async XLA Ops:
  0.0 17.6 %copy-start = (f32[3,16,16,256]{3,2,1,0:T(8,128)S(1)}, f32[3,16,16,256]{3,2,1,0:T(8,128)}, u32[]{:S(2)}) copy-start(f32[3,16,16,256]{3,2,1,0:T(8,128)} %now.5) | copy-start | bytes 2359300
  0.0 17.6 %copy-start.1 = (f32[3,16,16,256]{3,2,1,0:T(8,128)S(1)}, f32[3,16,16,256]{3,2,1,0:T(8,128)}, u32[]{:S(2)}) copy-start(f32[3,16,16,256]{3,2,1,0:T(8,128)} %prev.5) | copy-start | bytes 2359300
  1.7 16.0 %all-to-all-start = ((f32[32,1,128]{2,1,0:T(1,128)}), f32[32,1,128]{2,1,0:T(1,128)S(1)}, u32[]{:S(2)}, u32[]{:S(2)}) async-start(f32[32,1,128]{2,1,0:T(1,128)} %bitcast.6), calls=%async_computation | async-start | bytes 32768 | tf_op jit(solution)/shard_map/all_to_all | solution.py:514
  10.7 7.2 %collective-permute-start.1 = (f32[9,4,256]{2,1,0:T(4,128)S(1)}, f32[9,4,256]{2,1,0:T(4,128)S(1)}, u32[]{:S(2)}, u32[]{:S(2)}) collective-permute-start(f32[9,4,256]{2,1,0:T(4,128)S(1)} %get-tuple-element.23), channel_id=1, source_target_pairs={{8,16},{16,8},{24,32},{32,24},{40,48},{48,40},{56,64},{64,56},{72,... | collective-permute-start | bytes 110600 | tf_op jit(solution)/shard_map/ppermute | solution.py:20
  14.0 3.9 %collective-permute-start = (f32[9,16,256]{2,1,0:T(8,128)S(1)}, f32[9,16,256]{2,1,0:T(8,128)S(1)}, u32[]{:S(2)}, u32[]{:S(2)}) collective-permute-start(f32[9,16,256]{2,1,0:T(8,128)S(1)} %get-tuple-element.22), channel_id=1, source_target_pairs={{0,8},{8,0},{16,24},{24,16},{32,40},{40,32},{48,56},{56,48},{64,72... | collective-permute-start | bytes 442376 | tf_op jit(solution)/shard_map/ppermute | solution.py:20
  14.1 10.2 %collective-permute-start.3 = (f32[10,16,256]{2,1,0:T(8,128)S(1)}, f32[10,16,256]{2,1,0:T(8,128)S(1)}, u32[]{:S(2)}, u32[]{:S(2)}) collective-permute-start(f32[10,16,256]{2,1,0:T(8,128)S(1)} %get-tuple-element.25), channel_id=1, source_target_pairs={{8,16},{16,8},{24,32},{32,24},{40,48},{48,40},{56,64},{64,56},{72,... | collective-permute-start | bytes 491528 | tf_op jit(solution)/shard_map/ppermute | solution.py:20
  18.2 15.8 %collective-permute-start.2 = (f32[120,256]{1,0:T(8,128)S(1)}, f32[120,256]{1,0:T(8,128)S(1)}, u32[]{:S(2)}, u32[]{:S(2)}) collective-permute-start(f32[120,256]{1,0:T(8,128)S(1)} %shard_map.76.po_sent), channel_id=1, source_target_pairs={{1,2},{2,1},{3,4},{4,3},{5,6},{6,5},{9,10},{10,9},{11,12},{12,11},... | collective-permute-start | bytes 368648 | tf_op jit(solution)/shard_map/ppermute | solution.py:20
  24.2 5.1 %collective-permute-start.4 = (f32[119,256]{1,0:T(8,128)S(1)}, f32[119,256]{1,0:T(8,128)S(1)}, u32[]{:S(2)}, u32[]{:S(2)}) collective-permute-start(f32[119,256]{1,0:T(8,128)S(1)} %shard_map.77.pe_sent), channel_id=1, source_target_pairs={{0,1},{1,0},{2,3},{3,2},{4,5},{5,4},{6,7},{7,6},{8,9},{9,8},{10,11... | collective-permute-start | bytes 365576 | tf_op jit(solution)/shard_map/ppermute | solution.py:20

commit v14 on v13

--- a/solution.py
+++ b/solution.py
@@ -502,7 +502,7 @@
     small = [v.reshape(1, -1) for v in (occupancy, materials, shear_table, lame_table, density_table)]
     small_so, se, so, blocks = call(
         functools.partial(slice_kernel, factor=0.8 / height),
-        [shape(9, 4, WIDE), face, shape(10, 16, WIDE), shape(stories, 128)],
+        [shape(9, 4, WIDE), shape(10, 16, WIDE), face, shape(stories, 128)],
         [HB] * 7,
         [pltpu.VMEM(v.shape, v.dtype) for v in small] + [pltpu.VMEM((8, 128), F32), pltpu.VMEM((stories, 128), F32), pltpu.SemaphoreType.DMA((18,))],
         moved=1 << 20,

time: 35.3 us -> 35.4 us (level)
  the two profiles are of different devices: /device:TPU:57 before, /device:TPU:26 now
where the time goes in v14:
time: 35.4 us; the launch traced here: 35.2 us
  starting transfers between devices  23.6 us (67%)
  Pallas kernels  8.93 us (25%)
  waiting for transfers between devices  2.58 us (7%)
    ppermute x5, starting transfers between devices, swap(): return lax.ppermute(values, axis, pairs)  14.5 us
    all_to_all x1, starting transfers between devices, local(): blocks = lax.all_to_all(blocks, 'story', 0, 0, tiled=True)  9.06 us
    pallas_call x1, Pallas kernels, local(): call(main_kernel, [shape(*cells), shape(2, 3, 16, WIDE), side, side], [VM...  4.06 us
    ppermute x5, waiting for transfers between devices, swap(): return lax.ppermute(values, axis, pairs)  2.58 us
    pallas_call x1, Pallas kernels, local(): call(functools.partial(slice_kernel, factor=0.8 / height), [shape(9, 4, W...  1.73 us
    pallas_call x1, Pallas kernels, local(): call(tail_pe_kernel, [shape(*cells)], [VM] * 4, [half, held, pltpu.Semaph...  1.26 us
    pallas_call x1, Pallas kernels, local(): call(tail_po_kernel, [shape(*cells)], [VM] * 4 + [HB], [half, held, pltpu...  1.13 us
  transfers between devices with their start and end apart: 6, of which 3 were waited for; matrix products, arithmetic and copies ran while one was open for 0% of the time, Pallas kernels for 17%

profile of v14, /device:TPU:26, one launch (start us, length us, event | category | flops | bytes accessed | tf_op | source)
XLA Modules:
  0.0 35.2 jit_solution(14321969041650162318)
XLA Ops:
  0.0 0.0 copy-start
  0.0 0.0 copy-start.1
  0.0 1.7 %shard_map.73 = (f32[9,4,256]{2,1,0:T(4,128)S(1)}, f32[10,16,256]{2,1,0:T(8,128)S(1)}, f32[9,16,256]{2,1,0:T(8,128)S(1)}, f32[32,128]{1,0:T(8,128)}) custom-call(f32[3,16,16,256]{3,2,1,0:T(8,128)} %now.5, f32[3,16,16,256]{3,2,1,0:T(8,128)} %prev.5, s32[1,16]{1,0:T(1,128)} %bitcast.10, s32[1,16]{1,0:T(1,128)} %bitcast.11, f32[1,8]{1,0:T(1,128)} %bitcast.12, ...), custom_call_target="tpu_custom_call" | custom-call | bytes 1048576 | tf_op jit(solution)/shard_map/pallas_call | solution.py:503
  1.7 9.1 %all-to-all-start = ((f32[32,1,128]{2,1,0:T(1,128)}), f32[32,1,128]{2,1,0:T(1,128)S(1)}, u32[]{:S(2)}, u32[]{:S(2)}) async-start(f32[32,1,128]{2,1,0:T(1,128)} %bitcast.6), calls=%async_computation | async-start | bytes 32768 | tf_op jit(solution)/shard_map/all_to_all | solution.py:514
  10.8 4.9 %collective-permute-start.1 = (f32[9,4,256]{2,1,0:T(4,128)S(1)}, f32[9,4,256]{2,1,0:T(4,128)S(1)}, u32[]{:S(2)}, u32[]{:S(2)}) collective-permute-start(f32[9,4,256]{2,1,0:T(4,128)S(1)} %get-tuple-element.23), channel_id=1, source_target_pairs={{8,16},{16,8},{24,32},{32,24},{40,48},{48,40},{56,64},{64,56},{72,... | collective-permute-start | bytes 110600 | tf_op jit(solution)/shard_map/ppermute | solution.py:20
  15.7 3.3 %collective-permute-start.3 = (f32[9,16,256]{2,1,0:T(8,128)S(1)}, f32[9,16,256]{2,1,0:T(8,128)S(1)}, u32[]{:S(2)}, u32[]{:S(2)}) collective-permute-start(f32[9,16,256]{2,1,0:T(8,128)S(1)} %get-tuple-element.25), channel_id=1, source_target_pairs={{8,16},{16,8},{24,32},{32,24},{40,48},{48,40},{56,64},{64,56},{72,... | collective-permute-start | bytes 442376 | tf_op jit(solution)/shard_map/ppermute | solution.py:20
  19.1 0.1 collective-permute-start
  19.2 0.0 copy-done
  19.2 0.0 copy-done.1
  19.2 0.1 shard_map.74
  19.3 0.0 all-to-all-done
  19.4 0.1 shard_map.75
  19.5 0.0 collective-permute-done.1.small
  19.5 1.1 %collective-permute-done.se = f32[10,16,256]{2,1,0:T(8,128)S(1)} collective-permute-done((f32[10,16,256]{2,1,0:T(8,128)S(1)}, f32[10,16,256]{2,1,0:T(8,128)S(1)}, u32[]{:S(2)}, u32[]{:S(2)}) %collective-permute-start) | collective-permute-done | bytes 163872 | tf_op jit(solution)/shard_map/ppermute | solution.py:20
  20.6 0.2 shard_map.76.po_sent
  20.8 6.1 %collective-permute-start.2 = (f32[120,256]{1,0:T(8,128)S(1)}, f32[120,256]{1,0:T(8,128)S(1)}, u32[]{:S(2)}, u32[]{:S(2)}) collective-permute-start(f32[120,256]{1,0:T(8,128)S(1)} %shard_map.76.po_sent), channel_id=1, source_target_pairs={{1,2},{2,1},{3,4},{4,3},{5,6},{6,5},{9,10},{10,9},{11,12},{12,11},... | collective-permute-start | bytes 368648 | tf_op jit(solution)/shard_map/ppermute | solution.py:20
  26.9 0.3 shard_map.77.pe_sent
  27.1 0.1 collective-permute-start.4
  27.2 0.0 collective-permute-done.3.so
  27.3 4.1 %shard_map.78 = (f32[3,16,16,256]{3,2,1,0:T(8,128)S(1)}, f32[2,3,16,256]{3,2,1,0:T(8,128)S(1)}, f32[6,24,256]{2,1,0:T(8,128)S(1)}, f32[6,24,256]{2,1,0:T(8,128)S(1)}) custom-call(f32[16,256]{1,0:T(8,128)S(1)} %get-tuple-element.21.consts, f32[4,24,256]{2,1,0:T(8,128)S(1)} %get-tuple-element.20.coef, f32[10,16,256]{2,1,0:T(8,128)S(1)} %collective-permute-done.se, ...), custom_call_target="tpu_custom_call" | custom-call | flops 60000000 | bytes 4194304 | tf_op jit(solution)/shard_map/pallas_call | solution.py:529
  31.3 1.0 %collective-permute-done.4.got = f32[119,256]{1,0:T(8,128)S(1)} collective-permute-done((f32[119,256]{1,0:T(8,128)S(1)}, f32[119,256]{1,0:T(8,128)S(1)}, u32[]{:S(2)}, u32[]{:S(2)}) %collective-permute-start.4) | collective-permute-done | bytes 121888 | tf_op jit(solution)/shard_map/ppermute | solution.py:20
  32.3 1.3 %shard_map.79.before = f32[3,16,16,256]{3,2,1,0:T(8,128)} custom-call(f32[4,24,256]{2,1,0:T(8,128)S(1)} %get-tuple-element.20.coef, f32[119,256]{1,0:T(8,128)S(1)} %collective-permute-done.4.got, f32[6,24,256]{2,1,0:T(8,128)S(1)} %get-tuple-element.29.own, f32[3,16,16,256]{3,2,1,0:T(8,128)S(1)} %get-tuple-element.30.inner), custom_call_target="tpu_custom_call" | custom-call | flops 5000000 | bytes 2097152 | tf_op jit(solution)/shard_map/pallas_call | solution.py:534
  33.6 0.5 %collective-permute-done.2.got = f32[120,256]{1,0:T(8,128)S(1)} collective-permute-done((f32[120,256]{1,0:T(8,128)S(1)}, f32[120,256]{1,0:T(8,128)S(1)}, u32[]{:S(2)}, u32[]{:S(2)}) %collective-permute-start.2) | collective-permute-done | bytes 122912 | tf_op jit(solution)/shard_map/ppermute | solution.py:20
  34.1 1.1 %shard_map.80 = f32[3,16,16,256]{3,2,1,0:T(8,128)} custom-call(f32[4,24,256]{2,1,0:T(8,128)S(1)} %get-tuple-element.20.coef, f32[120,256]{1,0:T(8,128)S(1)} %collective-permute-done.2.got, f32[6,24,256]{2,1,0:T(8,128)S(1)} %get-tuple-element.27.own, f32[2,3,16,256]{3,2,1,0:T(8,128)S(1)} %get-tuple-element.28.base, ...), custom_call_target="tpu_custom_call", output_to_operand_aliasing={{}: (4, {})} | custom-call | flops 5000000 | bytes 2097152 | tf_op jit(solution)/shard_map/pallas_call | solution.py:543
Async XLA Ops:
  0.0 19.2 %copy-start = (f32[3,16,16,256]{3,2,1,0:T(8,128)S(1)}, f32[3,16,16,256]{3,2,1,0:T(8,128)}, u32[]{:S(2)}) copy-start(f32[3,16,16,256]{3,2,1,0:T(8,128)} %now.5) | copy-start | bytes 2359300
  0.0 19.2 %copy-start.1 = (f32[3,16,16,256]{3,2,1,0:T(8,128)S(1)}, f32[3,16,16,256]{3,2,1,0:T(8,128)}, u32[]{:S(2)}) copy-start(f32[3,16,16,256]{3,2,1,0:T(8,128)} %prev.5) | copy-start | bytes 2359300
  1.7 17.6 %all-to-all-start = ((f32[32,1,128]{2,1,0:T(1,128)}), f32[32,1,128]{2,1,0:T(1,128)S(1)}, u32[]{:S(2)}, u32[]{:S(2)}) async-start(f32[32,1,128]{2,1,0:T(1,128)} %bitcast.6), calls=%async_computation | async-start | bytes 32768 | tf_op jit(solution)/shard_map/all_to_all | solution.py:514
  10.8 8.7 %collective-permute-start.1 = (f32[9,4,256]{2,1,0:T(4,128)S(1)}, f32[9,4,256]{2,1,0:T(4,128)S(1)}, u32[]{:S(2)}, u32[]{:S(2)}) collective-permute-start(f32[9,4,256]{2,1,0:T(4,128)S(1)} %get-tuple-element.23), channel_id=1, source_target_pairs={{8,16},{16,8},{24,32},{32,24},{40,48},{48,40},{56,64},{64,56},{72,... | collective-permute-start | bytes 110600 | tf_op jit(solution)/shard_map/ppermute | solution.py:20
  15.7 11.5 %collective-permute-start.3 = (f32[9,16,256]{2,1,0:T(8,128)S(1)}, f32[9,16,256]{2,1,0:T(8,128)S(1)}, u32[]{:S(2)}, u32[]{:S(2)}) collective-permute-start(f32[9,16,256]{2,1,0:T(8,128)S(1)} %get-tuple-element.25), channel_id=1, source_target_pairs={{8,16},{16,8},{24,32},{32,24},{40,48},{48,40},{56,64},{64,56},{72,... | collective-permute-start | bytes 442376 | tf_op jit(solution)/shard_map/ppermute | solution.py:20
  19.1 1.5 %collective-permute-start = (f32[10,16,256]{2,1,0:T(8,128)S(1)}, f32[10,16,256]{2,1,0:T(8,128)S(1)}, u32[]{:S(2)}, u32[]{:S(2)}) collective-permute-start(f32[10,16,256]{2,1,0:T(8,128)S(1)} %get-tuple-element.22), channel_id=1, source_target_pairs={{0,8},{8,0},{16,24},{24,16},{32,40},{40,32},{48,56},{56,48},{64,72... | collective-permute-start | bytes 491528 | tf_op jit(solution)/shard_map/ppermute | solution.py:20
  20.8 13.3 %collective-permute-start.2 = (f32[120,256]{1,0:T(8,128)S(1)}, f32[120,256]{1,0:T(8,128)S(1)}, u32[]{:S(2)}, u32[]{:S(2)}) collective-permute-start(f32[120,256]{1,0:T(8,128)S(1)} %shard_map.76.po_sent), channel_id=1, source_target_pairs={{1,2},{2,1},{3,4},{4,3},{5,6},{6,5},{9,10},{10,9},{11,12},{12,11},... | collective-permute-start | bytes 368648 | tf_op jit(solution)/shard_map/ppermute | solution.py:20
  27.1 5.2 %collective-permute-start.4 = (f32[119,256]{1,0:T(8,128)S(1)}, f32[119,256]{1,0:T(8,128)S(1)}, u32[]{:S(2)}, u32[]{:S(2)}) collective-permute-start(f32[119,256]{1,0:T(8,128)S(1)} %shard_map.77.pe_sent), channel_id=1, source_target_pairs={{0,1},{1,0},{2,3},{3,2},{4,5},{5,4},{6,7},{7,6},{8,9},{9,8},{10,11... | collective-permute-start | bytes 365576 | tf_op jit(solution)/shard_map/ppermute | solution.py:20
